TPU v7x, 32 devices: a whole 2x2x4 slice. The times are simulated.
32 devices in a mesh: img: 8 (over y, x, core), band: 4 (over z).
Axes of the slice: x: 2, y: 2, z: 4, core: 2. Of those that a mesh axis runs over, the one named last changes fastest.
Arguments:
- inputs: bfloat16 [32, 1024, 1152], P('img', 'band'), may hold values from -17 to 17
- condition: bfloat16 [32, 1152], P('img'), may hold values from -17 to 17
- valid_rows: int32 [32], P('img'), may hold values from 960 to 1024, as said below
- cotangent: bfloat16 [32, 1024, 1152], P('img', 'band'), may hold values from -17 to 17
- ada_weight: float32 [1152, 6912], P('band', 'img'), may hold values from -0.1875 to 0.1875
- qkv_weight: float32 [1152, 3456], P('band', 'img'), may hold values from -0.1875 to 0.1875
- out_weight: float32 [1152, 1152], P('band', 'img'), may hold values from -1 to 1
- up_weight: float32 [1152, 4608], P('band', 'img'), may hold values from -0.1875 to 0.1875
- down_weight: float32 [4608, 1152], P('band', 'img'), may hold values from -0.09375 to 0.09375
- biases: float32 [14, 1152], P(None, 'img'), may hold values from -3 to 3
- ada_first: float32 [1152, 6912], P('band', 'img'), may hold values from -0.00030517578 to 0.00030517578
- qkv_first: float32 [1152, 3456], P('band', 'img'), may hold values from -0.00030517578 to 0.00030517578
- out_first: float32 [1152, 1152], P('band', 'img'), may hold values from -6.1035156e-05 to 6.1035156e-05
- up_first: float32 [1152, 4608], P('band', 'img'), may hold values from -3.0517578e-05 to 3.0517578e-05
- down_first: float32 [4608, 1152], P('band', 'img'), may hold values from -7.6293945e-05 to 7.6293945e-05
- bias_first: float32 [14, 1152], P(None, 'img'), may hold values from -0.00030517578 to 0.00030517578
- ada_second: float32 [1152, 6912], P('band', 'img'), may hold values from 2.0917e-11 to 3.34672e-10
- qkv_second: float32 [1152, 3456], P('band', 'img'), may hold values from 2.0917e-11 to 3.34672e-10
- out_second: float32 [1152, 1152], P('band', 'img'), may hold values from 2.4263723e-12 to 9.621821e-12
- up_second: float32 [1152, 4608], P('band', 'img'), may hold values from 4.6017405e-13 to 1.8406962e-12
- down_second: float32 [4608, 1152], P('band', 'img'), may hold values from 3.6813924e-12 to 1.46419e-11
- bias_second: float32 [14, 1152], P(None, 'img'), may hold values from 2.0917e-11 to 3.34672e-10
Outputs:
- output: bfloat16 [32, 1024, 1152], P('img', 'band')
- input_grad: float32 [32, 1024, 1152], P('img', 'band')
- grad_norm: float32 [], replicated
- ada_new: float32 [1152, 6912], P('band', 'img')
- qkv_new: float32 [1152, 3456], P('band', 'img')
- out_new: float32 [1152, 1152], P('band', 'img')
- up_new: float32 [1152, 4608], P('band', 'img')
- down_new: float32 [4608, 1152], P('band', 'img')
- bias_new: float32 [14, 1152], P(None, 'img')
- ada_first_new: float32 [1152, 6912], P('band', 'img')
- qkv_first_new: float32 [1152, 3456], P('band', 'img')
- out_first_new: float32 [1152, 1152], P('band', 'img')
- up_first_new: float32 [1152, 4608], P('band', 'img')
- down_first_new: float32 [4608, 1152], P('band', 'img')
- bias_first_new: float32 [14, 1152], P(None, 'img')
- ada_second_new: float32 [1152, 6912], P('band', 'img')
- qkv_second_new: float32 [1152, 3456], P('band', 'img')
- out_second_new: float32 [1152, 1152], P('band', 'img')
- up_second_new: float32 [1152, 4608], P('band', 'img')
- down_second_new: float32 [4608, 1152], P('band', 'img')
- bias_second_new: float32 [14, 1152], P(None, 'img')
- branch_bias_grad: float32 [1152], P('img')
Inputs may be any that keep to these rules, and one draw needn't show every extreme that they name: Rows of an image at or past valid_rows are padding; among the 4 images of each index of img one has 1024 real rows and one has 960.
All inputs are finite; a program needn't handle non-finite values.
Results may differ from a plain program's by a relative error of at most 0.02.
The roundings to bfloat16 on the way count: a program that leaves them out, or rounds other values in their place, can miss the bound.
Values may be sent and summed in bfloat16 or wider, within the bound.
A program may use at most 448 MiB of HBM per device.

v0:
```python
import jax
import jax.numpy as jnp
from jax import lax
from jax.sharding import PartitionSpec as P

HEADS = 16
HEAD_DIM = 72
L = 1024
STEP = 10


norm_eps = 1e-06
beta_one = 0.9
beta_two = 0.999
adam_eps = 1e-08
learn_rate = 0.03
out_rate = 0.25
bias_rate = 0.4
clip_norm = 1.0
very_low = -1000000000.0


def normalize_keep(values):
    centre = values - jnp.mean(values, axis=-1, keepdims=True)
    inverse = lax.rsqrt(jnp.mean(centre * centre, axis=-1, keepdims=True) + norm_eps)
    return (centre * inverse, inverse)


def normalize_back(normed, inverse, incoming):
    return inverse * (
        incoming
        - jnp.mean(incoming, axis=-1, keepdims=True)
        - normed * jnp.mean(incoming * normed, axis=-1, keepdims=True)
    )


def smooth_gate(values):
    return jax.nn.gelu(values, approximate=True)


def adam_update(weight, first_old, second_old, gradient, factor, rate):
    clipped = gradient * factor
    first_new = beta_one * first_old + (1.0 - beta_one) * clipped
    second_new = beta_two * second_old + (1.0 - beta_two) * clipped * clipped
    first_hat = first_new / (1.0 - beta_one**STEP)
    second_hat = second_new / (1.0 - beta_two**STEP)
    return (weight - rate * first_hat / (jnp.sqrt(second_hat) + adam_eps), first_new, second_new)


def attention_forward(query_heads, key_heads, value_heads, key_bias, score_scale):
    scores = (
        jnp.einsum("iqhd,ikhd->ihqk", query_heads, key_heads, preferred_element_type=jnp.float32)
        * score_scale
        + key_bias
    )
    top_score = jnp.max(scores, axis=-1, keepdims=True)
    log_total = top_score + jnp.log(jnp.sum(jnp.exp(scores - top_score), axis=-1, keepdims=True))
    probs_low = jnp.exp(scores - log_total).astype(jnp.bfloat16)
    mixed = jnp.einsum(
        "ihqk,ikhd->iqhd", probs_low, value_heads, preferred_element_type=jnp.float32
    )
    return (mixed, log_total)


def attention_backward(
    query_heads, key_heads, value_heads, key_bias, score_scale, log_total, mixed_heads_grad
):
    scores = (
        jnp.einsum("iqhd,ikhd->ihqk", query_heads, key_heads, preferred_element_type=jnp.float32)
        * score_scale
        + key_bias
    )
    probs_full = jnp.exp(scores - log_total)
    prob_grad = jnp.einsum(
        "iqhd,ikhd->ihqk", mixed_heads_grad, value_heads, preferred_element_type=jnp.float32
    )
    inner_sum = jnp.sum(probs_full * prob_grad, axis=-1, keepdims=True)
    score_grad = (probs_full * (prob_grad - inner_sum) * score_scale).astype(jnp.bfloat16)
    query_grad = jnp.einsum(
        "ihqk,ikhd->iqhd", score_grad, key_heads, preferred_element_type=jnp.float32
    )
    key_part = jnp.einsum(
        "ihqk,iqhd->ikhd", score_grad, query_heads, preferred_element_type=jnp.float32
    )
    value_part = jnp.einsum(
        "ihqk,iqhd->ikhd",
        probs_full.astype(jnp.bfloat16),
        mixed_heads_grad,
        preferred_element_type=jnp.float32,
    )
    return (query_grad, key_part, value_part)


def body(
    inputs,
    condition,
    valid_rows,
    cotangent,
    ada_weight,
    qkv_weight,
    out_weight,
    up_weight,
    down_weight,
    biases,
    ada_first,
    qkv_first,
    out_first,
    up_first,
    down_first,
    bias_first,
    ada_second,
    qkv_second,
    out_second,
    up_second,
    down_second,
    bias_second,
):
    columns_low = (
        lax.all_gather(ada_weight.astype(jnp.bfloat16), "img", axis=1, tiled=True),
        lax.all_gather(qkv_weight.astype(jnp.bfloat16), "img", axis=1, tiled=True),
        lax.all_gather(out_weight.astype(jnp.bfloat16), "img", axis=1, tiled=True),
        lax.all_gather(up_weight.astype(jnp.bfloat16), "img", axis=1, tiled=True),
        lax.all_gather(down_weight.astype(jnp.bfloat16), "img", axis=1, tiled=True),
        lax.all_gather(biases.astype(jnp.bfloat16), "img", axis=1, tiled=True),
    )
    bias_vals = columns_low[5].astype(jnp.float32)
    images, local_rows, features = inputs.shape
    length = L
    head_count = HEADS
    head_size = HEAD_DIM
    score_scale = head_size ** (-0.5)
    band_count = lax.axis_size("band")
    band_rank = lax.axis_index("band")
    positions = band_rank * local_rows + jnp.arange(local_rows, dtype=jnp.int32)
    row_mask = (positions[None, :] < valid_rows[:, None]).astype(jnp.float32)[:, :, None]
    key_mask = jnp.arange(length, dtype=jnp.int32)[None, :] < valid_rows[:, None]
    key_bias = jnp.where(key_mask, 0.0, very_low).astype(jnp.float32)[:, None, None, :]
    silu_cond = jax.nn.silu(condition.astype(jnp.float32)).astype(jnp.bfloat16)
    ada_full, qkv_full, out_full, up_full, down_full = (
        lax.all_gather(columns_low[0], "band", axis=0, tiled=True),
        lax.all_gather(columns_low[1], "band", axis=0, tiled=True),
        lax.all_gather(columns_low[2], "band", axis=0, tiled=True),
        lax.all_gather(columns_low[3], "band", axis=0, tiled=True),
        lax.all_gather(columns_low[4], "band", axis=0, tiled=True),
    )
    modulation = jnp.dot(silu_cond, ada_full, preferred_element_type=jnp.float32) + bias_vals[
        0:6
    ].reshape(-1)
    mod_parts = modulation.reshape(images, 6, 1, features)
    shift_one = mod_parts[:, 0]
    scale_one = mod_parts[:, 1]
    gate_one = mod_parts[:, 2]
    shift_two = mod_parts[:, 3]
    scale_two = mod_parts[:, 4]
    gate_two = mod_parts[:, 5]
    tokens_in = inputs.astype(jnp.float32)
    normed_one, inverse_one = normalize_keep(tokens_in)
    first_in = (normed_one * (1.0 + scale_one) + shift_one).astype(jnp.bfloat16)
    grad_out = cotangent.astype(jnp.float32) * row_mask
    qkv_bias = jnp.concatenate([bias_vals[6], jnp.zeros((features,), jnp.float32), bias_vals[7]])
    projected = (
        jnp.einsum("ird,de->ire", first_in, qkv_full, preferred_element_type=jnp.float32) + qkv_bias
    ).astype(jnp.bfloat16)
    queries = projected[..., :features]
    keys_local = projected[..., features : 2 * features]
    values_local = projected[..., 2 * features :]
    keys_all, values_all = (
        lax.all_gather(keys_local, "band", axis=1, tiled=True),
        lax.all_gather(values_local, "band", axis=1, tiled=True),
    )
    query_heads = queries.reshape(images, local_rows, head_count, head_size)
    key_heads = keys_all.reshape(images, length, head_count, head_size)
    value_heads = values_all.reshape(images, length, head_count, head_size)
    mixed, log_total = attention_forward(query_heads, key_heads, value_heads, key_bias, score_scale)
    mixed = mixed.reshape(images, local_rows, features).astype(jnp.bfloat16)
    attended = (
        jnp.einsum("ird,de->ire", mixed, out_full, preferred_element_type=jnp.float32)
        + bias_vals[8]
    )
    middle = tokens_in + gate_one * attended
    normed_two, inverse_two = normalize_keep(middle)
    second_in = (normed_two * (1.0 + scale_two) + shift_two).astype(jnp.bfloat16)
    hidden_pre = jnp.einsum(
        "ird,df->irf", second_in, up_full, preferred_element_type=jnp.float32
    ) + bias_vals[9:13].reshape(-1)
    hidden, gelu_back = jax.vjp(smooth_gate, hidden_pre)
    hidden_low = hidden.astype(jnp.bfloat16)
    branch = (
        jnp.einsum("irf,fd->ird", hidden_low, down_full, preferred_element_type=jnp.float32)
        + bias_vals[13]
    )
    output = (middle + gate_two * branch).astype(jnp.bfloat16)
    branch_grad = (gate_two * grad_out).astype(jnp.bfloat16)
    gate_two_grad = jnp.sum(grad_out * branch, axis=1)
    down_grad = jnp.einsum(
        "irf,ird->fd", hidden_low, branch_grad, preferred_element_type=jnp.float32
    )
    hidden_grad = jnp.einsum(
        "ird,fd->irf", branch_grad, down_full, preferred_element_type=jnp.float32
    )
    pre_grad = gelu_back(hidden_grad)[0].astype(jnp.bfloat16)
    up_grad = jnp.einsum("ird,irf->df", second_in, pre_grad, preferred_element_type=jnp.float32)
    second_grad = jnp.einsum("irf,df->ird", pre_grad, up_full, preferred_element_type=jnp.float32)
    shift_two_grad = jnp.sum(second_grad, axis=1)
    scale_two_grad = jnp.sum(second_grad * normed_two, axis=1)
    middle_grad = grad_out + normalize_back(
        normed_two, inverse_two, second_grad * (1.0 + scale_two)
    )
    attended_grad = (gate_one * middle_grad).astype(jnp.bfloat16)
    gate_one_grad = jnp.sum(middle_grad * attended, axis=1)
    out_grad = jnp.einsum("ird,ire->de", mixed, attended_grad, preferred_element_type=jnp.float32)
    mixed_grad = jnp.einsum(
        "ire,de->ird", attended_grad, out_full, preferred_element_type=jnp.float32
    ).astype(jnp.bfloat16)
    mixed_heads_grad = mixed_grad.reshape(images, local_rows, head_count, head_size)
    query_part, key_part, value_part = attention_backward(
        query_heads, key_heads, value_heads, key_bias, score_scale, log_total, mixed_heads_grad
    )
    query_grad = query_part.reshape(images, local_rows, features).astype(jnp.bfloat16)
    key_grad, value_grad = (
        lax.psum_scatter(
            key_part.reshape(images, length, features), "band", scatter_dimension=1, tiled=True
        ),
        lax.psum_scatter(
            value_part.reshape(images, length, features), "band", scatter_dimension=1, tiled=True
        ),
    )
    key_grad_low = key_grad.astype(jnp.bfloat16)
    value_grad_low = value_grad.astype(jnp.bfloat16)
    qkv_grad = jnp.concatenate([query_grad, key_grad_low, value_grad_low], axis=-1)
    qkv_weight_grad = jnp.einsum(
        "ird,ire->de", first_in, qkv_grad, preferred_element_type=jnp.float32
    )
    first_grad = jnp.einsum("ire,de->ird", qkv_grad, qkv_full, preferred_element_type=jnp.float32)
    shift_one_grad = jnp.sum(first_grad, axis=1)
    scale_one_grad = jnp.sum(first_grad * normed_one, axis=1)
    input_grad = middle_grad + normalize_back(
        normed_one, inverse_one, first_grad * (1.0 + scale_one)
    )
    mod_grad = jnp.stack(
        [
            shift_one_grad,
            scale_one_grad,
            gate_one_grad,
            shift_two_grad,
            scale_two_grad,
            gate_two_grad,
        ],
        axis=1,
    ).reshape(images, 6 * features)
    ada_grad = jnp.einsum(
        "id,ie->de", silu_cond.astype(jnp.float32), mod_grad, precision=lax.Precision.HIGHEST
    )
    bias_grad = jnp.concatenate(
        [
            jnp.sum(mod_grad, axis=0).reshape(6, features),
            jnp.sum(query_grad.astype(jnp.float32), axis=(0, 1))[None],
            jnp.sum(value_grad_low.astype(jnp.float32), axis=(0, 1))[None],
            jnp.sum(attended_grad.astype(jnp.float32), axis=(0, 1))[None],
            jnp.sum(pre_grad.astype(jnp.float32), axis=(0, 1)).reshape(4, features),
            jnp.sum(branch_grad.astype(jnp.float32), axis=(0, 1))[None],
        ],
        axis=0,
    )
    row_grads = (
        lax.psum_scatter(ada_grad, "band", scatter_dimension=0, tiled=True),
        lax.psum_scatter(qkv_weight_grad, "band", scatter_dimension=0, tiled=True),
        lax.psum_scatter(out_grad, "band", scatter_dimension=0, tiled=True),
        lax.psum_scatter(up_grad, "band", scatter_dimension=0, tiled=True),
        lax.psum_scatter(down_grad, "band", scatter_dimension=0, tiled=True),
    )
    by_columns = (
        lax.psum_scatter(row_grads[0], "img", scatter_dimension=1, tiled=True),
        lax.psum_scatter(row_grads[1], "img", scatter_dimension=1, tiled=True),
        lax.psum_scatter(row_grads[2], "img", scatter_dimension=1, tiled=True),
        lax.psum_scatter(row_grads[3], "img", scatter_dimension=1, tiled=True),
        lax.psum_scatter(row_grads[4], "img", scatter_dimension=1, tiled=True),
        lax.psum_scatter(bias_grad, "img", scatter_dimension=1, tiled=True),
    )
    shards = by_columns[:5]
    bias_total = lax.psum(by_columns[5], "band")
    squares = jnp.sum(bias_total * bias_total) / band_count
    for shard_grad in shards:
        squares = squares + jnp.sum(shard_grad * shard_grad)
    squares_total = lax.psum(squares, ("img", "band"))
    grad_norm = jnp.sqrt(squares_total)
    factor = clip_norm / jnp.maximum(grad_norm, clip_norm)
    ada_new, ada_first_new, ada_second_new = adam_update(
        ada_weight, ada_first, ada_second, shards[0], factor, learn_rate
    )
    qkv_new, qkv_first_new, qkv_second_new = adam_update(
        qkv_weight, qkv_first, qkv_second, shards[1], factor, learn_rate
    )
    out_new, out_first_new, out_second_new = adam_update(
        out_weight, out_first, out_second, shards[2], factor, out_rate
    )
    up_new, up_first_new, up_second_new = adam_update(
        up_weight, up_first, up_second, shards[3], factor, learn_rate
    )
    down_new, down_first_new, down_second_new = adam_update(
        down_weight, down_first, down_second, shards[4], factor, learn_rate
    )
    bias_new, bias_first_new, bias_second_new = adam_update(
        biases, bias_first, bias_second, bias_total, factor, bias_rate
    )
    branch_bias_grad = bias_total[13] * factor
    return (
        output,
        input_grad,
        grad_norm,
        ada_new,
        qkv_new,
        out_new,
        up_new,
        down_new,
        bias_new,
        ada_first_new,
        qkv_first_new,
        out_first_new,
        up_first_new,
        down_first_new,
        bias_first_new,
        ada_second_new,
        qkv_second_new,
        out_second_new,
        up_second_new,
        down_second_new,
        bias_second_new,
        branch_bias_grad,
    )


def solution(mesh):
    return jax.shard_map(
        body,
        mesh=mesh,
        in_specs=(
            P("img", "band", None),
            P("img", None),
            P("img"),
            P("img", "band", None),
            P("band", "img"),
            P("band", "img"),
            P("band", "img"),
            P("band", "img"),
            P("band", "img"),
            P(None, "img"),
            P("band", "img"),
            P("band", "img"),
            P("band", "img"),
            P("band", "img"),
            P("band", "img"),
            P(None, "img"),
            P("band", "img"),
            P("band", "img"),
            P("band", "img"),
            P("band", "img"),
            P("band", "img"),
            P(None, "img"),
        ),
        out_specs=(
            P("img", "band", None),
            P("img", "band", None),
            P(),
            P("band", "img"),
            P("band", "img"),
            P("band", "img"),
            P("band", "img"),
            P("band", "img"),
            P(None, "img"),
            P("band", "img"),
            P("band", "img"),
            P("band", "img"),
            P("band", "img"),
            P("band", "img"),
            P(None, "img"),
            P("band", "img"),
            P("band", "img"),
            P("band", "img"),
            P("band", "img"),
            P("band", "img"),
            P(None, "img"),
            P("img"),
        ),
        check_vma=False,
    )
```

profile of v0, /device:TPU:0, one launch (start us, length us, event | category | flops | bytes accessed | tf_op | source)
XLA Modules:
  0.0 4237.2 jit_solution(16332343498256626606)
XLA Ops:
  11.3 38.4 all-gather.32.cloned.1.call-done
  105.8 249.8 %all-gather.16.cloned.1.call-done = bf16[1152,6912]{1,0:T(8,128)(2,1)} async-done(((bf16[288,6912]{1,0:T(8,128)(2,1)}), bf16[1152,6912]{1,0:T(8,128)(2,1)}) %all-gather.16.cloned.1.call-update) | async-done | bytes 15925264 | tf_op jit(solution)/shard_map/all_gather | solution.py:140
  363.5 135.0 %all-gather.18.cloned.1.call-done = bf16[1152,3456]{1,0:T(8,128)(2,1)} async-done(((bf16[288,3456]{1,0:T(8,128)(2,1)}), bf16[1152,3456]{1,0:T(8,128)(2,1)}) %all-gather.18.cloned.1.call-update) | async-done | bytes 7962640 | tf_op jit(solution)/shard_map/all_gather | solution.py:141
  574.2 159.1 %all-gather.22.cloned.1.call-done = bf16[4,1024,1152]{2,1,0:T(8,128)(2,1)} async-done(((bf16[4,256,1152]{2,1,0:T(8,128)(2,1)}), bf16[4,1024,1152]{2,1,0:T(8,128)(2,1)}) %all-gather.22.cloned.1.call-update) | async-done | bytes 9437200 | tf_op jit(solution)/shard_map/all_gather | solution.py:168
  746.0 153.8 %all-gather.20.cloned.1.call-done = bf16[4,1024,1152]{2,1,0:T(8,128)(2,1)} async-done(((bf16[4,256,1152]{2,1,0:T(8,128)(2,1)}), bf16[4,1024,1152]{2,1,0:T(8,128)(2,1)}) %all-gather.20.cloned.1.call-update) | async-done | bytes 9437200 | tf_op jit(solution)/shard_map/all_gather | solution.py:169
  1004.6 137.2 %all-gather.26.cloned.1.call-done = bf16[1152,4608]{1,0:T(8,128)(2,1)} async-done(((bf16[288,4608]{1,0:T(8,128)(2,1)}), bf16[1152,4608]{1,0:T(8,128)(2,1)}) %all-gather.26.cloned.1.call-update) | async-done | bytes 10616848 | tf_op jit(solution)/shard_map/all_gather | solution.py:143
  1162.8 165.0 %all-gather.30.cloned.1.call-done = bf16[4608,1152]{1,0:T(8,128)(2,1)} async-done(((bf16[1152,1152]{1,0:T(8,128)(2,1)}), bf16[4608,1152]{1,0:T(8,128)(2,1)}) %all-gather.30.cloned.1.call-update) | async-done | bytes 10616848 | tf_op jit(solution)/shard_map/all_gather | solution.py:144
  1440.3 108.8 %fusion.7 = f32[4,16,72,1024]{3,2,1,0:T(8,128)} fusion(bf16[4,256,16,72]{1,3,2,0:T(8,128)(2,1)} %bitcast.163, f32[4,16,256,1024]{3,2,1,0:T(8,128)} %fusion.105, f32[4,16,256,1024]{3,2,1,0:T(8,128)} %get-tuple-element.187, f32[4,16,256]{2,1,0:T(8,128)S(1)} %copy-done.19, f32[4,1024]{1,0:T(4,128)S(1)} %copy-done.11), kind=kOutput, calls=%fused_computation.9 | convolution fusion | flops 2600485888 | bytes 155533312 | tf_op jit(solution)/shard_map/ihqk,iqhd->ikhd/dot_general | solution.py:82
  1567.8 31.3 fusion.69
  1672.5 104.6 %convert_reduce_fusion.5 = (f32[16,72]{1,0:T(8,128)S(1)}, bf16[4,16,72,256]{3,2,1,0:T(8,128)(2,1)S(1)}) fusion(bf16[4,1024,16,72]{1,3,2,0:T(8,128)(2,1)} %bitcast.151, f32[4,16,256,1024]{3,2,1,0:T(8,128)} %fusion.105, f32[4,16,256,1024]{3,2,1,0:T(8,128)} %get-tuple-element.187, f32[4,16,256]{2,1,0:T(8,128)S(1)} %copy-done.19, f32[4,1024]{1,0:T(4,128)S(1)} %copy-done.11), kind=kOutput, calls=%fused_computation.67 | convolution fusion | flops 2604023808 | bytes 146100736 | tf_op jit(solution)/shard_map/ihqk,ikhd->iqhd/dot_general | solution.py:79
  1779.8 100.1 %reduce-scatter.26.cloned.1.call-done = f32[4,256,1152]{2,1,0:T(8,128)} async-done(((f32[4,1024,1152]{2,1,0:T(8,128)}), f32[4,256,1152]{2,1,0:T(8,128)}) %reduce-scatter.26.cloned.1.call-update) | async-done | bytes 4718608 | tf_op jit(solution)/shard_map/reduce_scatter | solution.py:221
  1883.9 313.4 %reduce-scatter.28.cloned.1.call-done = f32[4,256,1152]{2,1,0:T(8,128)} async-done(((f32[4,1024,1152]{2,1,0:T(8,128)}), f32[4,256,1152]{2,1,0:T(8,128)}) %reduce-scatter.28.cloned.1.call-update) | async-done | bytes 4718608 | tf_op jit(solution)/shard_map/reduce_scatter | solution.py:224
  2256.8 38.5 reduce-scatter.34.cloned.1.call-done
  2300.0 349.7 %reduce-scatter.38.cloned.1.call-done = f32[1152,1152]{1,0:T(8,128)} async-done(((f32[4608,1152]{1,0:T(8,128)}), f32[1152,1152]{1,0:T(8,128)}) %reduce-scatter.38.cloned.1.call-update) | async-done | bytes 5308432 | tf_op jit(solution)/shard_map/reduce_scatter | solution.py:270
  2656.5 348.2 %reduce-scatter.36.cloned.1.call-done = f32[288,4608]{1,0:T(8,128)} async-done(((f32[1152,4608]{1,0:T(8,128)}), f32[288,4608]{1,0:T(8,128)}) %reduce-scatter.36.cloned.1.call-update) | async-done | bytes 5308432 | tf_op jit(solution)/shard_map/reduce_scatter | solution.py:269
  3011.5 264.5 %reduce-scatter.32.cloned.1.call-done = f32[288,3456]{1,0:T(8,128)} async-done(((f32[1152,3456]{1,0:T(8,128)}), f32[288,3456]{1,0:T(8,128)}) %reduce-scatter.32.cloned.1.call-update) | async-done | bytes 3981328 | tf_op jit(solution)/shard_map/reduce_scatter | solution.py:267
  3281.9 523.1 %reduce-scatter.30.cloned.1.call-done = f32[288,6912]{1,0:T(8,128)} async-done(((f32[1152,6912]{1,0:T(8,128)}), f32[288,6912]{1,0:T(8,128)}) %reduce-scatter.30.cloned.1.call-update) | async-done | bytes 7962640 | tf_op jit(solution)/shard_map/reduce_scatter | solution.py:266
  3816.5 32.3 reduce-scatter.46.cloned.1.call-done
  3850.5 36.5 reduce-scatter.40.cloned.1.call-done
  3908.3 39.5 reduce-scatter.50.cloned.1.call-done
  3949.3 67.6 %reduce-scatter.48.cloned.1.call-done = f32[576,288]{1,0:T(8,128)} async-done(((f32[4608,288]{1,0:T(8,128)}), f32[576,288]{1,0:T(8,128)}) %reduce-scatter.48.cloned.1.call-update) | async-done | bytes 663568
  4020.0 57.6 %reduce-scatter.44.cloned.1.call-done = f32[432,288]{1,0:T(8,128)} async-done(((f32[3456,288]{1,0:T(8,128)}), f32[432,288]{1,0:T(8,128)}) %reduce-scatter.44.cloned.1.call-update) | async-done | bytes 497680
  4079.7 83.5 %reduce-scatter.42.cloned.1.call-done = f32[864,288]{1,0:T(8,128)} async-done(((f32[6912,288]{1,0:T(8,128)}), f32[864,288]{1,0:T(8,128)}) %reduce-scatter.42.cloned.1.call-update) | async-done | bytes 995344
  4170.2 39.4 psum.15
  (279 shorter events, 639.0 us)
Async XLA Ops:
  7.2 42.5 %all-gather.32.cloned.1.call-start = ((), (), s32[]{:S(2)}) async-start(), calls=%async_computation.28 | async-start | bytes 4644864 | tf_op jit(solution)/shard_map/all_gather | solution.py:119
  9.3 71.8 %all-gather.34.cloned.1.call-start = ((), (), s32[]{:S(2)}) async-start(), calls=%async_computation.29 | async-start | bytes 2654208 | tf_op jit(solution)/shard_map/all_gather | solution.py:120
  11.2 344.4 %all-gather.16.cloned.1.call-start = ((), (), s32[]{:S(2)}) async-start(), calls=%async_computation.13 | async-start | bytes 19906560 | tf_op jit(solution)/shard_map/all_gather | solution.py:140
  63.0 435.5 %all-gather.18.cloned.1.call-start = ((), (), s32[]{:S(2)}) async-start(), calls=%async_computation.14 | async-start | bytes 9953280 | tf_op jit(solution)/shard_map/all_gather | solution.py:141
  91.4 442.1 %all-gather.36.cloned.1.call-start = ((), (), s32[]{:S(2)}) async-start(), calls=%async_computation.30 | async-start | bytes 3317760 | tf_op jit(solution)/shard_map/all_gather | solution.py:122
  92.3 472.0 %all-gather.28.cloned.1.call-start = ((), (), s32[]{:S(2)}) async-start(), calls=%async_computation.19 | async-start | bytes 2985984 | tf_op jit(solution)/shard_map/all_gather | solution.py:123
  94.4 638.9 %all-gather.22.cloned.1.call-start = ((), (), s32[]{:S(2)}) async-start(), calls=%async_computation.16 | async-start | bytes 11796480 | tf_op jit(solution)/shard_map/all_gather | solution.py:168
  514.4 385.4 %all-gather.20.cloned.1.call-start = ((), (), s32[]{:S(2)}) async-start(), calls=%async_computation.15 | async-start | bytes 11796480 | tf_op jit(solution)/shard_map/all_gather | solution.py:169
  515.2 478.0 %all-gather.24.cloned.1.call-start = ((), (), s32[]{:S(2)}) async-start(), calls=%async_computation.17 | async-start | bytes 3317760 | tf_op jit(solution)/shard_map/all_gather | solution.py:142
  530.7 611.1 %all-gather.26.cloned.1.call-start = ((), (), s32[]{:S(2)}) async-start(), calls=%async_computation.18 | async-start | bytes 13271040 | tf_op jit(solution)/shard_map/all_gather | solution.py:143
  543.6 784.1 %all-gather.30.cloned.1.call-start = ((), (), s32[]{:S(2)}) async-start(), calls=%async_computation.20 | async-start | bytes 13271040 | tf_op jit(solution)/shard_map/all_gather | solution.py:144
  569.5 1310.3 %reduce-scatter.26.cloned.1.call-start = ((), (), s32[]{:S(2)}) async-start(), calls=%async_computation.21 | async-start | bytes 23592960 | tf_op jit(solution)/shard_map/reduce_scatter | solution.py:221
  1567.8 629.5 %reduce-scatter.28.cloned.1.call-start = ((), (), s32[]{:S(2)}) async-start(), calls=%async_computation.22 | async-start | bytes 23592960 | tf_op jit(solution)/shard_map/reduce_scatter | solution.py:224
  1617.8 677.5 %reduce-scatter.34.cloned.1.call-start = ((), (), s32[]{:S(2)}) async-start(), calls=%async_computation.25 | async-start | bytes 6635520 | tf_op jit(solution)/shard_map/reduce_scatter | solution.py:268
  1626.0 1023.6 %reduce-scatter.38.cloned.1.call-start = ((), (), s32[]{:S(2)}) async-start(), calls=%async_computation.27 | async-start | bytes 26542080 | tf_op jit(solution)/shard_map/reduce_scatter | solution.py:270
  1651.8 1352.9 %reduce-scatter.36.cloned.1.call-start = ((), (), s32[]{:S(2)}) async-start(), calls=%async_computation.26 | async-start | bytes 26542080 | tf_op jit(solution)/shard_map/reduce_scatter | solution.py:269
  1672.5 1603.5 %reduce-scatter.32.cloned.1.call-start = ((), (), s32[]{:S(2)}) async-start(), calls=%async_computation.24 | async-start | bytes 19906560 | tf_op jit(solution)/shard_map/reduce_scatter | solution.py:267
  2215.6 1589.5 %reduce-scatter.30.cloned.1.call-start = ((), (), s32[]{:S(2)}) async-start(), calls=%async_computation.23 | async-start | bytes 39813120 | tf_op jit(solution)/shard_map/reduce_scatter | solution.py:266
  2256.8 1592.0 %reduce-scatter.46.cloned.1.call-start = ((), (), s32[]{:S(2)}) async-start(), calls=%async_computation.34 | async-start | bytes 1990656
  2298.4 1588.6 %reduce-scatter.40.cloned.1.call-start = ((), (), s32[]{:S(2)}) async-start(), calls=%async_computation.31 | async-start | bytes 663552
  2299.9 1647.9 %reduce-scatter.50.cloned.1.call-start = ((), (), s32[]{:S(2)}) async-start(), calls=%async_computation.36 | async-start | bytes 5971968
  2656.5 1360.4 %reduce-scatter.48.cloned.1.call-start = ((), (), s32[]{:S(2)}) async-start(), calls=%async_computation.35 | async-start | bytes 7962624
  3011.4 1066.2 %reduce-scatter.44.cloned.1.call-start = ((), (), s32[]{:S(2)}) async-start(), calls=%async_computation.33 | async-start | bytes 5971968
  3281.9 881.3 %reduce-scatter.42.cloned.1.call-start = ((), (), s32[]{:S(2)}) async-start(), calls=%async_computation.32 | async-start | bytes 11943936
  (53 other events, 6078.8 us)
Sparse Core Ops, SparseCore 0:
  10.5 39.1 all-gather.31
  52.1 29.0 all-gather.33
  82.7 272.8 all-gather.15
  357.6 140.8 all-gather.17
  500.8 32.6 all-gather.35
  535.8 28.4 all-gather.27
  566.4 166.7 all-gather.21
  734.8 164.9 all-gather.19
  902.0 53.5 all-gather.23
  956.9 184.8 all-gather.25
  1143.4 184.2 all-gather.29
  1567.9 311.9 reduce-scatter.25
  1882.4 314.8 reduce-scatter.27
  2199.4 95.8 reduce-scatter.33
  2297.7 351.8 reduce-scatter.37
  2651.8 352.8 reduce-scatter.35
  3007.1 268.8 reduce-scatter.31
  3278.2 526.7 reduce-scatter.29
  3808.8 39.9 reduce-scatter.45
  3852.6 34.3 reduce-scatter.39
  3890.8 56.9 reduce-scatter.49
  3951.4 65.4 reduce-scatter.47
  4020.7 56.9 reduce-scatter.43
  4081.0 82.1 reduce-scatter.41
where the time goes:
time: 4240 us
  waiting for transfers between devices  3330 us (79%)
  matrix products  560 us (13%)
  local copies, waits for them, and re-layouts  175 us (4%)
  blocking collectives  82.1 us (2%)
  other arithmetic  63.3 us (1%)
    reduce_scatter x1, waiting for transfers between devices, body(): lax.psum_scatter(ada_grad, 'band', scatter_dimension=0, tiled=True)  523 us
    reduce_scatter x1, waiting for transfers between devices, body(): lax.psum_scatter(down_grad, 'band', scatter_dimension=0, tiled=True)  350 us
    reduce_scatter x1, waiting for transfers between devices, body(): lax.psum_scatter(up_grad, 'band', scatter_dimension=0, tiled=True)  348 us
    unnamed x30, waiting for transfers between devices  318 us
    reduce_scatter x1, waiting for transfers between devices, body(): lax.psum_scatter(value_part.reshape(images, length, features), 'band', sc...  313 us
    reduce_scatter x1, waiting for transfers between devices, body(): lax.psum_scatter(qkv_weight_grad, 'band', scatter_dimension=0, tiled=True)  265 us
    all_gather x1, waiting for transfers between devices, body(): lax.all_gather(columns_low[0], 'band', axis=0, tiled=True)  250 us
    all_gather x1, waiting for transfers between devices, body(): lax.all_gather(columns_low[4], 'band', axis=0, tiled=True)  165 us
  transfers between devices with their start and end apart: 24, of which 23 were waited for; matrix products, arithmetic and copies ran while one was open for 12% of the time, Pallas kernels for 0%

commit v1 on v0

--- a/solution.py
+++ b/solution.py
@@ -115,64 +115,102 @@
     down_second,
     bias_second,
 ):
-    columns_low = (
-        lax.all_gather(ada_weight.astype(jnp.bfloat16), "img", axis=1, tiled=True),
-        lax.all_gather(qkv_weight.astype(jnp.bfloat16), "img", axis=1, tiled=True),
-        lax.all_gather(out_weight.astype(jnp.bfloat16), "img", axis=1, tiled=True),
-        lax.all_gather(up_weight.astype(jnp.bfloat16), "img", axis=1, tiled=True),
-        lax.all_gather(down_weight.astype(jnp.bfloat16), "img", axis=1, tiled=True),
-        lax.all_gather(biases.astype(jnp.bfloat16), "img", axis=1, tiled=True),
-    )
-    bias_vals = columns_low[5].astype(jnp.float32)
     images, local_rows, features = inputs.shape
     length = L
     head_count = HEADS
     head_size = HEAD_DIM
     score_scale = head_size ** (-0.5)
     band_count = lax.axis_size("band")
+    img_count = lax.axis_size("img")
     band_rank = lax.axis_index("band")
-    positions = band_rank * local_rows + jnp.arange(local_rows, dtype=jnp.int32)
-    row_mask = (positions[None, :] < valid_rows[:, None]).astype(jnp.float32)[:, :, None]
-    key_mask = jnp.arange(length, dtype=jnp.int32)[None, :] < valid_rows[:, None]
-    key_bias = jnp.where(key_mask, 0.0, very_low).astype(jnp.float32)[:, None, None, :]
-    silu_cond = jax.nn.silu(condition.astype(jnp.float32)).astype(jnp.bfloat16)
-    ada_full, qkv_full, out_full, up_full, down_full = (
-        lax.all_gather(columns_low[0], "band", axis=0, tiled=True),
-        lax.all_gather(columns_low[1], "band", axis=0, tiled=True),
-        lax.all_gather(columns_low[2], "band", axis=0, tiled=True),
-        lax.all_gather(columns_low[3], "band", axis=0, tiled=True),
-        lax.all_gather(columns_low[4], "band", axis=0, tiled=True),
-    )
-    modulation = jnp.dot(silu_cond, ada_full, preferred_element_type=jnp.float32) + bias_vals[
-        0:6
-    ].reshape(-1)
-    mod_parts = modulation.reshape(images, 6, 1, features)
+    img_rank = lax.axis_index("img")
+    own = max(1, images // band_count)
+    split = max(1, band_count // images)
+    mates = band_count // split
+    image_rows = length // split
+    exchange_groups = None
+    share_groups = None
+    if split > 1:
+        exchange_groups = [[g * mates + m for m in range(mates)] for g in range(split)]
+        share_groups = [[g * mates + m for g in range(split)] for m in range(mates)]
+    low_type = jnp.bfloat16
+
+    def to_images(rows):
+        return lax.all_to_all(rows, "band", split_axis=0, concat_axis=1, axis_index_groups=exchange_groups, tiled=True)
+
+    def to_bands(whole):
+        return lax.all_to_all(whole, "band", split_axis=1, concat_axis=0, axis_index_groups=exchange_groups, tiled=True)
+
+    def gather_weight(weight):
+        rows = lax.all_gather(weight.astype(low_type), "band", axis=0, tiled=True)
+        return lax.all_gather(rows, "img", axis=1, tiled=True)
+
+    def scatter_grad(grad):
+        columns = lax.psum_scatter(grad.astype(low_type), "img", scatter_dimension=1, tiled=True)
+        return lax.psum_scatter(columns, "band", scatter_dimension=0, tiled=True).astype(jnp.float32)
+
+    condition_all = lax.all_gather(condition, "img", axis=0, tiled=True)
+    tokens_low = to_images(inputs)
+    bias_vals = lax.all_gather(biases.astype(low_type), "img", axis=1, tiled=True).astype(
+        jnp.float32
+    )
+    qkv_full = gather_weight(qkv_weight)
+    out_full = gather_weight(out_weight)
+    up_full = gather_weight(up_weight)
+    cotangent_low = to_images(cotangent)
+    down_full = gather_weight(down_weight)
+
+    silu_all = jax.nn.silu(condition_all.astype(jnp.float32)).astype(low_type)
+    ada_rows = ada_weight.shape[0]
+    silu_rows = lax.dynamic_slice_in_dim(silu_all, band_rank * ada_rows, ada_rows, axis=1)
+    mod_partial = jnp.dot(
+        silu_rows, ada_weight.astype(low_type), preferred_element_type=jnp.float32
+    )
+    ada_columns = mod_partial.shape[1]
+    mod_sent = jnp.tile(
+        mod_partial.reshape(img_count, 1, images * ada_columns), (1, split, 1)
+    )
+    mod_pieces = lax.all_to_all(
+        mod_sent.reshape(img_count * band_count, own * ada_columns),
+        ("img", "band"),
+        split_axis=0,
+        concat_axis=0,
+        tiled=True,
+    ).reshape(img_count, band_count, own, ada_columns)
+    modulation = (
+        jnp.sum(mod_pieces, axis=1).transpose(1, 0, 2).reshape(own, img_count * ada_columns)
+        + bias_vals[0:6].reshape(-1)
+    )
+    mod_parts = modulation.reshape(own, 6, 1, features)
     shift_one = mod_parts[:, 0]
     scale_one = mod_parts[:, 1]
     gate_one = mod_parts[:, 2]
     shift_two = mod_parts[:, 3]
     scale_two = mod_parts[:, 4]
     gate_two = mod_parts[:, 5]
-    tokens_in = inputs.astype(jnp.float32)
+    valid_own = lax.dynamic_slice_in_dim(valid_rows, lax.rem(band_rank, mates) * own, own, axis=0)
+    key_mask = jnp.arange(length, dtype=jnp.int32)[None, :] < valid_own[:, None]
+    positions = lax.div(band_rank, mates) * image_rows + jnp.arange(image_rows, dtype=jnp.int32)
+    row_mask = (positions[None, :] < valid_own[:, None]).astype(jnp.float32)[:, :, None]
+    key_bias = jnp.where(key_mask, 0.0, very_low).astype(jnp.float32)[:, None, None, :]
+    tokens_in = tokens_low.astype(jnp.float32)
     normed_one, inverse_one = normalize_keep(tokens_in)
     first_in = (normed_one * (1.0 + scale_one) + shift_one).astype(jnp.bfloat16)
-    grad_out = cotangent.astype(jnp.float32) * row_mask
+    grad_out = cotangent_low.astype(jnp.float32) * row_mask
     qkv_bias = jnp.concatenate([bias_vals[6], jnp.zeros((features,), jnp.float32), bias_vals[7]])
     projected = (
         jnp.einsum("ird,de->ire", first_in, qkv_full, preferred_element_type=jnp.float32) + qkv_bias
     ).astype(jnp.bfloat16)
-    queries = projected[..., :features]
-    keys_local = projected[..., features : 2 * features]
-    values_local = projected[..., 2 * features :]
-    keys_all, values_all = (
-        lax.all_gather(keys_local, "band", axis=1, tiled=True),
-        lax.all_gather(values_local, "band", axis=1, tiled=True),
-    )
-    query_heads = queries.reshape(images, local_rows, head_count, head_size)
-    key_heads = keys_all.reshape(images, length, head_count, head_size)
-    value_heads = values_all.reshape(images, length, head_count, head_size)
+    query_heads = projected[..., :features].reshape(own, image_rows, head_count, head_size)
+    keys_values = projected[..., features:]
+    if split > 1:
+        keys_values = lax.all_gather(
+            keys_values, "band", axis=1, axis_index_groups=share_groups, tiled=True
+        )
+    key_heads = keys_values[..., :features].reshape(own, length, head_count, head_size)
+    value_heads = keys_values[..., features:].reshape(own, length, head_count, head_size)
     mixed, log_total = attention_forward(query_heads, key_heads, value_heads, key_bias, score_scale)
-    mixed = mixed.reshape(images, local_rows, features).astype(jnp.bfloat16)
+    mixed = mixed.reshape(own, image_rows, features).astype(jnp.bfloat16)
     attended = (
         jnp.einsum("ird,de->ire", mixed, out_full, preferred_element_type=jnp.float32)
         + bias_vals[8]
@@ -189,17 +227,19 @@
         jnp.einsum("irf,fd->ird", hidden_low, down_full, preferred_element_type=jnp.float32)
         + bias_vals[13]
     )
-    output = (middle + gate_two * branch).astype(jnp.bfloat16)
+    output = to_bands((middle + gate_two * branch).astype(jnp.bfloat16))
     branch_grad = (gate_two * grad_out).astype(jnp.bfloat16)
     gate_two_grad = jnp.sum(grad_out * branch, axis=1)
-    down_grad = jnp.einsum(
-        "irf,ird->fd", hidden_low, branch_grad, preferred_element_type=jnp.float32
+    down_shard = scatter_grad(
+        jnp.einsum("irf,ird->fd", hidden_low, branch_grad, preferred_element_type=jnp.float32)
     )
     hidden_grad = jnp.einsum(
         "ird,fd->irf", branch_grad, down_full, preferred_element_type=jnp.float32
     )
     pre_grad = gelu_back(hidden_grad)[0].astype(jnp.bfloat16)
-    up_grad = jnp.einsum("ird,irf->df", second_in, pre_grad, preferred_element_type=jnp.float32)
+    up_shard = scatter_grad(
+        jnp.einsum("ird,irf->df", second_in, pre_grad, preferred_element_type=jnp.float32)
+    )
     second_grad = jnp.einsum("irf,df->ird", pre_grad, up_full, preferred_element_type=jnp.float32)
     shift_two_grad = jnp.sum(second_grad, axis=1)
     scale_two_grad = jnp.sum(second_grad * normed_two, axis=1)
@@ -208,35 +248,41 @@
     )
     attended_grad = (gate_one * middle_grad).astype(jnp.bfloat16)
     gate_one_grad = jnp.sum(middle_grad * attended, axis=1)
-    out_grad = jnp.einsum("ird,ire->de", mixed, attended_grad, preferred_element_type=jnp.float32)
+    out_shard = scatter_grad(
+        jnp.einsum("ird,ire->de", mixed, attended_grad, preferred_element_type=jnp.float32)
+    )
     mixed_grad = jnp.einsum(
         "ire,de->ird", attended_grad, out_full, preferred_element_type=jnp.float32
     ).astype(jnp.bfloat16)
-    mixed_heads_grad = mixed_grad.reshape(images, local_rows, head_count, head_size)
+    mixed_heads_grad = mixed_grad.reshape(own, image_rows, head_count, head_size)
     query_part, key_part, value_part = attention_backward(
         query_heads, key_heads, value_heads, key_bias, score_scale, log_total, mixed_heads_grad
     )
-    query_grad = query_part.reshape(images, local_rows, features).astype(jnp.bfloat16)
-    key_grad, value_grad = (
-        lax.psum_scatter(
-            key_part.reshape(images, length, features), "band", scatter_dimension=1, tiled=True
-        ),
-        lax.psum_scatter(
-            value_part.reshape(images, length, features), "band", scatter_dimension=1, tiled=True
-        ),
-    )
-    key_grad_low = key_grad.astype(jnp.bfloat16)
-    value_grad_low = value_grad.astype(jnp.bfloat16)
+    query_grad = query_part.reshape(own, image_rows, features).astype(jnp.bfloat16)
+    key_part = key_part.reshape(own, length, features)
+    value_part = value_part.reshape(own, length, features)
+    if split > 1:
+        key_part, value_part = (
+            lax.psum_scatter(
+                part, "band", scatter_dimension=1, axis_index_groups=share_groups, tiled=True
+            )
+            for part in (key_part, value_part)
+        )
+    key_grad_low = key_part.astype(jnp.bfloat16)
+    value_grad_low = value_part.astype(jnp.bfloat16)
     qkv_grad = jnp.concatenate([query_grad, key_grad_low, value_grad_low], axis=-1)
-    qkv_weight_grad = jnp.einsum(
-        "ird,ire->de", first_in, qkv_grad, preferred_element_type=jnp.float32
+    qkv_shard = scatter_grad(
+        jnp.einsum("ird,ire->de", first_in, qkv_grad, preferred_element_type=jnp.float32)
     )
     first_grad = jnp.einsum("ire,de->ird", qkv_grad, qkv_full, preferred_element_type=jnp.float32)
     shift_one_grad = jnp.sum(first_grad, axis=1)
     scale_one_grad = jnp.sum(first_grad * normed_one, axis=1)
-    input_grad = middle_grad + normalize_back(
-        normed_one, inverse_one, first_grad * (1.0 + scale_one)
-    )
+    input_grad = to_bands(
+        (
+            middle_grad
+            + normalize_back(normed_one, inverse_one, first_grad * (1.0 + scale_one))
+        ).astype(low_type)
+    ).astype(jnp.float32)
     mod_grad = jnp.stack(
         [
             shift_one_grad,
@@ -247,13 +293,9 @@
             gate_two_grad,
         ],
         axis=1,
-    ).reshape(images, 6 * features)
-    ada_grad = jnp.einsum(
-        "id,ie->de", silu_cond.astype(jnp.float32), mod_grad, precision=lax.Precision.HIGHEST
-    )
-    bias_grad = jnp.concatenate(
+    )
+    row_sums = jnp.concatenate(
         [
-            jnp.sum(mod_grad, axis=0).reshape(6, features),
             jnp.sum(query_grad.astype(jnp.float32), axis=(0, 1))[None],
             jnp.sum(value_grad_low.astype(jnp.float32), axis=(0, 1))[None],
             jnp.sum(attended_grad.astype(jnp.float32), axis=(0, 1))[None],
@@ -262,23 +304,31 @@
         ],
         axis=0,
     )
-    row_grads = (
-        lax.psum_scatter(ada_grad, "band", scatter_dimension=0, tiled=True),
-        lax.psum_scatter(qkv_weight_grad, "band", scatter_dimension=0, tiled=True),
-        lax.psum_scatter(out_grad, "band", scatter_dimension=0, tiled=True),
-        lax.psum_scatter(up_grad, "band", scatter_dimension=0, tiled=True),
-        lax.psum_scatter(down_grad, "band", scatter_dimension=0, tiled=True),
-    )
-    by_columns = (
-        lax.psum_scatter(row_grads[0], "img", scatter_dimension=1, tiled=True),
-        lax.psum_scatter(row_grads[1], "img", scatter_dimension=1, tiled=True),
-        lax.psum_scatter(row_grads[2], "img", scatter_dimension=1, tiled=True),
-        lax.psum_scatter(row_grads[3], "img", scatter_dimension=1, tiled=True),
-        lax.psum_scatter(row_grads[4], "img", scatter_dimension=1, tiled=True),
-        lax.psum_scatter(bias_grad, "img", scatter_dimension=1, tiled=True),
-    )
-    shards = by_columns[:5]
-    bias_total = lax.psum(by_columns[5], "band")
+    mod_all = lax.all_gather(
+        mod_grad.reshape(own, 6 * features), ("img", "band"), axis=0, tiled=True
+    )
+    bias_columns = biases.shape[1]
+    mod_columns = lax.dynamic_slice_in_dim(mod_all, img_rank * ada_columns, ada_columns, axis=1)
+    silu_terms = jnp.tile(
+        silu_rows.astype(jnp.float32).reshape(img_count, 1, images, ada_rows), (1, split, 1, 1)
+    ).reshape(img_count * band_count * own, ada_rows)
+    ada_shard = jnp.einsum(
+        "id,ie->de",
+        silu_terms,
+        mod_columns,
+        precision=lax.Precision.HIGHEST,
+    )
+    mod_sums = lax.dynamic_slice_in_dim(
+        jnp.sum(mod_all, axis=0).reshape(6, features),
+        img_rank * bias_columns,
+        bias_columns,
+        axis=1,
+    )
+    sums_shard = lax.psum(
+        lax.psum_scatter(row_sums, "img", scatter_dimension=1, tiled=True), "band"
+    )
+    bias_total = jnp.concatenate([mod_sums, sums_shard], axis=0)
+    shards = (ada_shard, qkv_shard, out_shard, up_shard, down_shard)
     squares = jnp.sum(bias_total * bias_total) / band_count
     for shard_grad in shards:
         squares = squares + jnp.sum(shard_grad * shard_grad)

time: 4240 us -> 1180 us (0.28)
  waiting for transfers between devices: 3330 us -> 245 us
  matrix products: 560 us -> 421 us
  blocking collectives: 82.1 us -> 221 us
  other arithmetic: 63.3 us -> 136 us
  local copies, waits for them, and re-layouts: 175 us -> 113 us
    reduce_scatter x7 -> x4, waiting for transfers between devices: 1940 us -> 105 us  [scatter_grad(): lax.psum_scatter(grad.astype(low_type), 'img', scatter_dimension=1, tiled...]
    all_gather x11 -> x6, waiting for transfers between devices: 1080 us -> 0.06 us  [the longest x2 0.04 us: gather_weight(): rows = lax.all_gather(weight.astype(low_type), 'band', axis=0, tiled=True)]
    unnamed x30 -> x20, waiting for transfers between devices: 318 us -> 50.3 us
    all_gather x2 -> x5, blocking collectives: 23.7 us -> 158 us  [the longest x1 81.4 us: body(): lax.all_gather(mod_grad.reshape(own, 6 * features), ('img', 'band'), axis...]
    dot_general x1, matrix products: 109 us -> 15.8 us  [attention_backward(): jnp.einsum('ihqk,iqhd->ikhd', score_grad, query_heads, preferred_element_...]
    all_to_all x0 -> x4, waiting for transfers between devices: none -> 89.6 us  [the longest x2 89.6 us: to_images(): lax.all_to_all(rows, 'band', split_axis=0, concat_axis=1, axis_index_grou...]
    sub x0 -> x1, matrix products: none -> 64.5 us  [attention_backward(): prob_grad - inner_sum]
    convert_element_type x5 -> x12, other arithmetic: 6.09 us -> 55.7 us  [the longest x1 33.7 us: attention_forward(): probs_low = jnp.exp(scores - log_total).astype(jnp.bfloat16)]
  transfers between devices with their start and end apart: 24 -> 19, of which waited for: 23 -> 6; matrix products, arithmetic and copies ran while one was open for 12% -> 39% of each run, Pallas kernels for 0% -> 0%
where the time goes in v1:
time: 1180 us
  matrix products  421 us (36%)
  waiting for transfers between devices  245 us (21%)
  blocking collectives  221 us (19%)
  other arithmetic  136 us (12%)
  local copies, waits for them, and re-layouts  113 us (10%)
  between operations  21 us (2%)
  starting transfers between devices  18.5 us (2%)
    reduce_scatter x4, waiting for transfers between devices, scatter_grad(): lax.psum_scatter(grad.astype(low_type), 'img', scatter_dimension=1, tiled...  105 us
    all_to_all x2, waiting for transfers between devices, to_images(): lax.all_to_all(rows, 'band', split_axis=0, concat_axis=1, axis_index_grou...  89.6 us
    all_gather x1, blocking collectives, body(): lax.all_gather(mod_grad.reshape(own, 6 * features), ('img', 'band'), axis...  81.4 us
    unnamed x174, local copies, waits for them, and re-layouts  73.7 us
    dot_general x1, matrix products, attention_backward(): jnp.einsum('ihqk,ikhd->iqhd', score_grad, key_heads, preferred_element_ty...  73.2 us
    sub x1, matrix products, attention_backward(): prob_grad - inner_sum  64.5 us
    all_gather x2, blocking collectives, gather_weight(): rows = lax.all_gather(weight.astype(low_type), 'band', axis=0, tiled=True)  58.6 us
    unnamed x20, waiting for transfers between devices  50.3 us
  transfers between devices with their start and end apart: 19, of which 6 were waited for; matrix products, arithmetic and copies ran while one was open for 39% of the time, Pallas kernels for 0%

profile of v1, /device:TPU:0, one launch (start us, length us, event | category | flops | bytes accessed | tf_op | source)
XLA Modules:
  0.0 1175.5 jit_solution(5658547935939656800)
XLA Ops:
  12.3 41.5 %all_gather.35 = bf16[1152,432]{1,0:T(8,128)(2,1)S(1)} all-gather(bf16[288,432]{1,0:T(8,128)(2,1)S(1)} %convert_element_type.329), channel_id=1, replica_groups=mesh['img'=8,'band'=4] {'band'}, dimensions={0}, use_global_device_ids=true | all-gather | bytes 1244160 | tf_op jit(solution)/shard_map/all_gather | solution.py:145
  55.4 17.1 %all-gather.2 = bf16[4,288,144]{1,2,0:T(8,128)(2,1)S(1)} all-gather(bf16[1,288,144]{1,2,0:T(8,128)(2,1)S(1)} %convert_bitcast_fusion), channel_id=1, replica_groups=mesh['img'=8,'band'=4] {'band'}, dimensions={0}, use_global_device_ids=true | all-gather | bytes 414720 | tf_op jit(solution)/shard_map/all_gather | solution.py:145
  113.5 45.5 %all-to-all-done = bf16[4,256,1152]{2,1,0:T(8,128)(2,1)S(1)} async-done(((bf16[4,256,1152]{2,1,0:T(8,128)(2,1)}), bf16[4,256,1152]{2,1,0:T(8,128)(2,1)S(1)}, u32[]{:S(2)}, u32[]{:S(2)}) %all-to-all-start) | async-done | bytes 2359328 | tf_op jit(solution)/shard_map/all_to_all | solution.py:139
  173.2 44.1 %all-to-all-done.3 = bf16[4,256,1152]{2,1,0:T(8,128)(2,1)} async-done(((bf16[4,256,1152]{2,1,0:T(8,128)(2,1)}), bf16[4,256,1152]{2,1,0:T(8,128)(2,1)}, u32[]{:S(2)}, u32[]{:S(2)}) %all-to-all-start.3) | async-done | bytes 2359328 | tf_op jit(solution)/shard_map/all_to_all | solution.py:139
  250.9 27.2 %fusion.2 = (f32[16,1024]{1,0:T(8,128)S(1)}, f32[16,1024,1024]{1,2,0:T(8,128)}) fusion(f32[1024]{0:T(1024)S(1)} %fusion.87, bf16[1024,16,72]{0,2,1:T(8,128)(2,1)} %bitcast.190, bf16[1024,16,72]{0,2,1:T(8,128)(2,1)} %bitcast.198), kind=kOutput, calls=%fused_computation.7 | convolution fusion | flops 2466234368 | bytes 71897088 | tf_op jit(solution)/shard_map/iqhd,ikhd->ihqk/dot_general | solution.py:52
  278.2 23.3 %exponential_reduce_fusion = f32[16,1024]{1,0:T(8,128)S(1)} fusion(f32[16,1024,1024]{1,2,0:T(8,128)} %get-tuple-element.208, f32[16,1024]{1,0:T(8,128)S(1)} %get-tuple-element.207, f32[1024]{0:T(1024)S(1)} %fusion.87), kind=kLoop, calls=%fused_computation.5 | loop fusion | flops 67092480 | bytes 67244032 | tf_op jit(solution)/shard_map/reduce_sum | solution.py:57
  301.5 33.7 %fusion.5 = bf16[16,1024,1024]{1,2,0:T(8,128)(2,1)} fusion(f32[16,1024,1024]{1,2,0:T(8,128)} %get-tuple-element.208, f32[16,1024]{1,0:T(8,128)S(1)} %log_add_fusion, f32[1024]{0:T(1024)S(1)} %fusion.87), kind=kLoop, calls=%fused_computation.8 | loop fusion | flops 67108864 | bytes 100732928 | tf_op jit(solution)/shard_map/convert_element_type | solution.py:58
  335.3 18.6 %convolution_convert_fusion.6 = bf16[16,72,1024]{2,1,0:T(8,128)(2,1)} fusion(bf16[1024,16,72]{0,2,1:T(8,128)(2,1)} %bitcast.203, bf16[16,1024,1024]{1,2,0:T(8,128)(2,1)} %fusion.5), kind=kOutput, calls=%fused_computation.86 | convolution fusion | flops 2417098752 | bytes 38273024 | tf_op jit(solution)/shard_map/ihqk,ikhd->iqhd/dot_general | solution.py:59
  365.1 21.0 %fusion.98 = f32[1024,4608]{1,0:T(8,128)} fusion(bf16[1152,4608]{0,1:T(8,128)(2,1)} %all-gather.17.cloned.1.call-done, f32[1024,1152]{1,0:T(8,128)} %copy-done.4, f32[1152]{0:T(1024)S(1)} %get-tuple-element.167, f32[1152]{0:T(1024)S(1)} %get-tuple-element.168, f32[1024]{0:T(1024)S(1)} %add_rsqrt_fusion, f32[1024]{0:T(1024)S(1)} %broadcast_multiply_fusion.4), kind=kOutput, calls=%fused_computation.177 | convolution fusion | flops 10877534208 | bytes 34227200 | tf_op jit(solution)/shard_map/ird,df->irf/dot_general | solution.py:221
  386.1 28.7 %convert_reduce_fusion = (f32[4608]{0:T(1024)}, bf16[1024,4608]{1,0:T(8,128)(2,1)}) fusion(f32[1024,4608]{1,0:T(8,128)} %fusion.98, f32[4608]{0:T(1024)S(1)} %add.332, bf16[1024,1152]{1,0:T(8,128)(2,1)S(1)} %copy-done.20, bf16[4608,1152]{0,1:T(8,128)(2,1)} %all-gather.21.cloned.1.call-done), kind=kOutput, calls=%fused_computation.23 | convolution fusion | flops 10980159488 | bytes 41324544 | tf_op jit(solution)/shard_map/ird,fd->irf/dot_general | solution.py:236
  414.8 18.0 %multiply_reduce_fusion.2 = (f32[1152]{0:T(1024)}, f32[1024]{0:T(1024)S(1)}, f32[1024]{0:T(1024)S(1)}, f32[1152]{0:T(1024)}, f32[1024,1152]{1,0:T(8,128)}) fusion(f32[1024,1152]{1,0:T(8,128)S(1)} %copy-done.5, f32[1024]{0:T(1024)S(1)} %add_rsqrt_fusion, f32[1024]{0:T(1024)S(1)} %broadcast_multiply_fusion.4, f32[1152]{0:T(1024)S(1)} %get-tuple-element.168, ...), kind=kOutput, calls=%fused_computation.67 | convolution fusion | flops 10882248704 | bytes 29521408 | tf_op jit(solution)/shard_map/irf,df->ird/dot_general | solution.py:243
  432.9 25.1 %multiply_reduce_fusion.1 = (f32[1152]{0:T(1024)}, bf16[1,1024,1152]{2,1,0:T(8,128)(2,1)}, f32[1152]{0:T(1024)}, f32[1024,1152]{1,0:T(8,128)}) fusion(bf16[4,256,1152]{2,1,0:T(8,128)(2,1)} %all-to-all-done.3, f32[1024]{0:T(1024)S(1)} %copy-done.42, f32[1024,1152]{1,0:T(8,128)} %copy-done.4, f32[1152]{0:T(1024)S(1)} %copy-done.33, ...), kind=kOutput, calls=%fused_computation.66 | convolution fusion | flops 10940053504 | bytes 53146112 | tf_op jit(solution)/shard_map/irf,fd->ird/dot_general | solution.py:227
  470.7 18.3 %convert_reduce_fusion.4 = (f32[16,72]{1,0:T(8,128)}, bf16[16,72,1024]{2,1,0:T(8,128)(2,1)}) fusion(bf16[1024,16,72]{0,2,1:T(8,128)(2,1)S(1)} %bitcast.200, bf16[16,1024,1024]{1,2,0:T(8,128)(2,1)} %fusion.5), kind=kOutput, calls=%fused_computation.64 | convolution fusion | flops 2419457024 | bytes 38277632 | tf_op jit(solution)/shard_map/ihqk,iqhd->ikhd/dot_general | solution.py:85
  489.0 64.5 %multiply_convert_fusion.clone.10 = bf16[16,1024,1024]{1,2,0:T(8,128)(2,1)} fusion(f32[16,1024,1024]{1,2,0:T(8,128)} %get-tuple-element.208, f32[16,1024]{1,0:T(8,128)S(1)} %copy-done.27, f32[1024]{0:T(1024)S(1)} %copy-done.29, bf16[1024,16,72]{0,2,1:T(8,128)(2,1)S(1)} %bitcast.201, bf16[1024,16,72]{0,2,1:T(8,128)(2,1)} %bitcast.204), kind=kOutput, calls=%fused_computation.1.clone.clone.clone.clone.clone.1 | convolution fusion | flops 5016404992 | bytes 105451520 | tf_op jit(solution)/shard_map/sub | solution.py:78
  560.7 73.2 %convert_reduce_fusion.5 = (f32[16,72]{1,0:T(8,128)S(1)}, bf16[16,72,1024]{2,1,0:T(8,128)(2,1)}) fusion(bf16[1024,16,72]{0,2,1:T(8,128)(2,1)} %bitcast.199, f32[16,1024,1024]{1,2,0:T(8,128)} %get-tuple-element.208, f32[16,1024]{1,0:T(8,128)S(1)} %copy-done.27, f32[1024]{0:T(1024)S(1)} %copy-done.29, bf16[1024,16,72]{0,2,1:T(8,128)(2,1)} %bitcast.202, ...), kind=kOutput, calls=%fused_computation.65 | convolution fusion | flops 7435862016 | bytes 76620288 | tf_op jit(solution)/shard_map/ihqk,ikhd->iqhd/dot_general | solution.py:79
  651.2 17.0 %convolution_convert_fusion.2 = bf16[1152,3456]{0,1:T(8,128)(2,1)} fusion(bf16[1024,1152]{1,0:T(8,128)(2,1)S(1)} %bitcast.215, bf16[1,1024,1152]{1,2,0:T(8,128)(2,1)S(1)} %bitcast.209, bf16[1,1024,1152]{1,2,0:T(8,128)(2,1)S(1)} %bitcast.210, bf16[1,1024,1152]{1,2,0:T(8,128)(2,1)S(1)} %bitcast.228), kind=kOutput, calls=%fused_computation.25 | convolution fusion | flops 8178941952 | bytes 17399808 | tf_op jit(solution)/shard_map/ird,ire->de/dot_general | solution.py:275
  668.9 19.6 %convolution_convert_fusion.1 = bf16[1152,4608]{0,1:T(8,128)(2,1)} fusion(bf16[1024,4608]{1,0:T(8,128)(2,1)} %get-tuple-element.193, f32[1024,1152]{1,0:T(8,128)} %copy-done.4, f32[1152]{0:T(1024)S(1)} %copy-done.57, f32[1152]{0:T(1024)S(1)} %copy-done.59, f32[1024]{0:T(1024)S(1)} %copy-done.66, f32[1024]{0:T(1024)S(1)} %copy-done.52), kind=kOutput, calls=%fused_computation.15 | convolution fusion | flops 10882842624 | bytes 24790016 | tf_op jit(solution)/shard_map/ird,irf->df/dot_general | solution.py:241
  690.2 19.1 %convolution_convert_fusion = bf16[4608,1152]{0,1:T(8,128)(2,1)} fusion(bf16[1024,1152]{1,0:T(8,128)(2,1)S(1)} %copy-done.21, f32[1024,4608]{1,0:T(8,128)} %fusion.98, f32[4608]{0:T(1024)S(1)} %copy-done.49), kind=kOutput, calls=%fused_computation.14 | convolution fusion | flops 10924130304 | bytes 31868928 | tf_op jit(solution)/shard_map/irf,ird->fd/dot_general | solution.py:234
  746.9 18.7 %fusion.45 = (f32[1152]{0:T(1024)S(1)}, f32[1024]{0:T(1024)S(1)}, f32[1024]{0:T(1024)S(1)}, f32[1152]{0:T(1024)S(1)}, f32[1024,1152]{1,0:T(8,128)}) fusion(bf16[4,256,1152]{2,1,0:T(8,128)(2,1)S(1)} %copy-done.1, f32[1024]{0:T(1024)S(1)} %copy-done.40, f32[1024]{0:T(1024)S(1)} %bitcast.223, f32[1152]{0:T(1024)S(1)} %copy-done.31, ...), kind=kOutput, calls=%fused_computation.57 | convolution fusion | flops 8186753024 | bytes 22148608 | tf_op jit(solution)/shard_map/ire,de->ird/dot_general | solution.py:277
  765.6 58.2 %reduce-scatter.24.cloned.1.call-done = bf16[1152,576]{0,1:T(8,128)(2,1)} async-done(((bf16[1152,4608]{0,1:T(8,128)(2,1)}), bf16[1152,576]{0,1:T(8,128)(2,1)}) %reduce-scatter.24.cloned.1.call-update) | async-done | bytes 1327120 | tf_op jit(solution)/shard_map/reduce_scatter | solution.py:149
  863.0 46.4 %reduce-scatter.26.cloned.1.call-done = bf16[4608,144]{0,1:T(8,128)(2,1)} async-done(((bf16[4608,1152]{0,1:T(8,128)(2,1)}), bf16[4608,144]{0,1:T(8,128)(2,1)}) %reduce-scatter.26.cloned.1.call-update) | async-done | bytes 1327120 | tf_op jit(solution)/shard_map/reduce_scatter | solution.py:149
  925.9 81.4 %all-gather.3 = f32[32,1,6912]{2,1,0:T(1,128)S(1)} all-gather(f32[1,1,6912]{2,1,0:T(1,128)S(1)} %reshape.759), channel_id=1, replica_groups=mesh['img'=8,'band'=4] {'img','band'}, dimensions={0}, use_global_device_ids=true | all-gather | bytes 912384 | tf_op jit(solution)/shard_map/all_gather | solution.py:307
  1044.7 47.1 %reduce-scatter.36.cloned.1.call-done = bf16[1152,144]{1,0:T(8,128)(2,1)} async-done(((bf16[4608,144]{1,0:T(8,128)(2,1)}), bf16[1152,144]{1,0:T(8,128)(2,1)}) %reduce-scatter.36.cloned.1.call-update) | async-done | bytes 331792
  1100.1 39.7 %psum.15 = f32[]{:T(128)} all-reduce(f32[]{:T(128)S(6)} %add.353), channel_id=1, replica_groups=mesh['img'=8,'band'=4] {'img','band'}, use_global_device_ids=true, to_apply=%region_40.41 | all-reduce | flops 1 | bytes 8 | tf_op jit(solution)/shard_map/psum | solution.py:335
  (317 shorter events, 307.4 us)
Async XLA Ops:
  7.2 66.6 %all-gather.15.cloned.1.call-start = ((), (), s32[]{:S(2)}) async-start(), calls=%async_computation.16 | async-start | bytes 1843200 | tf_op jit(solution)/shard_map/all_gather | solution.py:145
  9.2 157.8 %all-gather.19.cloned.1.call-start = ((), (), s32[]{:S(2)}) async-start(), calls=%async_computation.18 | async-start | bytes 1658880 | tf_op jit(solution)/shard_map/all_gather | solution.py:145
  11.1 209.8 %all-gather.11.cloned.1.call-start = ((), (), s32[]{:S(2)}) async-start(), calls=%async_computation.14 | async-start | bytes 8957952 | tf_op jit(solution)/shard_map/all_gather | solution.py:146
  55.3 298.6 %all-gather.13.cloned.1.call-start = ((), (), s32[]{:S(2)}) async-start(), calls=%async_computation.15 | async-start | bytes 2985984 | tf_op jit(solution)/shard_map/all_gather | solution.py:146
  73.8 291.3 %all-gather.17.cloned.1.call-start = ((), (), s32[]{:S(2)}) async-start(), calls=%async_computation.17 | async-start | bytes 11943936 | tf_op jit(solution)/shard_map/all_gather | solution.py:146
  100.8 58.2 %all-to-all-start = ((bf16[4,256,1152]{2,1,0:T(8,128)(2,1)}), bf16[4,256,1152]{2,1,0:T(8,128)(2,1)S(1)}, u32[]{:S(2)}, u32[]{:S(2)}) async-start(bf16[4,256,1152]{2,1,0:T(8,128)(2,1)} %param.22), calls=%async_computation | async-start | bytes 4718592 | tf_op jit(solution)/shard_map/all_to_all | solution.py:139
  159.0 194.9 %copy-start = (bf16[4,256,1152]{2,1,0:T(8,128)(2,1)}, bf16[4,256,1152]{2,1,0:T(8,128)(2,1)S(1)}, u32[]{:S(2)}) copy-start(bf16[4,256,1152]{2,1,0:T(8,128)(2,1)S(1)} %all-to-all-done) | copy-start | bytes 7077892
  159.0 58.2 %all-to-all-start.3 = ((bf16[4,256,1152]{2,1,0:T(8,128)(2,1)}), bf16[4,256,1152]{2,1,0:T(8,128)(2,1)}, u32[]{:S(2)}, u32[]{:S(2)}) async-start(bf16[4,256,1152]{2,1,0:T(8,128)(2,1)} %param.25), calls=%async_computation.3 | async-start | bytes 4718592 | tf_op jit(solution)/shard_map/all_to_all | solution.py:139
  163.5 222.5 %all-gather.21.cloned.1.call-start = ((), (), s32[]{:S(2)}) async-start(), calls=%async_computation.19 | async-start | bytes 11943936 | tf_op jit(solution)/shard_map/all_gather | solution.py:146
  163.8 269.1 %copy-start.48 = (f32[4608]{0:T(1024)}, f32[4608]{0:T(1024)S(1)}, u32[]{:S(2)}) copy-start(f32[4608]{0:T(1024)S(1)} %add.332) | copy-start | bytes 55300
  167.0 186.9 %copy-start.44 = (f32[1152]{0:T(1024)}, f32[1152]{0:T(1024)S(1)}, u32[]{:S(2)}) copy-start(f32[1152]{0:T(1024)S(1)} %get-tuple-element.171) | copy-start | bytes 13828
  167.0 198.1 %copy-start.56 = (f32[1152]{0:T(1024)}, f32[1152]{0:T(1024)S(1)}, u32[]{:S(2)}) copy-start(f32[1152]{0:T(1024)S(1)} %get-tuple-element.167) | copy-start | bytes 13828
  167.0 265.8 %copy-start.58 = (f32[1152]{0:T(1024)}, f32[1152]{0:T(1024)S(1)}, u32[]{:S(2)}) copy-start(f32[1152]{0:T(1024)S(1)} %get-tuple-element.168) | copy-start | bytes 13828
  167.1 546.3 %reduce-scatter.22.cloned.1.call-start = ((), (), s32[]{:S(2)}) async-start(), calls=%async_computation.21 | async-start | bytes 2985984 | tf_op jit(solution)/shard_map/reduce_scatter | solution.py:149
  560.6 183.7 %reduce-scatter.20.cloned.1.call-start = ((), (), s32[]{:S(2)}) async-start(), calls=%async_computation.20 | async-start | bytes 8957952 | tf_op jit(solution)/shard_map/reduce_scatter | solution.py:149
  668.2 155.6 %reduce-scatter.24.cloned.1.call-start = ((), (), s32[]{:S(2)}) async-start(), calls=%async_computation.22 | async-start | bytes 11943936 | tf_op jit(solution)/shard_map/reduce_scatter | solution.py:149
  688.6 220.9 %reduce-scatter.26.cloned.1.call-start = ((), (), s32[]{:S(2)}) async-start(), calls=%async_computation.23 | async-start | bytes 11943936 | tf_op jit(solution)/shard_map/reduce_scatter | solution.py:149
  709.3 301.2 %reduce-scatter.28.cloned.1.call-start = ((), (), s32[]{:S(2)}) async-start(), calls=%async_computation.24 | async-start | bytes 663552
  713.3 321.4 %reduce-scatter.32.cloned.1.call-start = ((), (), s32[]{:S(2)}) async-start(), calls=%async_computation.26 | async-start | bytes 737280
  739.6 118.5 %all-to-all-start.2 = ((bf16[4,2,147456]{2,1,0:T(2,128)(2,1)}), bf16[4,2,147456]{2,1,0:T(2,128)(2,1)}, u32[]{:S(2)}, u32[]{:S(2)}) async-start(bf16[4,2,147456]{2,1,0:T(2,128)(2,1)} %reshape.788), calls=%async_computation.2 | async-start | bytes 4718592 | tf_op jit(solution)/shard_map/all_to_all | solution.py:142
  744.3 292.2 %reduce-scatter.30.cloned.1.call-start = ((), (), s32[]{:S(2)}) async-start(), calls=%async_computation.25 | async-start | bytes 1474560
  746.8 295.8 %reduce-scatter.34.cloned.1.call-start = ((), (), s32[]{:S(2)}) async-start(), calls=%async_computation.27 | async-start | bytes 1843200
  858.1 173.1 %all-to-all-start.4 = ((bf16[4,2,147456]{2,1,0:T(2,128)(2,1)}), bf16[4,2,147456]{2,1,0:T(2,128)(2,1)S(1)}, u32[]{:S(2)}, u32[]{:S(2)}) async-start(bf16[4,2,147456]{2,1,0:T(2,128)(2,1)} %reshape.786), calls=%async_computation.4 | async-start | bytes 4718592 | tf_op jit(solution)/shard_map/all_to_all | solution.py:142
  863.0 228.8 %reduce-scatter.36.cloned.1.call-start = ((), (), s32[]{:S(2)}) async-start(), calls=%async_computation.28 | async-start | bytes 2949120
  (66 other events, 1297.1 us)
Sparse Core Ops, SparseCore 0:
  10.2 54.0 all-gather.14
  66.4 34.7 all-gather.18
  103.6 51.4 all-gather.10
  157.4 30.2 all-gather.12
  189.4 63.8 all-gather.16
  255.0 63.8 all-gather.20
  560.7 43.4 reduce-scatter.21
  668.4 69.6 reduce-scatter.19
  741.6 82.1 reduce-scatter.23
  827.2 82.1 reduce-scatter.25
  913.1 34.3 reduce-scatter.27
  950.2 23.5 reduce-scatter.31
  976.1 31.1 reduce-scatter.29
  1009.5 33.1 reduce-scatter.33
  1044.9 46.8 reduce-scatter.35

commit v2 on v1

--- a/solution.py
+++ b/solution.py
@@ -1,6 +1,10 @@
+import functools
+
 import jax
 import jax.numpy as jnp
 from jax import lax
+from jax.experimental import pallas as pl
+from jax.experimental.pallas import tpu as pltpu
 from jax.sharding import PartitionSpec as P
 
 HEADS = 16
@@ -47,48 +51,180 @@
     return (weight - rate * first_hat / (jnp.sqrt(second_hat) + adam_eps), first_new, second_new)
 
 
-def attention_forward(query_heads, key_heads, value_heads, key_bias, score_scale):
-    scores = (
-        jnp.einsum("iqhd,ikhd->ihqk", query_heads, key_heads, preferred_element_type=jnp.float32)
-        * score_scale
-        + key_bias
-    )
-    top_score = jnp.max(scores, axis=-1, keepdims=True)
-    log_total = top_score + jnp.log(jnp.sum(jnp.exp(scores - top_score), axis=-1, keepdims=True))
-    probs_low = jnp.exp(scores - log_total).astype(jnp.bfloat16)
-    mixed = jnp.einsum(
-        "ihqk,ikhd->iqhd", probs_low, value_heads, preferred_element_type=jnp.float32
-    )
-    return (mixed, log_total)
-
-
-def attention_backward(
-    query_heads, key_heads, value_heads, key_bias, score_scale, log_total, mixed_heads_grad
+WINDOW = 256
+CONTRACT_LAST = (((1,), (1,)), ((), ()))
+LOG2_E = 1.4426950408889634
+
+
+def head_window(head, features):
+    start = head * HEAD_DIM
+    base = pl.multiple_of(jnp.minimum(start // 128 * 128, features - WINDOW), 128)
+    lane = lax.broadcasted_iota(jnp.int32, (1, WINDOW), 1)
+    inside = (lane >= start - base) & (lane < start - base + HEAD_DIM)
+    return base, inside
+
+
+def attention_forward_kernel(
+    query_ref, keyval_ref, bias_ref, mixed_ref, log_ref, scaled, value_t, mixed_t, *, features, shift, block
 ):
-    scores = (
-        jnp.einsum("iqhd,ikhd->ihqk", query_heads, key_heads, preferred_element_type=jnp.float32)
-        * score_scale
-        + key_bias
-    )
-    probs_full = jnp.exp(scores - log_total)
-    prob_grad = jnp.einsum(
-        "iqhd,ikhd->ihqk", mixed_heads_grad, value_heads, preferred_element_type=jnp.float32
-    )
-    inner_sum = jnp.sum(probs_full * prob_grad, axis=-1, keepdims=True)
-    score_grad = (probs_full * (prob_grad - inner_sum) * score_scale).astype(jnp.bfloat16)
-    query_grad = jnp.einsum(
-        "ihqk,ikhd->iqhd", score_grad, key_heads, preferred_element_type=jnp.float32
-    )
-    key_part = jnp.einsum(
-        "ihqk,iqhd->ikhd", score_grad, query_heads, preferred_element_type=jnp.float32
-    )
-    value_part = jnp.einsum(
-        "ihqk,iqhd->ikhd",
-        probs_full.astype(jnp.bfloat16),
-        mixed_heads_grad,
-        preferred_element_type=jnp.float32,
-    )
-    return (query_grad, key_part, value_part)
+    length = keyval_ref.shape[0]
+    rows = mixed_ref.shape[0]
+    scaled[...] = (query_ref[:, :features].astype(jnp.float32) * (HEAD_DIM**-0.5 * LOG2_E)).astype(
+        jnp.bfloat16
+    )
+
+    @pl.loop(0, features // 128)
+    def _(tile):
+        columns = pl.ds(pl.multiple_of(tile * 128, 128), 128)
+        source = pl.ds(pl.multiple_of(shift + features + tile * 128, 128), 128)
+        value_t[columns, :] = keyval_ref[:, source].astype(jnp.float32).T
+
+    @pl.loop(0, HEADS)
+    def _(head):
+        base, inside = head_window(head, features)
+        head_rows = pl.ds(pl.multiple_of(head * HEAD_DIM, 8), HEAD_DIM)
+        query = scaled[:, pl.ds(base, WINDOW)]
+        ones = jnp.ones((8, block), jnp.float32)
+        top = None
+        for at in range(0, length, block):
+            key = keyval_ref[pl.ds(at, block), pl.ds(pl.multiple_of(base + shift, 128), WINDOW)]
+            key = jnp.where(inside, key, jnp.zeros_like(key))
+            scores = lax.dot_general(key, query, CONTRACT_LAST, preferred_element_type=jnp.float32)
+            if at + block == length:
+                scores = scores + bias_ref[pl.ds(at, block), :]
+            block_top = jnp.max(scores, axis=0, keepdims=True)
+            value = jnp.concatenate([value_t[head_rows, pl.ds(at, block)], ones], axis=0).astype(jnp.bfloat16)
+            if top is None:
+                top = block_top
+                probs = jnp.exp2(scores - top).astype(jnp.bfloat16)
+                total = jnp.dot(value, probs, preferred_element_type=jnp.float32)
+            else:
+                new_top = jnp.maximum(top, block_top)
+                fade = jnp.exp2(top - new_top)
+                top = new_top
+                probs = jnp.exp2(scores - top).astype(jnp.bfloat16)
+                total = total * fade + jnp.dot(value, probs, preferred_element_type=jnp.float32)
+        weight = total[HEAD_DIM : HEAD_DIM + 1]
+        mixed_t[head_rows, :] = total[:HEAD_DIM] * (1.0 / weight)
+        log_ref[pl.ds(head, 1), :] = top + jnp.log2(weight)
+
+    @pl.loop(0, features // 128)
+    def _(tile):
+        columns = pl.ds(pl.multiple_of(tile * 128, 128), 128)
+        mixed_ref[:, columns] = mixed_t[columns, :].T.astype(jnp.bfloat16)
+
+
+def attention_forward(query, keyval, key_bias, features, shift, block):
+    rows, length = query.shape[0], keyval.shape[0]
+    return pl.pallas_call(
+        functools.partial(attention_forward_kernel, features=features, shift=shift, block=block),
+        out_shape=(
+            jax.ShapeDtypeStruct((rows, features), jnp.bfloat16),
+            jax.ShapeDtypeStruct((HEADS, rows), jnp.float32),
+        ),
+        scratch_shapes=[
+            pltpu.VMEM((rows, features), jnp.bfloat16),
+            pltpu.VMEM((features, length), jnp.float32),
+            pltpu.VMEM((features, rows), jnp.float32),
+        ],
+        compiler_params=pltpu.CompilerParams(vmem_limit_bytes=56 * 2**20),
+    )(query, keyval, key_bias)
+
+
+def attention_backward_kernel(
+    query_ref, keyval_ref, bias_ref, mixed_ref, grad_ref, log_ref, out_ref, keyval_grad_ref,
+    scaled, key_t, wide_t, *, features, shift, out_shift, block
+):
+    length = keyval_ref.shape[0]
+    rows = mixed_ref.shape[0]
+    scale = HEAD_DIM**-0.5
+    scaled[...] = (query_ref[:, :features].astype(jnp.float32) * (scale * LOG2_E)).astype(jnp.bfloat16)
+
+    @pl.loop(0, features // 128)
+    def _(tile):
+        columns = pl.ds(pl.multiple_of(tile * 128, 128), 128)
+        key_t[columns, :] = keyval_ref[:, pl.ds(pl.multiple_of(shift + tile * 128, 128), 128)].astype(jnp.float32).T
+        wide_t[columns, :] = (
+            mixed_ref[:, columns].astype(jnp.float32) * grad_ref[:, columns].astype(jnp.float32)
+        ).T
+
+    @pl.loop(0, HEADS)
+    def _(head):
+        base, inside = head_window(head, features)
+        head_rows = pl.ds(pl.multiple_of(head * HEAD_DIM, 8), HEAD_DIM)
+        window = pl.ds(base, WINDOW)
+        delta = jnp.sum(wide_t[head_rows, :], axis=0, keepdims=True)
+        log_total = log_ref[pl.ds(head, 1), :]
+        query = query_ref[:, window]
+        query_scaled = scaled[:, window]
+        grad = grad_ref[:, window]
+        query_grad = None
+        for at in range(0, length, block):
+            here = pl.ds(at, block)
+            key_window = pl.ds(pl.multiple_of(base + shift, 128), WINDOW)
+            value_window = pl.ds(pl.multiple_of(base + shift + features, 128), WINDOW)
+            key = keyval_ref[here, key_window]
+            value = keyval_ref[here, value_window]
+            key = jnp.where(inside, key, jnp.zeros_like(key))
+            value = jnp.where(inside, value, jnp.zeros_like(value))
+            scores = lax.dot_general(key, query_scaled, CONTRACT_LAST, preferred_element_type=jnp.float32)
+            if at + block == length:
+                scores = scores + bias_ref[here, :]
+            probs = jnp.exp2(scores - log_total)
+            prob_grad = lax.dot_general(value, grad, CONTRACT_LAST, preferred_element_type=jnp.float32)
+            score_grad = (probs * (prob_grad - delta)).astype(jnp.bfloat16)
+            value_grad = jnp.dot(probs.astype(jnp.bfloat16), grad, preferred_element_type=jnp.float32)
+            key_grad = jnp.dot(score_grad, query, preferred_element_type=jnp.float32) * scale
+            key_out = pl.ds(pl.multiple_of(base + out_shift, 128), WINDOW)
+            value_out = pl.ds(pl.multiple_of(base + out_shift + features, 128), WINDOW)
+            keyval_grad_ref[here, key_out] = jnp.where(inside, key_grad.astype(jnp.bfloat16), keyval_grad_ref[here, key_out])
+            keyval_grad_ref[here, value_out] = jnp.where(inside, value_grad.astype(jnp.bfloat16), keyval_grad_ref[here, value_out])
+            part = jnp.dot(
+                key_t[head_rows, here].astype(jnp.bfloat16), score_grad, preferred_element_type=jnp.float32
+            )
+            query_grad = part if query_grad is None else query_grad + part
+        wide_t[head_rows, :] = query_grad * scale
+
+    @pl.loop(0, features // 128)
+    def _(tile):
+        columns = pl.ds(pl.multiple_of(tile * 128, 128), 128)
+        out_ref[:, columns] = wide_t[columns, :].T.astype(jnp.bfloat16)
+
+
+def attention_backward(query, keyval, key_bias, mixed, grad, log_total, features, block):
+    rows, length = query.shape[0], keyval.shape[0]
+    shared = query is keyval
+    scratch = [
+        pltpu.VMEM((rows, features), jnp.bfloat16),
+        pltpu.VMEM((features, length), jnp.float32),
+        pltpu.VMEM((features, rows), jnp.float32),
+    ]
+    params = pltpu.CompilerParams(vmem_limit_bytes=56 * 2**20)
+    if shared:
+
+        def shared_kernel(both_ref, bias_ref, mixed_ref, grad_ref, log_ref, out_ref, *held):
+            attention_backward_kernel(
+                both_ref, both_ref, bias_ref, mixed_ref, grad_ref, log_ref, out_ref, out_ref, *held,
+                features=features, shift=features, out_shift=features, block=block,
+            )
+
+        return pl.pallas_call(
+            shared_kernel,
+            out_shape=jax.ShapeDtypeStruct((rows, 3 * features), jnp.bfloat16),
+            scratch_shapes=scratch,
+            compiler_params=params,
+        )(query, key_bias, mixed, grad, log_total)
+    return pl.pallas_call(
+        functools.partial(
+            attention_backward_kernel, features=features, shift=0, out_shift=0, block=block
+        ),
+        out_shape=(
+            jax.ShapeDtypeStruct((rows, features), jnp.bfloat16),
+            jax.ShapeDtypeStruct((length, 2 * features), jnp.bfloat16),
+        ),
+        scratch_shapes=scratch,
+        compiler_params=params,
+    )(query, keyval, key_bias, mixed, grad, log_total)
 
 
 def body(
@@ -139,25 +275,47 @@
         return lax.all_to_all(rows, "band", split_axis=0, concat_axis=1, axis_index_groups=exchange_groups, tiled=True)
 
     def to_bands(whole):
-        return lax.all_to_all(whole, "band", split_axis=1, concat_axis=0, axis_index_groups=exchange_groups, tiled=True)
+        cut = whole.reshape(own, mates, local_rows, features).transpose(1, 0, 2, 3)
+        back = lax.all_to_all(
+            cut, "band", split_axis=0, concat_axis=0, axis_index_groups=exchange_groups, tiled=True
+        )
+        return back.reshape(images, local_rows, features)
+
+    def after(value, *earlier):
+        return lax.optimization_barrier((value,) + earlier)[0]
+
+    def sum_everywhere(partial):
+        sent = jnp.broadcast_to(partial, (img_count * band_count, 128))
+        got = lax.all_to_all(sent, ("img", "band"), split_axis=0, concat_axis=0, tiled=True)
+        return jnp.sum(got[:, 0])
 
     def gather_weight(weight):
         rows = lax.all_gather(weight.astype(low_type), "band", axis=0, tiled=True)
         return lax.all_gather(rows, "img", axis=1, tiled=True)
 
     def scatter_grad(grad):
-        columns = lax.psum_scatter(grad.astype(low_type), "img", scatter_dimension=1, tiled=True)
+        columns = lax.psum_scatter(grad, "img", scatter_dimension=1, tiled=True)
         return lax.psum_scatter(columns, "band", scatter_dimension=0, tiled=True).astype(jnp.float32)
 
-    condition_all = lax.all_gather(condition, "img", axis=0, tiled=True)
+    bias_rows, bias_columns = biases.shape
+    small = lax.all_gather(
+        jnp.concatenate([condition.reshape(1, -1), biases.astype(low_type).reshape(1, -1)], axis=1),
+        "img",
+        axis=0,
+        tiled=True,
+    )
+    condition_all = small[:, : images * features].reshape(img_count * images, features)
+    bias_vals = (
+        small[:, images * features :]
+        .astype(jnp.float32)
+        .reshape(img_count, bias_rows, bias_columns)
+        .transpose(1, 0, 2)
+        .reshape(bias_rows, features)
+    )
     tokens_low = to_images(inputs)
-    bias_vals = lax.all_gather(biases.astype(low_type), "img", axis=1, tiled=True).astype(
-        jnp.float32
-    )
     qkv_full = gather_weight(qkv_weight)
     out_full = gather_weight(out_weight)
     up_full = gather_weight(up_weight)
-    cotangent_low = to_images(cotangent)
     down_full = gather_weight(down_weight)
 
     silu_all = jax.nn.silu(condition_all.astype(jnp.float32)).astype(low_type)
@@ -192,25 +350,34 @@
     key_mask = jnp.arange(length, dtype=jnp.int32)[None, :] < valid_own[:, None]
     positions = lax.div(band_rank, mates) * image_rows + jnp.arange(image_rows, dtype=jnp.int32)
     row_mask = (positions[None, :] < valid_own[:, None]).astype(jnp.float32)[:, :, None]
-    key_bias = jnp.where(key_mask, 0.0, very_low).astype(jnp.float32)[:, None, None, :]
     tokens_in = tokens_low.astype(jnp.float32)
     normed_one, inverse_one = normalize_keep(tokens_in)
     first_in = (normed_one * (1.0 + scale_one) + shift_one).astype(jnp.bfloat16)
+    cotangent_low = to_images(after(cotangent, tokens_low))
     grad_out = cotangent_low.astype(jnp.float32) * row_mask
     qkv_bias = jnp.concatenate([bias_vals[6], jnp.zeros((features,), jnp.float32), bias_vals[7]])
     projected = (
         jnp.einsum("ird,de->ire", first_in, qkv_full, preferred_element_type=jnp.float32) + qkv_bias
     ).astype(jnp.bfloat16)
-    query_heads = projected[..., :features].reshape(own, image_rows, head_count, head_size)
-    keys_values = projected[..., features:]
+    key_bias = jnp.where(key_mask, 0.0, very_low).astype(jnp.float32)[:, :, None]
+    queries = [projected[i] for i in range(own)]
     if split > 1:
         keys_values = lax.all_gather(
-            keys_values, "band", axis=1, axis_index_groups=share_groups, tiled=True
+            projected[..., features:], "band", axis=1, axis_index_groups=share_groups, tiled=True
         )
-    key_heads = keys_values[..., :features].reshape(own, length, head_count, head_size)
-    value_heads = keys_values[..., features:].reshape(own, length, head_count, head_size)
-    mixed, log_total = attention_forward(query_heads, key_heads, value_heads, key_bias, score_scale)
-    mixed = mixed.reshape(own, image_rows, features).astype(jnp.bfloat16)
+        keys_values = [keys_values[i] for i in range(own)]
+        key_shift = 0
+    else:
+        keys_values = queries
+        key_shift = features
+    mixed, log_total = zip(
+        *[
+            attention_forward(queries[i], keys_values[i], key_bias[i], features, key_shift, 512)
+            for i in range(own)
+        ]
+    )
+    mixed_parts = mixed
+    mixed = jnp.stack(mixed)
     attended = (
         jnp.einsum("ird,de->ire", mixed, out_full, preferred_element_type=jnp.float32)
         + bias_vals[8]
@@ -230,17 +397,22 @@
     output = to_bands((middle + gate_two * branch).astype(jnp.bfloat16))
     branch_grad = (gate_two * grad_out).astype(jnp.bfloat16)
     gate_two_grad = jnp.sum(grad_out * branch, axis=1)
-    down_shard = scatter_grad(
-        jnp.einsum("irf,ird->fd", hidden_low, branch_grad, preferred_element_type=jnp.float32)
-    )
+    down_grad = jnp.einsum(
+        "irf,ird->fd", hidden_low, branch_grad, preferred_element_type=jnp.float32
+    ).astype(low_type)
+    down_shard = scatter_grad(down_grad)
     hidden_grad = jnp.einsum(
-        "ird,fd->irf", branch_grad, down_full, preferred_element_type=jnp.float32
+        "ird,fd->irf",
+        after(branch_grad, down_grad),
+        down_full,
+        preferred_element_type=jnp.float32,
     )
     pre_grad = gelu_back(hidden_grad)[0].astype(jnp.bfloat16)
-    up_shard = scatter_grad(
-        jnp.einsum("ird,irf->df", second_in, pre_grad, preferred_element_type=jnp.float32)
-    )
-    second_grad = jnp.einsum("irf,df->ird", pre_grad, up_full, preferred_element_type=jnp.float32)
+    up_grad = jnp.einsum(
+        "ird,irf->df", second_in, pre_grad, preferred_element_type=jnp.float32
+    ).astype(low_type)
+    up_shard = scatter_grad(up_grad)
+    second_grad = jnp.einsum("irf,df->ird", after(pre_grad, up_grad), up_full, preferred_element_type=jnp.float32)
     shift_two_grad = jnp.sum(second_grad, axis=1)
     scale_two_grad = jnp.sum(second_grad * normed_two, axis=1)
     middle_grad = grad_out + normalize_back(
@@ -248,33 +420,39 @@
     )
     attended_grad = (gate_one * middle_grad).astype(jnp.bfloat16)
     gate_one_grad = jnp.sum(middle_grad * attended, axis=1)
-    out_shard = scatter_grad(
-        jnp.einsum("ird,ire->de", mixed, attended_grad, preferred_element_type=jnp.float32)
-    )
+    out_grad = jnp.einsum(
+        "ird,ire->de", mixed, attended_grad, preferred_element_type=jnp.float32
+    ).astype(low_type)
+    out_shard = scatter_grad(out_grad)
     mixed_grad = jnp.einsum(
-        "ire,de->ird", attended_grad, out_full, preferred_element_type=jnp.float32
+        "ire,de->ird", after(attended_grad, out_grad), out_full, preferred_element_type=jnp.float32
     ).astype(jnp.bfloat16)
-    mixed_heads_grad = mixed_grad.reshape(own, image_rows, head_count, head_size)
-    query_part, key_part, value_part = attention_backward(
-        query_heads, key_heads, value_heads, key_bias, score_scale, log_total, mixed_heads_grad
-    )
-    query_grad = query_part.reshape(own, image_rows, features).astype(jnp.bfloat16)
-    key_part = key_part.reshape(own, length, features)
-    value_part = value_part.reshape(own, length, features)
+    attention_grads = [
+        attention_backward(
+            queries[i], keys_values[i], key_bias[i], mixed_parts[i], mixed_grad[i], log_total[i],
+            features, 512,
+        )
+        for i in range(own)
+    ]
     if split > 1:
-        key_part, value_part = (
-            lax.psum_scatter(
-                part, "band", scatter_dimension=1, axis_index_groups=share_groups, tiled=True
-            )
-            for part in (key_part, value_part)
+        shared_grads = lax.psum_scatter(
+            jnp.stack([pair[1] for pair in attention_grads]),
+            "band",
+            scatter_dimension=1,
+            axis_index_groups=share_groups,
+            tiled=True,
         )
-    key_grad_low = key_part.astype(jnp.bfloat16)
-    value_grad_low = value_part.astype(jnp.bfloat16)
-    qkv_grad = jnp.concatenate([query_grad, key_grad_low, value_grad_low], axis=-1)
-    qkv_shard = scatter_grad(
-        jnp.einsum("ird,ire->de", first_in, qkv_grad, preferred_element_type=jnp.float32)
-    )
-    first_grad = jnp.einsum("ire,de->ird", qkv_grad, qkv_full, preferred_element_type=jnp.float32)
+        qkv_grad = jnp.concatenate(
+            [jnp.stack([pair[0] for pair in attention_grads]), shared_grads], axis=-1
+        )
+    else:
+        qkv_grad = jnp.stack(attention_grads)
+    qkv_sums = jnp.sum(qkv_grad.astype(jnp.float32), axis=(0, 1))
+    qkv_weight_grad = jnp.einsum(
+        "ird,ire->de", first_in, qkv_grad, preferred_element_type=jnp.float32
+    ).astype(low_type)
+    qkv_shard = scatter_grad(qkv_weight_grad)
+    first_grad = jnp.einsum("ire,de->ird", after(qkv_grad, qkv_weight_grad), qkv_full, preferred_element_type=jnp.float32)
     shift_one_grad = jnp.sum(first_grad, axis=1)
     scale_one_grad = jnp.sum(first_grad * normed_one, axis=1)
     input_grad = to_bands(
@@ -296,19 +474,31 @@
     )
     row_sums = jnp.concatenate(
         [
-            jnp.sum(query_grad.astype(jnp.float32), axis=(0, 1))[None],
-            jnp.sum(value_grad_low.astype(jnp.float32), axis=(0, 1))[None],
+            qkv_sums[:features][None],
+            qkv_sums[2 * features :][None],
             jnp.sum(attended_grad.astype(jnp.float32), axis=(0, 1))[None],
             jnp.sum(pre_grad.astype(jnp.float32), axis=(0, 1)).reshape(4, features),
             jnp.sum(branch_grad.astype(jnp.float32), axis=(0, 1))[None],
         ],
         axis=0,
     )
-    mod_all = lax.all_gather(
-        mod_grad.reshape(own, 6 * features), ("img", "band"), axis=0, tiled=True
-    )
-    bias_columns = biases.shape[1]
-    mod_columns = lax.dynamic_slice_in_dim(mod_all, img_rank * ada_columns, ada_columns, axis=1)
+    pieces = jnp.concatenate(
+        [
+            mod_grad.reshape(own, img_count, ada_columns)
+            .transpose(1, 0, 2)
+            .reshape(img_count, own * ada_columns),
+            jnp.concatenate([jnp.sum(mod_grad, axis=0).reshape(6, features), row_sums], axis=0)
+            .reshape(bias_rows, img_count, bias_columns)
+            .transpose(1, 0, 2)
+            .reshape(img_count, -1),
+        ],
+        axis=1,
+    )
+    sent = jnp.broadcast_to(pieces[:, None], (img_count, band_count, pieces.shape[1])).reshape(
+        img_count * band_count, -1
+    )
+    got = lax.all_to_all(sent, ("img", "band"), split_axis=0, concat_axis=0, tiled=True)
+    mod_columns = got[:, : own * ada_columns].reshape(-1, ada_columns)
     silu_terms = jnp.tile(
         silu_rows.astype(jnp.float32).reshape(img_count, 1, images, ada_rows), (1, split, 1, 1)
     ).reshape(img_count * band_count * own, ada_rows)
@@ -318,21 +508,12 @@
         mod_columns,
         precision=lax.Precision.HIGHEST,
     )
-    mod_sums = lax.dynamic_slice_in_dim(
-        jnp.sum(mod_all, axis=0).reshape(6, features),
-        img_rank * bias_columns,
-        bias_columns,
-        axis=1,
-    )
-    sums_shard = lax.psum(
-        lax.psum_scatter(row_sums, "img", scatter_dimension=1, tiled=True), "band"
-    )
-    bias_total = jnp.concatenate([mod_sums, sums_shard], axis=0)
+    bias_total = jnp.sum(got[:, own * ada_columns :], axis=0).reshape(bias_rows, bias_columns)
     shards = (ada_shard, qkv_shard, out_shard, up_shard, down_shard)
     squares = jnp.sum(bias_total * bias_total) / band_count
     for shard_grad in shards:
         squares = squares + jnp.sum(shard_grad * shard_grad)
-    squares_total = lax.psum(squares, ("img", "band"))
+    squares_total = sum_everywhere(squares)
     grad_norm = jnp.sqrt(squares_total)
     factor = clip_norm / jnp.maximum(grad_norm, clip_norm)
     ada_new, ada_first_new, ada_second_new = adam_update(

time: 1180 us -> 958 us (0.81)
  matrix products: 421 us -> 202 us
  waiting for transfers between devices: 245 us -> 384 us
  blocking collectives: 221 us -> 82.5 us
  Pallas kernels: 0 us -> 93.6 us
  other arithmetic: 136 us -> 56.4 us
  local copies, waits for them, and re-layouts: 113 us -> 82.4 us
    dot_general x9 -> x4, matrix products: 223 us -> 71.4 us  [the longest x1 28 us: body(): jnp.einsum('ird,fd->irf', after(branch_grad, down_grad), down_full, prefe...]
    unnamed x20 -> x19, waiting for transfers between devices: 50.3 us -> 197 us
    pallas_call x0 -> x2, Pallas kernels: none -> 93.6 us  [the longest x1 57 us: attention_backward(): pl.pallas_call(shared_kernel, out_shape=jax.ShapeDtypeStruct((rows, 3 * f...]
    all_gather x3 -> x1, blocking collectives: 99.7 us -> 9.58 us  [body(): lax.all_gather(jnp.concatenate([condition.reshape(1, -1), biases.astype(l...]
    sub x1 -> x0, matrix products: 64.5 us -> none  [attention_backward(): prob_grad - inner_sum]
    psum x2 -> x0, blocking collectives: 48.2 us -> none  [the longest x1 39.7 us: body(): squares_total = lax.psum(squares, ('img', 'band'))]
    convert_element_type x2, other arithmetic: 33.7 us -> 0.02 us  [the longest x1 0.01 us: body(): silu_all = jax.nn.silu(condition_all.astype(jnp.float32)).astype(low_type)]
    reduce_scatter x4 -> x3, waiting for transfers between devices: 105 us -> 73.8 us  [scatter_grad(): lax.psum_scatter(columns, 'band', scatter_dimension=0, tiled=True)]
  transfers between devices with their start and end apart: 19 -> 20, of which waited for: 6 -> 11; matrix products, arithmetic and copies ran while one was open for 39% -> 23% of each run, Pallas kernels for 0% -> 10%
where the time goes in v2:
time: 958 us; the launch traced here: 949 us
  waiting for transfers between devices  384 us (40%)
  matrix products  202 us (21%)
  Pallas kernels  93.6 us (10%)
  blocking collectives  82.5 us (9%)
  local copies, waits for them, and re-layouts  82.4 us (9%)
  other arithmetic  56.4 us (6%)
  starting transfers between devices  27.2 us (3%)
  between operations  20.9 us (2%)
    unnamed x19, waiting for transfers between devices  197 us
    all_to_all x2, waiting for transfers between devices, to_images(): lax.all_to_all(rows, 'band', split_axis=0, concat_axis=1, axis_index_grou...  99.6 us
    reduce_scatter x3, waiting for transfers between devices, scatter_grad(): lax.psum_scatter(columns, 'band', scatter_dimension=0, tiled=True)  73.8 us
    unnamed x125, local copies, waits for them, and re-layouts  72.7 us
    all_gather x2, blocking collectives, gather_weight(): rows = lax.all_gather(weight.astype(low_type), 'band', axis=0, tiled=True)  58.4 us
    pallas_call x1, Pallas kernels, attention_backward(): pl.pallas_call(shared_kernel, out_shape=jax.ShapeDtypeStruct((rows, 3 * f...  57 us
    pallas_call x1, Pallas kernels, attention_forward(): pl.pallas_call(functools.partial(attention_forward_kernel, features=featu...  36.7 us
    dot_general x1, matrix products, body(): jnp.einsum('ird,fd->irf', after(branch_grad, down_grad), down_full, prefe...  28 us
  transfers between devices with their start and end apart: 20, of which 11 were waited for; matrix products, arithmetic and copies ran while one was open for 23% of the time, Pallas kernels for 10%

profile of v2, /device:TPU:0, one launch (start us, length us, event | category | flops | bytes accessed | tf_op | source)
XLA Modules:
  0.0 949.3 jit_solution(4724198012993304165)
XLA Ops:
  12.3 41.5 %all_gather.28 = bf16[1152,432]{1,0:T(8,128)(2,1)S(1)} all-gather(bf16[288,432]{1,0:T(8,128)(2,1)S(1)} %convert_element_type.217), channel_id=1, replica_groups=mesh['img'=8,'band'=4] {'band'}, dimensions={0}, use_global_device_ids=true | all-gather | bytes 1244160 | tf_op jit(solution)/shard_map/all_gather | solution.py:293
  55.4 16.9 %all-gather.1 = bf16[4,288,144]{1,2,0:T(8,128)(2,1)S(1)} all-gather(bf16[1,288,144]{1,2,0:T(8,128)(2,1)S(1)} %convert_bitcast_fusion), channel_id=1, replica_groups=mesh['img'=8,'band'=4] {'band'}, dimensions={0}, use_global_device_ids=true | all-gather | bytes 414720 | tf_op jit(solution)/shard_map/all_gather | solution.py:293
  86.5 14.5 %all_to_all.58 = f32[32,1,864]{2,1,0:T(1,128)S(1)} all-to-all(f32[32,1,864]{2,1,0:T(1,128)S(1)} %copy.189), channel_id=1, replica_groups=mesh['img'=8,'band'=4] {'img','band'}, dimensions={0} | all-to-all | bytes 221184 | tf_op jit(solution)/shard_map/all_to_all | solution.py:331
  105.4 53.8 %all-to-all-done = bf16[4,256,1152]{2,1,0:T(8,128)(2,1)S(1)} async-done(((bf16[4,256,1152]{2,1,0:T(8,128)(2,1)}), bf16[4,256,1152]{2,1,0:T(8,128)(2,1)S(1)}, u32[]{:S(2)}, u32[]{:S(2)}) %all-to-all-start) | async-done | bytes 2359328 | tf_op jit(solution)/shard_map/all_to_all | solution.py:275
  171.5 45.8 %all-to-all-done.3 = bf16[4,256,1152]{2,1,0:T(8,128)(2,1)} async-done(((bf16[4,256,1152]{2,1,0:T(8,128)(2,1)}), bf16[4,256,1152]{2,1,0:T(8,128)(2,1)}, u32[]{:S(2)}, u32[]{:S(2)}) %all-to-all-start.3) | async-done | bytes 2359328 | tf_op jit(solution)/shard_map/all_to_all | solution.py:275
  229.6 15.5 %add_convert_fusion.query_ref.keyval_ref.both_ref = bf16[1024,3456]{1,0:T(8,128)(2,1)} fusion(bf16[1024,1152]{1,0:T(8,128)(2,1)} %add_convert_fusion.4, bf16[1152,3456]{0,1:T(8,128)(2,1)} %all-gather.9.cloned.1.call-done, f32[3456]{0:T(1024)S(1)} %pad_maximum_fusion.1), kind=kOutput, calls=%fused_computation.15 | convolution fusion | flops 8160804864 | bytes 17413632 | tf_op jit(solution)/shard_map/ird,de->ire/dot_general | solution.py:360
  245.2 36.7 %shard_map.381 = (bf16[1024,1152]{1,0:T(8,128)(2,1)}, f32[16,1024]{1,0:T(8,128)}) custom-call(bf16[1024,3456]{1,0:T(8,128)(2,1)} %add_convert_fusion.query_ref.keyval_ref.both_ref, bf16[1024,3456]{1,0:T(8,128)(2,1)} %add_convert_fusion.query_ref.keyval_ref.both_ref, f32[1024,1]{1,0:T(8,128)} %fusion.34.bias_ref), custom_call_target="tpu_custom_call" | custom-call | tf_op jit(solution)/shard_map/pallas_call | solution.py:119
  292.9 21.1 %fusion.46 = f32[1024,4608]{1,0:T(8,128)} fusion(bf16[1152,4608]{0,1:T(8,128)(2,1)} %all-gather.15.cloned.1.call-done, f32[1024,1152]{1,0:T(8,128)} %copy-done.3, f32[1152]{0:T(1024)S(1)} %get-tuple-element.245, f32[1152]{0:T(1024)S(1)} %get-tuple-element.246, f32[1024]{0:T(1024)S(1)} %add_rsqrt_fusion, f32[1024]{0:T(1024)S(1)} %broadcast_multiply_fusion.5), kind=kOutput, calls=%fused_computation.152 | convolution fusion | flops 10877534208 | bytes 34227200 | tf_op jit(solution)/shard_map/ird,df->irf/dot_general | solution.py:388
  314.1 22.5 %convolution_convert_fusion.1 = bf16[4608,1152]{1,0:T(8,128)(2,1)} fusion(bf16[1024,1152]{1,0:T(8,128)(2,1)S(1)} %copy-done.9, f32[1024,4608]{1,0:T(8,128)} %fusion.46, f32[4608]{0:T(1024)S(1)} %add.291), kind=kOutput, calls=%fused_computation.3 | convolution fusion | flops 10924130304 | bytes 31868928 | tf_op jit(solution)/shard_map/irf,ird->fd/dot_general | solution.py:400
  336.6 28.0 %convert_reduce_fusion = (f32[4608]{0:T(1024)}, bf16[1024,4608]{1,0:T(8,128)(2,1)S(1)}) fusion(f32[1024,4608]{1,0:T(8,128)} %fusion.46, f32[4608]{0:T(1024)S(1)} %add.291, bf16[4608,1152]{0,1:T(8,128)(2,1)} %all-gather.19.cloned.1.call-done, bf16[1,1024,1152]{2,1,0:T(8,128)(2,1)S(1)} %copy-done.7), kind=kOutput, calls=%fused_computation.11 | convolution fusion | flops 10980159488 | bytes 41324544 | tf_op jit(solution)/shard_map/ird,fd->irf/dot_general | solution.py:404
  364.6 17.1 %convolution_convert_fusion = bf16[1152,4608]{1,0:T(8,128)(2,1)} fusion(bf16[1024,4608]{1,0:T(8,128)(2,1)S(1)} %get-tuple-element.288, f32[1024,1152]{1,0:T(8,128)} %copy-done.3, f32[1152]{0:T(1024)S(1)} %get-tuple-element.245, f32[1152]{0:T(1024)S(1)} %get-tuple-element.246, f32[1024]{0:T(1024)S(1)} %add_rsqrt_fusion, f32[1024]{0:T(1024)S(1)} %broadcast_multiply_fusion.5), kind=kOutput, calls=%fused_computation.2 | convolution fusion | flops 10882842624 | bytes 24790016 | tf_op jit(solution)/shard_map/ird,irf->df/dot_general | solution.py:411
  381.7 19.8 %multiply_reduce_fusion.1 = (f32[1152]{0:T(1024)S(1)}, f32[1024]{0:T(1024)S(1)}, f32[1024]{0:T(1024)S(1)}, f32[1152]{0:T(1024)S(1)}, f32[1024,1152]{1,0:T(8,128)}) fusion(f32[1024,1152]{1,0:T(8,128)} %copy-done.3, f32[1024]{0:T(1024)S(1)} %add_rsqrt_fusion, f32[1024]{0:T(1024)S(1)} %broadcast_multiply_fusion.5, f32[1152]{0:T(1024)S(1)} %get-tuple-element.246, ...), kind=kOutput, calls=%fused_computation.35 | convolution fusion | flops 10882248704 | bytes 29521408 | tf_op jit(solution)/shard_map/irf,df->ird/dot_general | solution.py:415
  401.5 24.2 %multiply_reduce_fusion = (f32[1152]{0:T(1024)S(1)}, bf16[1024,1152]{1,0:T(8,128)(2,1)}, f32[1152]{0:T(1024)S(1)}, bf16[1024,1152]{1,0:T(8,128)(2,1)}, f32[1024,1152]{1,0:T(8,128)}) fusion(bf16[4,256,1152]{2,1,0:T(8,128)(2,1)} %all-to-all-done.3, f32[1024]{0:T(1024)S(1)} %copy-done.37, f32[1024,1152]{1,0:T(8,128)} %copy-done.3, f32[1152]{0:T(1024)S(1)} %copy-done.29, ...), kind=kOutput, calls=%fused_computation.34 | convolution fusion | flops 10942412800 | bytes 50791424 | tf_op jit(solution)/shard_map/irf,fd->ird/dot_general | solution.py:394
  442.3 57.0 %shard_map.382 = bf16[1024,3456]{1,0:T(8,128)(2,1)} custom-call(bf16[1024,3456]{1,0:T(8,128)(2,1)} %add_convert_fusion.query_ref.keyval_ref.both_ref, f32[1024,1]{1,0:T(8,128)} %fusion.34.bias_ref, bf16[1024,1152]{1,0:T(8,128)(2,1)} %get-tuple-element.28.mixed_ref, bf16[1024,1152]{1,0:T(8,128)(2,1)} %convolution_convert_fusion.4.grad_ref, ...), custom_call_target="tpu_custom_call" | custom-call | tf_op jit(solution)/shard_map/pallas_call | solution.py:211
  499.3 13.7 %convolution_convert_fusion.2 = bf16[1152,3456]{1,0:T(8,128)(2,1)} fusion(bf16[1024,1152]{1,0:T(8,128)(2,1)S(1)} %copy-done.8, bf16[1024,3456]{1,0:T(8,128)(2,1)} %shard_map.382), kind=kOutput, calls=%fused_computation.13 | convolution fusion | flops 8157708288 | bytes 17399808 | tf_op jit(solution)/shard_map/ird,ire->de/dot_general | solution.py:451
  524.6 15.1 %copy.210 = bf16[1152,4608]{0,1:T(8,128)(2,1)} copy(bf16[1152,4608]{1,0:T(8,128)(2,1)} %convolution_convert_fusion) | data formatting | bytes 21233664
  539.8 15.5 %copy.212 = bf16[4608,1152]{0,1:T(8,128)(2,1)} copy(bf16[4608,1152]{1,0:T(8,128)(2,1)} %convolution_convert_fusion.1) | data formatting | bytes 21233664
  556.9 16.3 %multiply_reduce_fusion.3 = (f32[1152]{0:T(1024)S(1)}, f32[1024]{0:T(1024)S(1)}, f32[1024]{0:T(1024)S(1)}, f32[1152]{0:T(1024)S(1)}, f32[1024,1152]{1,0:T(8,128)}) fusion(bf16[4,256,1152]{2,1,0:T(8,128)(2,1)S(1)} %copy-done.1, f32[1024]{0:T(1024)S(1)} %copy-done.35, f32[1024]{0:T(1024)S(1)} %bitcast.142, f32[1152]{0:T(1024)S(1)} %copy-done.27, ...), kind=kOutput, calls=%fused_computation.37 | convolution fusion | flops 8165519360 | bytes 22148608 | tf_op jit(solution)/shard_map/ire,de->ird/dot_general | solution.py:455
  609.6 70.7 %reduce-scatter.29.cloned.1.call-done = bf16[576,1152]{1,0:T(8,128)(2,1)} async-done(((bf16[4608,1152]{1,0:T(8,128)(2,1)}), bf16[576,1152]{1,0:T(8,128)(2,1)}) %reduce-scatter.29.cloned.1.call-update) | async-done | bytes 1327120
  687.7 78.2 %reduce-scatter.31.cloned.1.call-done = bf16[144,4608]{1,0:T(8,128)(2,1)} async-done(((bf16[1152,4608]{1,0:T(8,128)(2,1)}), bf16[144,4608]{1,0:T(8,128)(2,1)}) %reduce-scatter.31.cloned.1.call-update) | async-done | bytes 1327120
  777.5 13.3 %reduce-scatter.21.cloned.1.call-done = bf16[288,144]{1,0:T(8,128)(2,1)} async-done(((bf16[1152,144]{1,0:T(8,128)(2,1)}), bf16[288,144]{1,0:T(8,128)(2,1)}) %reduce-scatter.21.cloned.1.call-update) | async-done | bytes 82960 | tf_op jit(solution)/shard_map/reduce_scatter | solution.py:298
  792.5 28.0 %reduce-scatter.19.cloned.1.call-done = bf16[288,432]{1,0:T(8,128)(2,1)} async-done(((bf16[1152,432]{1,0:T(8,128)(2,1)}), bf16[288,432]{1,0:T(8,128)(2,1)}) %reduce-scatter.19.cloned.1.call-update) | async-done | bytes 248848 | tf_op jit(solution)/shard_map/reduce_scatter | solution.py:298
  823.5 32.4 %reduce-scatter.23.cloned.1.call-done = bf16[288,576]{1,0:T(8,128)(2,1)} async-done(((bf16[1152,576]{1,0:T(8,128)(2,1)}), bf16[288,576]{1,0:T(8,128)(2,1)}) %reduce-scatter.23.cloned.1.call-update) | async-done | bytes 331792 | tf_op jit(solution)/shard_map/reduce_scatter | solution.py:298
  858.4 47.4 %reduce-scatter.33.cloned.1.call-done = bf16[1152,144]{1,0:T(8,128)(2,1)} async-done(((bf16[4608,144]{1,0:T(8,128)(2,1)}), bf16[1152,144]{1,0:T(8,128)(2,1)}) %reduce-scatter.33.cloned.1.call-update) | async-done | bytes 331792
  (273 shorter events, 183.4 us)
Async XLA Ops:
  7.2 66.4 %all-gather.13.cloned.1.call-start = ((), (), s32[]{:S(2)}) async-start(), calls=%async_computation.17 | async-start | bytes 1843200 | tf_op jit(solution)/shard_map/all_gather | solution.py:293
  9.2 95.6 %all-gather.17.cloned.1.call-start = ((), (), s32[]{:S(2)}) async-start(), calls=%async_computation.19 | async-start | bytes 1658880 | tf_op jit(solution)/shard_map/all_gather | solution.py:293
  11.1 218.5 %all-gather.9.cloned.1.call-start = ((), (), s32[]{:S(2)}) async-start(), calls=%async_computation.15 | async-start | bytes 8957952 | tf_op jit(solution)/shard_map/all_gather | solution.py:294
  55.3 226.6 %all-gather.11.cloned.1.call-start = ((), (), s32[]{:S(2)}) async-start(), calls=%async_computation.16 | async-start | bytes 2985984 | tf_op jit(solution)/shard_map/all_gather | solution.py:294
  73.5 219.4 %all-gather.15.cloned.1.call-start = ((), (), s32[]{:S(2)}) async-start(), calls=%async_computation.18 | async-start | bytes 11943936 | tf_op jit(solution)/shard_map/all_gather | solution.py:294
  101.0 58.1 %all-to-all-start = ((bf16[4,256,1152]{2,1,0:T(8,128)(2,1)}), bf16[4,256,1152]{2,1,0:T(8,128)(2,1)S(1)}, u32[]{:S(2)}, u32[]{:S(2)}) async-start(bf16[4,256,1152]{2,1,0:T(8,128)(2,1)} %param.22), calls=%async_computation | async-start | bytes 4718592 | tf_op jit(solution)/shard_map/all_to_all | solution.py:275
  104.8 231.8 %all-gather.19.cloned.1.call-start = ((), (), s32[]{:S(2)}) async-start(), calls=%async_computation.20 | async-start | bytes 11943936 | tf_op jit(solution)/shard_map/all_gather | solution.py:294
  159.1 122.7 %copy-start = (bf16[4,256,1152]{2,1,0:T(8,128)(2,1)}, bf16[4,256,1152]{2,1,0:T(8,128)(2,1)S(1)}, u32[]{:S(2)}) copy-start(bf16[4,256,1152]{2,1,0:T(8,128)(2,1)S(1)} %all-to-all-done) | copy-start | bytes 7077892
  159.2 58.1 %all-to-all-start.3 = ((bf16[4,256,1152]{2,1,0:T(8,128)(2,1)}), bf16[4,256,1152]{2,1,0:T(8,128)(2,1)}, u32[]{:S(2)}, u32[]{:S(2)}) async-start(bf16[4,256,1152]{2,1,0:T(8,128)(2,1)} %param.25), calls=%async_computation.3 | async-start | bytes 4718592 | tf_op jit(solution)/shard_map/all_to_all | solution.py:275
  163.7 422.2 %reduce-scatter.27.cloned.1.call-start = ((), (), s32[]{:S(2)}) async-start(), calls=%async_computation.25 | async-start | bytes 2985984
  168.6 113.3 %copy-start.43 = (f32[1152]{0:T(1024)}, f32[1152]{0:T(1024)S(1)}, u32[]{:S(2)}) copy-start(f32[1152]{0:T(1024)S(1)} %get-tuple-element.249) | copy-start | bytes 13828
  434.7 159.9 %reduce-scatter.25.cloned.1.call-start = ((), (), s32[]{:S(2)}) async-start(), calls=%async_computation.24 | async-start | bytes 8957952
  524.5 155.8 %reduce-scatter.29.cloned.1.call-start = ((), (), s32[]{:S(2)}) async-start(), calls=%async_computation.26 | async-start | bytes 11943936
  539.8 226.1 %reduce-scatter.31.cloned.1.call-start = ((), (), s32[]{:S(2)}) async-start(), calls=%async_computation.27 | async-start | bytes 11943936
  555.3 235.5 %reduce-scatter.21.cloned.1.call-start = ((), (), s32[]{:S(2)}) async-start(), calls=%async_computation.22 | async-start | bytes 737280 | tf_op jit(solution)/shard_map/reduce_scatter | solution.py:298
  589.3 16.4 %all-to-all-start.5 = ((f32[32,1,2880]{2,1,0:T(1,128)}), f32[32,1,2880]{2,1,0:T(1,128)S(1)}, u32[]{:S(2)}, u32[]{:S(2)}) async-start(f32[32,1,2880]{2,1,0:T(1,128)} %all_to_all.46), calls=%async_computation.5 | async-start | bytes 753664 | tf_op jit(solution)/shard_map/all_to_all | solution.py:500
  594.2 226.4 %reduce-scatter.19.cloned.1.call-start = ((), (), s32[]{:S(2)}) async-start(), calls=%async_computation.21 | async-start | bytes 1474560 | tf_op jit(solution)/shard_map/reduce_scatter | solution.py:298
  605.7 77.2 %all-to-all-start.4 = ((bf16[4,1,256,1152]{3,2,1,0:T(8,128)(2,1)}), bf16[4,1,256,1152]{3,2,1,0:T(8,128)(2,1)S(1)}, u32[]{:S(2)}, u32[]{:S(2)}) async-start(bf16[4,1,256,1152]{3,2,1,0:T(8,128)(2,1)} %bitcast.20), calls=%async_computation.4 | async-start | bytes 4718592 | tf_op jit(solution)/shard_map/all_to_all | solution.py:279
  609.5 246.4 %reduce-scatter.23.cloned.1.call-start = ((), (), s32[]{:S(2)}) async-start(), calls=%async_computation.23 | async-start | bytes 1843200 | tf_op jit(solution)/shard_map/reduce_scatter | solution.py:298
  682.9 87.6 %copy-start.24 = (f32[288,144]{0,1:T(8,128)S(1)}, f32[288,144]{0,1:T(8,128)}, u32[]{:S(2)}) copy-start(f32[288,144]{0,1:T(8,128)} %param.34) | copy-start | bytes 497668
  682.9 227.2 %all-to-all-start.2 = ((bf16[4,1,256,1152]{3,2,1,0:T(8,128)(2,1)}), bf16[4,1,256,1152]{3,2,1,0:T(8,128)(2,1)}, u32[]{:S(2)}, u32[]{:S(2)}) async-start(bf16[4,1,256,1152]{3,2,1,0:T(8,128)(2,1)} %bitcast.126), calls=%async_computation.2 | async-start | bytes 4718592 | tf_op jit(solution)/shard_map/all_to_all | solution.py:279
  687.7 218.1 %reduce-scatter.33.cloned.1.call-start = ((), (), s32[]{:S(2)}) async-start(), calls=%async_computation.28 | async-start | bytes 2949120
  790.8 134.2 %copy-start.20 = (bf16[288,144]{1,0:T(8,128)(2,1)S(1)}, bf16[288,144]{1,0:T(8,128)(2,1)}, u32[]{:S(2)}) copy-start(bf16[288,144]{1,0:T(8,128)(2,1)} %reduce-scatter.21.cloned.1.call-done) | copy-start | bytes 248836
  910.8 11.5 %all-to-all-start.6 = ((f32[32,1,128]{2,1,0:T(1,128)}), f32[32,1,128]{2,1,0:T(1,128)}, u32[]{:S(2)}, u32[]{:S(2)}) async-start(f32[32,1,128]{2,1,0:T(1,128)} %broadcast_in_dim.18), calls=%async_computation.9 | async-start | bytes 32768 | tf_op jit(solution)/shard_map/all_to_all | solution.py:289
  (43 other events, 900.5 us)
Sparse Core Ops, SparseCore 0:
  10.2 53.8 all-gather.12
  66.2 34.7 all-gather.16
  103.5 51.4 all-gather.8
  157.3 30.2 all-gather.10
  189.3 63.8 all-gather.14
  254.9 63.8 all-gather.18
  434.8 43.4 reduce-scatter.26
  524.7 69.8 reduce-scatter.24
  598.1 82.1 reduce-scatter.28
  683.7 82.2 reduce-scatter.30
  768.8 22.0 reduce-scatter.20
  793.0 27.4 reduce-scatter.18
  823.4 32.4 reduce-scatter.22
  858.8 46.9 reduce-scatter.32

commit v3 on v2

--- a/solution.py
+++ b/solution.py
@@ -225,6 +225,227 @@
         scratch_shapes=scratch,
         compiler_params=params,
     )(query, keyval, key_bias, mixed, grad, log_total)
+
+
+MESH = pl.DeviceIdType.MESH
+
+
+def flip(index, bit):
+    return index + bit - 2 * bit * lax.rem(lax.div(index, bit), 2)
+
+
+def start_kernel(
+    wide_ref, tall_ref, tokens_ref,
+    qkv_ref, out_ref, up_ref, down_ref, rows_ref,
+    held, turned, line_send, line_recv, row_send, row_recv, flat_send, flat_recv, local_sem,
+    *, bands, qkv_part, out_part,
+):
+    img, band = lax.axis_index("img"), lax.axis_index("band")
+    depth, width = wide_ref.shape
+    tall_rows, tall_width = tall_ref.shape
+    row_block = tokens_ref.shape[1]
+    lanes = 128
+    first = -(-(qkv_part + out_part) // lanes) * lanes
+    beside_x, beside_y, sibling = flip(img, 2), flip(img, 4), flip(img, 1)
+    across = flip(beside_x, 4)
+
+    barrier = pltpu.get_barrier_semaphore()
+    for other in (beside_x, beside_y, sibling):
+        pl.semaphore_signal(barrier, inc=1, device_id={"img": other}, device_id_type=MESH)
+    for step in range(1, bands):
+        pl.semaphore_signal(
+            barrier, inc=1, device_id={"band": lax.rem(band + step, bands)}, device_id_type=MESH
+        )
+    pl.semaphore_wait(barrier, 3 + bands - 1)
+
+    def piece(part, owner):
+        if part == 2:
+            return down_ref.at[:, pl.ds(pl.multiple_of(owner * tall_width, lanes), tall_width)]
+        span = pl.ds(0, first) if part == 0 else pl.ds(first, width - first)
+        return held.at[pl.ds(pl.multiple_of(owner * depth, 16), depth), span]
+
+    def line_copy(part, way, step, owner, toward):
+        view = piece(part, owner)
+        return pltpu.make_async_remote_copy(
+            src_ref=view, dst_ref=view,
+            send_sem=line_send.at[part, way, step], recv_sem=line_recv.at[part, way, step],
+            device_id={"band": toward}, device_id_type=MESH,
+        )
+
+    def line_sends(part, step, act):
+        for way, sign in ((0, 1), (1, -1)):
+            owner, toward = band - sign * step, band + sign
+
+            @pl.when((owner >= 0) & (owner < bands) & (toward >= 0) & (toward < bands))
+            def _():
+                act(line_copy(part, way, step, owner, toward))
+
+    def line_arrivals(part, step):
+        for way, sign in ((0, 1), (1, -1)):
+            owner = band - sign * (step + 1)
+
+            @pl.when((owner >= 0) & (owner < bands))
+            def _():
+                line_copy(part, way, step, owner, band - sign).wait_recv()
+
+    def row_copy(step):
+        target = lax.rem(band + step, bands)
+        return pltpu.make_async_remote_copy(
+            src_ref=tokens_ref.at[target],
+            dst_ref=rows_ref.at[pl.ds(pl.multiple_of(band * row_block, 16), row_block), :],
+            send_sem=row_send.at[step - 1], recv_sem=row_recv.at[step - 1],
+            device_id={"band": target}, device_id_type=MESH,
+        )
+
+    def row_arrival(step):
+        source = lax.rem(band + bands - step, bands)
+        view = rows_ref.at[pl.ds(pl.multiple_of(source * row_block, 16), row_block), :]
+        return pltpu.make_async_remote_copy(
+            src_ref=view, dst_ref=view,
+            send_sem=row_send.at[step - 1], recv_sem=row_recv.at[step - 1],
+            device_id={"band": source}, device_id_type=MESH,
+        )
+
+    def qkv_rows(owner, start=0, count=qkv_part):
+        return qkv_ref.at[pl.ds(pl.multiple_of(owner * qkv_part + start, 16), count), :]
+
+    def out_rows(owner):
+        return out_ref.at[pl.ds(pl.multiple_of(owner * out_part, 16), out_part), :]
+
+    half = (qkv_part + out_part) // 2
+    own_qkv, own_out = turned.at[pl.ds(0, qkv_part), :], turned.at[pl.ds(qkv_part, out_part), :]
+    plan = [
+        (own_qkv, qkv_rows(img), beside_x, qkv_rows(beside_x)),
+        (own_out, out_rows(img), beside_x, out_rows(beside_x)),
+        (own_qkv, qkv_rows(img), beside_y, qkv_rows(beside_y)),
+        (own_out, out_rows(img), beside_y, out_rows(beside_y)),
+        (own_qkv, qkv_rows(img), sibling, qkv_rows(sibling)),
+        (own_out, out_rows(img), sibling, out_rows(sibling)),
+    ]
+    for owner, toward, whole in ((beside_x, beside_y, True), (beside_y, beside_x, False)):
+        if whole:
+            view = qkv_rows(owner, 0, half)
+            plan.append((view, view, toward, qkv_rows(across, 0, half)))
+        else:
+            rest = qkv_part - half
+            view = qkv_rows(owner, half, rest)
+            plan.append((view, view, toward, qkv_rows(across, half, rest)))
+            plan.append((out_rows(owner), out_rows(owner), toward, out_rows(across)))
+    for owner in (beside_x, beside_y):
+        plan.append((qkv_rows(owner), qkv_rows(owner), sibling, qkv_rows(flip(owner, 1))))
+        plan.append((out_rows(owner), out_rows(owner), sibling, out_rows(flip(owner, 1))))
+    far = flip(across, 1)
+    plan.append((qkv_rows(across, 0, half), qkv_rows(across, 0, half), sibling, qkv_rows(far, 0, half)))
+    rest = qkv_part - half
+    plan.append((qkv_rows(across, half, rest), qkv_rows(across, half, rest), sibling, qkv_rows(far, half, rest)))
+    plan.append((out_rows(across), out_rows(across), sibling, out_rows(far)))
+
+    def flat_copy(at):
+        source, target, toward, _ = plan[at]
+        return pltpu.make_async_remote_copy(
+            src_ref=source, dst_ref=target, send_sem=flat_send.at[at], recv_sem=flat_recv.at[at],
+            device_id={"img": toward}, device_id_type=MESH,
+        )
+
+    def flat_arrival(at):
+        landing = plan[at][3]
+        pltpu.make_async_remote_copy(
+            src_ref=landing, dst_ref=landing, send_sem=flat_send.at[at], recv_sem=flat_recv.at[at],
+            device_id={"img": sibling}, device_id_type=MESH,
+        ).wait_recv()
+
+    def turn(tile):
+        span = pl.ds(pl.multiple_of(tile * lanes, lanes), lanes)
+        turned[span, :] = held[:, span].astype(jnp.float32).T.astype(jnp.bfloat16)
+
+    start = lambda copy: copy.start()
+    own_rows = pltpu.make_async_copy(
+        tokens_ref.at[band],
+        rows_ref.at[pl.ds(pl.multiple_of(band * row_block, 16), row_block), :],
+        local_sem.at[0],
+    )
+    own_rows.start()
+    held[pl.ds(pl.multiple_of(band * depth, 16), depth), :] = wide_ref[...]
+    down_ref[:, pl.ds(pl.multiple_of(band * tall_width, lanes), tall_width)] = tall_ref[...]
+    line_sends(0, 0, start)
+    for step in range(bands - 1):
+        line_arrivals(0, step)
+        if step < bands - 2:
+            line_sends(0, step + 1, start)
+    line_sends(1, 0, start)
+    line_sends(2, 0, start)
+    for step in range(1, bands):
+        row_copy(step).start()
+    pl.loop(0, first // lanes)(turn)
+    keep_qkv = pltpu.make_async_copy(own_qkv, qkv_rows(img), local_sem.at[1])
+    keep_out = pltpu.make_async_copy(own_out, out_rows(img), local_sem.at[2])
+    for at in range(6):
+        flat_copy(at).start()
+    keep_qkv.start()
+    keep_out.start()
+    for step in range(bands - 2):
+        for part in (1, 2):
+            line_arrivals(part, step)
+            line_sends(part, step + 1, start)
+    for arrived, sent in (((0, 1), (6, 9, 10)), ((2, 3), (7, 8, 11, 12))):
+        for at in arrived:
+            flat_arrival(at)
+        for at in sent:
+            flat_copy(at).start()
+    for at in (6, 7, 8):
+        flat_arrival(at)
+        flat_copy(at + 7).start()
+    for part in (1, 2):
+        line_arrivals(part, bands - 2)
+    pl.loop(first // lanes, width // lanes)(turn)
+    up_ref[...] = turned[pl.ds(qkv_part + out_part, width - qkv_part - out_part), :]
+    for part in range(3):
+        for step in range(bands - 1):
+            line_sends(part, step, lambda copy: copy.wait_send())
+    for at in (4, 5, 9, 10, 11, 12, 13, 14, 15):
+        flat_arrival(at)
+    for at in range(16):
+        flat_copy(at).wait_send()
+    for step in range(1, bands):
+        row_copy(step).wait_send()
+        row_arrival(step).wait_recv()
+    own_rows.wait()
+    keep_qkv.wait()
+    keep_out.wait()
+
+
+def start_exchange(wide, tall, tokens, bands, imgs, qkv_part, out_part):
+    depth, width = wide.shape
+    up_part = width - qkv_part - out_part
+    low = jnp.bfloat16
+    anywhere, vmem = pl.BlockSpec(memory_space=pl.ANY), pl.BlockSpec(memory_space=pltpu.VMEM)
+    features = depth * bands
+    return pl.pallas_call(
+        functools.partial(start_kernel, bands=bands, qkv_part=qkv_part, out_part=out_part),
+        out_shape=(
+            jax.ShapeDtypeStruct((qkv_part * imgs, features), low),
+            jax.ShapeDtypeStruct((out_part * imgs, features), low),
+            jax.ShapeDtypeStruct((up_part, features), low),
+            jax.ShapeDtypeStruct((tall.shape[0], tall.shape[1] * bands), low),
+            jax.ShapeDtypeStruct((tokens.shape[1] * bands, tokens.shape[2]), low),
+        ),
+        in_specs=[vmem, vmem, anywhere],
+        out_specs=(anywhere, anywhere, vmem, vmem, anywhere),
+        scratch_shapes=[
+            pltpu.VMEM((features, width), low),
+            pltpu.VMEM((width, features), low),
+            pltpu.SemaphoreType.DMA((3, 2, bands - 1)),
+            pltpu.SemaphoreType.DMA((3, 2, bands - 1)),
+            pltpu.SemaphoreType.DMA((bands - 1,)),
+            pltpu.SemaphoreType.DMA((bands - 1,)),
+            pltpu.SemaphoreType.DMA((16,)),
+            pltpu.SemaphoreType.DMA((16,)),
+            pltpu.SemaphoreType.DMA((3,)),
+        ],
+        compiler_params=pltpu.CompilerParams(
+            collective_id=0, has_side_effects=True, vmem_limit_bytes=40 * 2**20
+        ),
+    )(wide, tall, tokens)
 
 
 def body(
@@ -289,13 +510,7 @@
         got = lax.all_to_all(sent, ("img", "band"), split_axis=0, concat_axis=0, tiled=True)
         return jnp.sum(got[:, 0])
 
-    def gather_weight(weight):
-        rows = lax.all_gather(weight.astype(low_type), "band", axis=0, tiled=True)
-        return lax.all_gather(rows, "img", axis=1, tiled=True)
-
-    def scatter_grad(grad):
-        columns = lax.psum_scatter(grad, "img", scatter_dimension=1, tiled=True)
-        return lax.psum_scatter(columns, "band", scatter_dimension=0, tiled=True).astype(jnp.float32)
+    qkv_part, out_part = qkv_weight.shape[1], out_weight.shape[1]
 
     bias_rows, bias_columns = biases.shape
     small = lax.all_gather(
@@ -312,11 +527,24 @@
         .transpose(1, 0, 2)
         .reshape(bias_rows, features)
     )
-    tokens_low = to_images(inputs)
-    qkv_full = gather_weight(qkv_weight)
-    out_full = gather_weight(out_weight)
-    up_full = gather_weight(up_weight)
-    down_full = gather_weight(down_weight)
+    wide = jnp.concatenate([qkv_weight, out_weight, up_weight], axis=1).astype(low_type)
+    tall = down_weight.T.astype(low_type)
+    if img_count == 8 and own == 1 and split == 1:
+        qkv_full, out_full, up_rows, down_rows, tokens_low = start_exchange(
+            wide, tall, inputs, band_count, img_count, qkv_part, out_part
+        )
+        tokens_low = tokens_low.reshape(own, image_rows, features)
+    else:
+        turned = lax.all_gather(wide, "band", axis=0, tiled=True).T
+        qkv_full = lax.all_gather(turned[:qkv_part], "img", axis=0, tiled=True)
+        out_full = lax.all_gather(
+            turned[qkv_part : qkv_part + out_part], "img", axis=0, tiled=True
+        )
+        up_rows = turned[qkv_part + out_part :]
+        down_rows = lax.all_gather(tall, "band", axis=1, tiled=True)
+        tokens_low = to_images(inputs)
+    up_full = lax.all_gather(up_rows, "img", axis=0, tiled=True)
+    down_full = lax.all_gather(after(down_rows, up_rows), "img", axis=0, tiled=True)
 
     silu_all = jax.nn.silu(condition_all.astype(jnp.float32)).astype(low_type)
     ada_rows = ada_weight.shape[0]
@@ -357,7 +585,7 @@
     grad_out = cotangent_low.astype(jnp.float32) * row_mask
     qkv_bias = jnp.concatenate([bias_vals[6], jnp.zeros((features,), jnp.float32), bias_vals[7]])
     projected = (
-        jnp.einsum("ird,de->ire", first_in, qkv_full, preferred_element_type=jnp.float32) + qkv_bias
+        jnp.einsum("ird,ed->ire", first_in, qkv_full, preferred_element_type=jnp.float32) + qkv_bias
     ).astype(jnp.bfloat16)
     key_bias = jnp.where(key_mask, 0.0, very_low).astype(jnp.float32)[:, :, None]
     queries = [projected[i] for i in range(own)]
@@ -379,40 +607,40 @@
     mixed_parts = mixed
     mixed = jnp.stack(mixed)
     attended = (
-        jnp.einsum("ird,de->ire", mixed, out_full, preferred_element_type=jnp.float32)
+        jnp.einsum("ird,ed->ire", mixed, out_full, preferred_element_type=jnp.float32)
         + bias_vals[8]
     )
     middle = tokens_in + gate_one * attended
     normed_two, inverse_two = normalize_keep(middle)
     second_in = (normed_two * (1.0 + scale_two) + shift_two).astype(jnp.bfloat16)
     hidden_pre = jnp.einsum(
-        "ird,df->irf", second_in, up_full, preferred_element_type=jnp.float32
+        "ird,fd->irf", second_in, up_full, preferred_element_type=jnp.float32
     ) + bias_vals[9:13].reshape(-1)
     hidden, gelu_back = jax.vjp(smooth_gate, hidden_pre)
     hidden_low = hidden.astype(jnp.bfloat16)
     branch = (
-        jnp.einsum("irf,fd->ird", hidden_low, down_full, preferred_element_type=jnp.float32)
+        jnp.einsum("irf,df->ird", hidden_low, down_full, preferred_element_type=jnp.float32)
         + bias_vals[13]
     )
     output = to_bands((middle + gate_two * branch).astype(jnp.bfloat16))
     branch_grad = (gate_two * grad_out).astype(jnp.bfloat16)
     gate_two_grad = jnp.sum(grad_out * branch, axis=1)
     down_grad = jnp.einsum(
-        "irf,ird->fd", hidden_low, branch_grad, preferred_element_type=jnp.float32
+        "ird,irf->df", branch_grad, hidden_low, preferred_element_type=jnp.float32
     ).astype(low_type)
-    down_shard = scatter_grad(down_grad)
+    down_sum = lax.psum_scatter(down_grad, "img", scatter_dimension=0, tiled=True)
     hidden_grad = jnp.einsum(
-        "ird,fd->irf",
+        "ird,df->irf",
         after(branch_grad, down_grad),
         down_full,
         preferred_element_type=jnp.float32,
     )
     pre_grad = gelu_back(hidden_grad)[0].astype(jnp.bfloat16)
     up_grad = jnp.einsum(
-        "ird,irf->df", second_in, pre_grad, preferred_element_type=jnp.float32
+        "irf,ird->fd", pre_grad, second_in, preferred_element_type=jnp.float32
     ).astype(low_type)
-    up_shard = scatter_grad(up_grad)
-    second_grad = jnp.einsum("irf,df->ird", after(pre_grad, up_grad), up_full, preferred_element_type=jnp.float32)
+    up_sum = lax.psum_scatter(up_grad, "img", scatter_dimension=0, tiled=True)
+    second_grad = jnp.einsum("irf,fd->ird", after(pre_grad, up_grad), up_full, preferred_element_type=jnp.float32)
     shift_two_grad = jnp.sum(second_grad, axis=1)
     scale_two_grad = jnp.sum(second_grad * normed_two, axis=1)
     middle_grad = grad_out + normalize_back(
@@ -421,11 +649,11 @@
     attended_grad = (gate_one * middle_grad).astype(jnp.bfloat16)
     gate_one_grad = jnp.sum(middle_grad * attended, axis=1)
     out_grad = jnp.einsum(
-        "ird,ire->de", mixed, attended_grad, preferred_element_type=jnp.float32
+        "ire,ird->ed", attended_grad, mixed, preferred_element_type=jnp.float32
     ).astype(low_type)
-    out_shard = scatter_grad(out_grad)
+    out_sum = lax.psum_scatter(out_grad, "img", scatter_dimension=0, tiled=True)
     mixed_grad = jnp.einsum(
-        "ire,de->ird", after(attended_grad, out_grad), out_full, preferred_element_type=jnp.float32
+        "ire,ed->ird", after(attended_grad, out_grad), out_full, preferred_element_type=jnp.float32
     ).astype(jnp.bfloat16)
     attention_grads = [
         attention_backward(
@@ -449,10 +677,10 @@
         qkv_grad = jnp.stack(attention_grads)
     qkv_sums = jnp.sum(qkv_grad.astype(jnp.float32), axis=(0, 1))
     qkv_weight_grad = jnp.einsum(
-        "ird,ire->de", first_in, qkv_grad, preferred_element_type=jnp.float32
+        "ire,ird->ed", qkv_grad, first_in, preferred_element_type=jnp.float32
     ).astype(low_type)
-    qkv_shard = scatter_grad(qkv_weight_grad)
-    first_grad = jnp.einsum("ire,de->ird", after(qkv_grad, qkv_weight_grad), qkv_full, preferred_element_type=jnp.float32)
+    qkv_sum = lax.psum_scatter(qkv_weight_grad, "img", scatter_dimension=0, tiled=True)
+    first_grad = jnp.einsum("ire,ed->ird", after(qkv_grad, qkv_weight_grad), qkv_full, preferred_element_type=jnp.float32)
     shift_one_grad = jnp.sum(first_grad, axis=1)
     scale_one_grad = jnp.sum(first_grad * normed_one, axis=1)
     input_grad = to_bands(
@@ -509,6 +737,18 @@
         precision=lax.Precision.HIGHEST,
     )
     bias_total = jnp.sum(got[:, own * ada_columns :], axis=0).reshape(bias_rows, bias_columns)
+    down_shard = lax.psum_scatter(down_sum, "band", scatter_dimension=1, tiled=True).T.astype(
+        jnp.float32
+    )
+    wide_shard = lax.psum_scatter(
+        jnp.concatenate([qkv_sum, out_sum, up_sum], axis=0).T,
+        "band",
+        scatter_dimension=0,
+        tiled=True,
+    ).astype(jnp.float32)
+    qkv_shard = wide_shard[:, :qkv_part]
+    out_shard = wide_shard[:, qkv_part : qkv_part + out_part]
+    up_shard = wide_shard[:, qkv_part + out_part :]
     shards = (ada_shard, qkv_shard, out_shard, up_shard, down_shard)
     squares = jnp.sum(bias_total * bias_total) / band_count
     for shard_grad in shards:

time: 958 us -> 838 us (0.87)
  waiting for transfers between devices: 384 us -> 238 us
  Pallas kernels: 93.6 us -> 208 us
  blocking collectives: 82.5 us -> 25.2 us
  local copies, waits for them, and re-layouts: 82.4 us -> 51.8 us
    pallas_call x0 -> x1, Pallas kernels: none -> 115 us  [start_exchange(): pl.pallas_call(functools.partial(start_kernel, bands=bands, qkv_part=qkv_...]
    all_to_all x2 -> x1, waiting for transfers between devices: 99.6 us -> 0.01 us  [to_images(): lax.all_to_all(rows, 'band', split_axis=0, concat_axis=1, axis_index_grou...]
    unnamed x19 -> x10, waiting for transfers between devices: 197 us -> 126 us
    all_gather x2 -> x0, blocking collectives: 58.4 us -> none  [gather_weight(): rows = lax.all_gather(weight.astype(low_type), 'band', axis=0, tiled=True)]
    reduce_scatter x3 -> x4, waiting for transfers between devices: 73.8 us -> 106 us  [the longest x1 85.6 us: body(): up_sum = lax.psum_scatter(up_grad, 'img', scatter_dimension=0, tiled=True)]
    unnamed x125 -> x110, local copies, waits for them, and re-layouts: 72.7 us -> 46.4 us
  transfers between devices with their start and end apart: 20 -> 13, of which waited for: 11 -> 6; matrix products, arithmetic and copies ran while one was open for 23% -> 32% of each run, Pallas kernels for 10% -> 11%
where the time goes in v3:
time: 838 us; the launch traced here: 832 us
  waiting for transfers between devices  238 us (28%)
  matrix products  209 us (25%)
  Pallas kernels  208 us (25%)
  local copies, waits for them, and re-layouts  51.8 us (6%)
  other arithmetic  51.6 us (6%)
  starting transfers between devices  27.1 us (3%)
  blocking collectives  25.2 us (3%)
  between operations  21.2 us (3%)
    unnamed x10, waiting for transfers between devices  126 us
    pallas_call x1, Pallas kernels, start_exchange(): pl.pallas_call(functools.partial(start_kernel, bands=bands, qkv_part=qkv_...  115 us
    reduce_scatter x1, waiting for transfers between devices, body(): up_sum = lax.psum_scatter(up_grad, 'img', scatter_dimension=0, tiled=True)  85.6 us
    pallas_call x1, Pallas kernels, attention_backward(): pl.pallas_call(shared_kernel, out_shape=jax.ShapeDtypeStruct((rows, 3 * f...  57.1 us
    unnamed x110, local copies, waits for them, and re-layouts  46.4 us
    pallas_call x1, Pallas kernels, attention_forward(): pl.pallas_call(functools.partial(attention_forward_kernel, features=featu...  36.9 us
    dot_general x1, matrix products, body(): jnp.einsum('ird,df->irf', after(branch_grad, down_grad), down_full, prefe...  29.1 us
    dot_general x1, matrix products, body(): jnp.einsum('irf,df->ird', hidden_low, down_full, preferred_element_type=j...  24.3 us
  transfers between devices with their start and end apart: 13, of which 6 were waited for; matrix products, arithmetic and copies ran while one was open for 32% of the time, Pallas kernels for 11%

profile of v3, /device:TPU:0, one launch (start us, length us, event | category | flops | bytes accessed | tf_op | source)
XLA Modules:
  0.0 832.5 jit_solution(10661358129999878735)
XLA Ops:
  14.0 114.5 %shard_map.381 = (bf16[3456,1152]{1,0:T(8,128)(2,1)}, bf16[1152,1152]{1,0:T(8,128)(2,1)S(1)}, bf16[576,1152]{1,0:T(8,128)(2,1)S(1)}, bf16[144,4608]{1,0:T(8,128)(2,1)S(1)}, bf16[1024,1152]{1,0:T(8,128)(2,1)S(1)}) custom-call(bf16[288,1152]{1,0:T(8,128)(2,1)S(1)} %concatenate.32.wide_ref, bf16[144,1152]{1,0:T(8,128)(2,1)S(1)} %convert_bitcast_fusion.tall_ref, ...), custom_call_target="tpu_custom_call" | custom-call | tf_op jit(solution)/shard_map/pallas_call | solution.py:423
  133.4 9.3 %all-gather = bf16[8,1,6624]{2,1,0:T(2,128)(2,1)S(1)} all-gather(bf16[1,1,6624]{2,1,0:T(2,128)(2,1)S(1)} %maximum_bitcast_fusion.1), channel_id=1, replica_groups=mesh['img'=8,'band'=4] {'img'}, dimensions={0}, use_global_device_ids=true | all-gather | bytes 119232 | tf_op jit(solution)/shard_map/all_gather | solution.py:516
  145.3 7.4 all-to-all-start
  166.7 17.1 %add_convert_fusion.query_ref.keyval_ref.both_ref = bf16[1024,3456]{1,0:T(8,128)(2,1)} fusion(bf16[3456,1152]{1,0:T(8,128)(2,1)} %get-tuple-element.35, f32[3456]{0:T(1024)S(1)} %pad_maximum_fusion.1, bf16[1024,1152]{1,0:T(8,128)(2,1)S(1)} %get-tuple-element.34, f32[1152]{0:T(1024)S(1)} %get-tuple-element.215, f32[1152]{0:T(1024)S(1)} %get-tuple-element.216, ...), kind=kOutput, calls=%fused_computation.15 | convolution fusion | flops 8167882752 | bytes 17431040 | tf_op jit(solution)/shard_map/ird,ed->ire/dot_general | solution.py:588
  183.9 36.9 %shard_map.382 = (bf16[1024,1152]{1,0:T(8,128)(2,1)}, f32[16,1024]{1,0:T(8,128)}) custom-call(bf16[1024,3456]{1,0:T(8,128)(2,1)} %add_convert_fusion.query_ref.keyval_ref.both_ref, bf16[1024,3456]{1,0:T(8,128)(2,1)} %add_convert_fusion.query_ref.keyval_ref.both_ref, f32[1024,1]{1,0:T(8,128)} %fusion.41.bias_ref), custom_call_target="tpu_custom_call" | custom-call | tf_op jit(solution)/shard_map/pallas_call | solution.py:119
  220.8 7.5 fusion.61
  233.4 22.0 %fusion.52 = f32[1024,4608]{1,0:T(8,128)} fusion(bf16[4608,1152]{1,0:T(8,128)(2,1)} %all-gather.4.cloned.1.call-done, f32[1024,1152]{1,0:T(8,128)} %copy-done.8, f32[1152]{0:T(1024)S(1)} %get-tuple-element.213, f32[1152]{0:T(1024)S(1)} %get-tuple-element.214, f32[1024]{0:T(1024)S(1)} %add_rsqrt_fusion, f32[1024]{0:T(1024)S(1)} %broadcast_multiply_fusion.5), kind=kOutput, calls=%fused_computation.155 | convolution fusion | flops 10877534208 | bytes 34227200 | tf_op jit(solution)/shard_map/ird,fd->irf/dot_general | solution.py:616
  255.4 18.1 %convolution_convert_fusion.1 = bf16[1152,4608]{1,0:T(8,128)(2,1)} fusion(bf16[1024,1152]{1,0:T(8,128)(2,1)S(1)} %multiply_convert_fusion.2, f32[1024,4608]{1,0:T(8,128)} %fusion.52, f32[4608]{0:T(1024)S(1)} %add.283), kind=kOutput, calls=%fused_computation.3 | convolution fusion | flops 10924130304 | bytes 31868928 | tf_op jit(solution)/shard_map/ird,irf->df/dot_general | solution.py:628
  276.9 29.1 %convert_reduce_fusion = (f32[4608]{0:T(1024)}, bf16[1024,4608]{1,0:T(8,128)(2,1)S(1)}) fusion(f32[1024,4608]{1,0:T(8,128)} %fusion.52, f32[4608]{0:T(1024)S(1)} %add.283, bf16[1152,4608]{1,0:T(8,128)(2,1)} %all-gather.6.cloned.1.call-done, bf16[1,1024,1152]{2,1,0:T(8,128)(2,1)S(1)} %get-tuple-element.41), kind=kOutput, calls=%fused_computation.11 | convolution fusion | flops 10980159488 | bytes 41324544 | tf_op jit(solution)/shard_map/ird,df->irf/dot_general | solution.py:632
  309.6 18.4 %convolution_convert_fusion = bf16[4608,1152]{1,0:T(8,128)(2,1)} fusion(bf16[1024,4608]{1,0:T(8,128)(2,1)S(1)} %get-tuple-element.256, f32[1024,1152]{1,0:T(8,128)} %copy-done.8, f32[1152]{0:T(1024)S(1)} %get-tuple-element.213, f32[1152]{0:T(1024)S(1)} %get-tuple-element.214, f32[1024]{0:T(1024)S(1)} %add_rsqrt_fusion, f32[1024]{0:T(1024)S(1)} %broadcast_multiply_fusion.5), kind=kOutput, calls=%fused_computation.2 | convolution fusion | flops 10882842624 | bytes 24790016 | tf_op jit(solution)/shard_map/irf,ird->fd/dot_general | solution.py:639
  328.0 21.2 %multiply_reduce_fusion.1 = (f32[1152]{0:T(1024)S(1)}, f32[1024]{0:T(1024)S(1)}, f32[1024]{0:T(1024)S(1)}, f32[1152]{0:T(1024)S(1)}, f32[1024,1152]{1,0:T(8,128)}) fusion(f32[1024,1152]{1,0:T(8,128)} %copy-done.8, f32[1024]{0:T(1024)S(1)} %add_rsqrt_fusion, f32[1024]{0:T(1024)S(1)} %broadcast_multiply_fusion.5, f32[1152]{0:T(1024)S(1)} %get-tuple-element.214, ...), kind=kOutput, calls=%fused_computation.47 | convolution fusion | flops 10882248704 | bytes 29521408 | tf_op jit(solution)/shard_map/irf,fd->ird/dot_general | solution.py:643
  349.2 24.3 %multiply_reduce_fusion = (f32[1152]{0:T(1024)S(1)}, bf16[1024,1152]{1,0:T(8,128)(2,1)}, f32[1152]{0:T(1024)S(1)}, bf16[1024,1152]{1,0:T(8,128)(2,1)}, f32[1024,1152]{1,0:T(8,128)}) fusion(bf16[4,256,1152]{2,1,0:T(8,128)(2,1)} %all-to-all-done.2, f32[1024]{0:T(1024)S(1)} %fusion.49, f32[1024,1152]{1,0:T(8,128)} %copy-done.8, ...), kind=kOutput, calls=%fused_computation.46 | convolution fusion | flops 10942412800 | bytes 50791424 | tf_op jit(solution)/shard_map/irf,df->ird/dot_general | solution.py:622
  373.5 7.3 convolution_convert_fusion.3
  381.0 6.6 convolution_convert_fusion.4.grad_ref
  387.6 57.1 %shard_map.383 = bf16[1024,3456]{1,0:T(8,128)(2,1)} custom-call(bf16[1024,3456]{1,0:T(8,128)(2,1)} %add_convert_fusion.query_ref.keyval_ref.both_ref, f32[1024,1]{1,0:T(8,128)} %fusion.41.bias_ref, bf16[1024,1152]{1,0:T(8,128)(2,1)} %get-tuple-element.36.mixed_ref, bf16[1024,1152]{1,0:T(8,128)(2,1)} %convolution_convert_fusion.4.grad_ref, ...), custom_call_target="tpu_custom_call" | custom-call | tf_op jit(solution)/shard_map/pallas_call | solution.py:211
  444.8 16.1 %convolution_convert_fusion.2 = bf16[3456,1152]{1,0:T(8,128)(2,1)} fusion(bf16[1024,3456]{1,0:T(8,128)(2,1)} %shard_map.383, bf16[1024,1152]{1,0:T(8,128)(2,1)S(1)} %copy-done.1, f32[1152]{0:T(1024)S(1)} %copy-done.35, f32[1152]{0:T(1024)S(1)} %copy-done.26, f32[1024]{0:T(1024)S(1)} %copy-done.30, f32[1024]{0:T(1024)S(1)} %copy-done.24), kind=kOutput, calls=%fused_computation.13 | convolution fusion | flops 8164786176 | bytes 17417216 | tf_op jit(solution)/shard_map/ire,ird->ed/dot_general | solution.py:679
  466.4 16.1 %fusion.24 = (f32[1152]{0:T(1024)S(1)}, f32[1024]{0:T(1024)S(1)}, f32[1024]{0:T(1024)S(1)}, f32[1152]{0:T(1024)S(1)}, f32[1024,1152]{1,0:T(8,128)S(1)}) fusion(bf16[1024,1152]{1,0:T(8,128)(2,1)S(1)} %copy-done.1, f32[1024]{0:T(1024)S(1)} %copy-done.30, f32[1024]{0:T(1024)S(1)} %copy-done.24, f32[1152]{0:T(1024)S(1)} %copy-done.26, ...), kind=kOutput, calls=%fused_computation.38 | convolution fusion | flops 8165519360 | bytes 22148608 | tf_op jit(solution)/shard_map/ire,ed->ird/dot_general | solution.py:683
  482.6 6.3 multiply_reduce_fusion.2
  494.2 15.8 %all_to_all.49 = f32[32,1,2880]{2,1,0:T(1,128)} all-to-all(f32[32,1,2880]{2,1,0:T(1,128)S(1)} %all_to_all.38), channel_id=1, replica_groups=mesh['img'=8,'band'=4] {'img','band'}, dimensions={0} | all-to-all | bytes 737280 | tf_op jit(solution)/shard_map/all_to_all | solution.py:728
  514.7 20.0 %reduce-scatter.11.cloned.1.call-done = bf16[432,1152]{1,0:T(8,128)(2,1)} async-done(((bf16[3456,1152]{1,0:T(8,128)(2,1)}), bf16[432,1152]{1,0:T(8,128)(2,1)}) %reduce-scatter.11.cloned.1.call-update) | async-done | bytes 995344 | tf_op jit(solution)/shard_map/reduce_scatter | solution.py:682
  534.7 85.6 %reduce-scatter.15.cloned.1.call-done = bf16[576,1152]{1,0:T(8,128)(2,1)} async-done(((bf16[4608,1152]{1,0:T(8,128)(2,1)}), bf16[576,1152]{1,0:T(8,128)(2,1)}) %reduce-scatter.15.cloned.1.call-update) | async-done | bytes 1327120 | tf_op jit(solution)/shard_map/reduce_scatter | solution.py:642
  625.5 5.0 all-to-all-start.3
  644.2 59.9 %reduce-scatter.21.cloned.1.call-done = bf16[1152,144]{1,0:T(8,128)(2,1)} async-done(((bf16[4608,144]{1,0:T(8,128)(2,1)}), bf16[1152,144]{1,0:T(8,128)(2,1)}) %reduce-scatter.21.cloned.1.call-update) | async-done | bytes 331792
  706.2 65.2 %reduce-scatter.19.cloned.1.call-done = bf16[288,1152]{1,0:T(8,128)(2,1)} async-done(((bf16[1152,1152]{1,0:T(8,128)(2,1)}), bf16[288,1152]{1,0:T(8,128)(2,1)}) %reduce-scatter.19.cloned.1.call-update) | async-done | bytes 663568
  (236 shorter events, 124.4 us)
Async XLA Ops:
  7.2 226.2 %all-gather.4.cloned.1.call-start = ((), (), s32[]{:S(2)}) async-start(), calls=%async_computation.12 | async-start | bytes 11943936 | tf_op jit(solution)/shard_map/all_gather | solution.py:546
  9.4 123.8 %copy-start.21 = (f32[14,144]{1,0:T(8,128)S(1)}, f32[14,144]{1,0:T(8,128)}, u32[]{:S(2)}) copy-start(f32[14,144]{1,0:T(8,128)} %param.31) | copy-start | bytes 24196
  9.4 123.9 %copy-start.33 = (bf16[4,1152]{1,0:T(4,128)(2,1)S(1)}, bf16[4,1152]{1,0:T(4,128)(2,1)}, u32[]{:S(2)}) copy-start(bf16[4,1152]{1,0:T(4,128)(2,1)} %param.23) | copy-start | bytes 27652
  14.0 139.5 %copy-start.38 = (s32[4]{0:T(128)S(1)}, s32[4]{0:T(128)}, u32[]{:S(2)}) copy-start(s32[4]{0:T(128)} %param.24) | copy-start | bytes 52
  132.4 88.4 %copy-start = (bf16[1024,1152]{1,0:T(8,128)(2,1)}, bf16[1024,1152]{1,0:T(8,128)(2,1)S(1)}, u32[]{:S(2)}) copy-start(bf16[1024,1152]{1,0:T(8,128)(2,1)S(1)} %get-tuple-element.34) | copy-start | bytes 7077892
  132.4 144.5 %all-gather.6.cloned.1.call-start = ((), (), s32[]{:S(2)}) async-start(), calls=%async_computation.13 | async-start | bytes 11943936 | tf_op jit(solution)/shard_map/all_gather | solution.py:547
  145.3 15.7 %all-to-all-start = ((f32[32,1,864]{2,1,0:T(1,128)}), f32[32,1,864]{2,1,0:T(1,128)S(1)}, u32[]{:S(2)}, u32[]{:S(2)}) async-start(f32[32,1,864]{2,1,0:T(1,128)} %copy.147), calls=%async_computation | async-start | bytes 229376 | tf_op jit(solution)/shard_map/all_to_all | solution.py:559
  161.0 70.1 %all-to-all-start.2 = ((bf16[4,256,1152]{2,1,0:T(8,128)(2,1)}), bf16[4,256,1152]{2,1,0:T(8,128)(2,1)}, u32[]{:S(2)}, u32[]{:S(2)}) async-start(bf16[4,256,1152]{2,1,0:T(8,128)(2,1)} %param.25), calls=%async_computation.2 | async-start | bytes 4718592 | tf_op jit(solution)/shard_map/all_to_all | solution.py:496
  165.5 323.7 %reduce-scatter.17.cloned.1.call-start = ((), (), s32[]{:S(2)}) async-start(), calls=%async_computation.17 | async-start | bytes 11943936 | tf_op jit(solution)/shard_map/reduce_scatter | solution.py:631
  166.7 54.0 %copy-start.36 = (f32[1152]{0:T(1024)}, f32[1152]{0:T(1024)S(1)}, u32[]{:S(2)}) copy-start(f32[1152]{0:T(1024)S(1)} %get-tuple-element.217) | copy-start | bytes 13828
  273.6 241.1 %reduce-scatter.13.cloned.1.call-start = ((), (), s32[]{:S(2)}) async-start(), calls=%async_computation.15 | async-start | bytes 2985984 | tf_op jit(solution)/shard_map/reduce_scatter | solution.py:654
  380.8 153.9 %reduce-scatter.11.cloned.1.call-start = ((), (), s32[]{:S(2)}) async-start(), calls=%async_computation.14 | async-start | bytes 8957952 | tf_op jit(solution)/shard_map/reduce_scatter | solution.py:682
  387.6 57.1 %copy-start.1 = (bf16[1024,1152]{1,0:T(8,128)(2,1)S(1)}, bf16[1024,1152]{1,0:T(8,128)(2,1)}, u32[]{:S(2)}) copy-start(bf16[1024,1152]{1,0:T(8,128)(2,1)} %copy-done) | copy-start | bytes 7077892
  387.6 57.1 %copy-start.24 = (f32[1024]{0:T(1024)S(1)}, f32[1024]{0:T(1024)}, u32[]{:S(2)}) copy-start(f32[1024]{0:T(1024)} %copy-done.23) | copy-start | bytes 12292
  387.6 57.2 %copy-start.26 = (f32[1152]{0:T(1024)S(1)}, f32[1152]{0:T(1024)}, u32[]{:S(2)}) copy-start(f32[1152]{0:T(1024)} %copy-done.25) | copy-start | bytes 13828
  387.6 57.2 %copy-start.30 = (f32[1024]{0:T(1024)S(1)}, f32[1024]{0:T(1024)}, u32[]{:S(2)}) copy-start(f32[1024]{0:T(1024)} %copy-done.29) | copy-start | bytes 12292
  387.6 57.2 %copy-start.35 = (f32[1152]{0:T(1024)S(1)}, f32[1152]{0:T(1024)}, u32[]{:S(2)}) copy-start(f32[1152]{0:T(1024)} %copy-done.34) | copy-start | bytes 13828
  460.9 159.4 %reduce-scatter.15.cloned.1.call-start = ((), (), s32[]{:S(2)}) async-start(), calls=%async_computation.16 | async-start | bytes 11943936 | tf_op jit(solution)/shard_map/reduce_scatter | solution.py:642
  461.5 242.6 %reduce-scatter.21.cloned.1.call-start = ((), (), s32[]{:S(2)}) async-start(), calls=%async_computation.19 | async-start | bytes 2949120
  510.0 115.5 %all-to-all-start.1 = ((bf16[4,1,256,1152]{3,2,1,0:T(8,128)(2,1)}), bf16[4,1,256,1152]{3,2,1,0:T(8,128)(2,1)}, u32[]{:S(2)}, u32[]{:S(2)}) async-start(bf16[4,1,256,1152]{3,2,1,0:T(8,128)(2,1)} %bitcast.6), calls=%async_computation.1 | async-start | bytes 4718592 | tf_op jit(solution)/shard_map/all_to_all | solution.py:500
  514.6 256.8 %reduce-scatter.19.cloned.1.call-start = ((), (), s32[]{:S(2)}) async-start(), calls=%async_computation.18 | async-start | bytes 3317760
  625.5 154.3 %all-to-all-start.3 = ((bf16[4,1,256,1152]{3,2,1,0:T(8,128)(2,1)}), bf16[4,1,256,1152]{3,2,1,0:T(8,128)(2,1)}, u32[]{:S(2)}, u32[]{:S(2)}) async-start(bf16[4,1,256,1152]{3,2,1,0:T(8,128)(2,1)} %bitcast.101), calls=%async_computation.3 | async-start | bytes 4718592 | tf_op jit(solution)/shard_map/all_to_all | solution.py:500
  705.4 65.9 %copy-start.11 = (bf16[144,1152]{1,0:T(8,128)(2,1)}, bf16[144,1152]{1,0:T(8,128)(2,1)S(1)}, u32[]{:S(2)}) copy-start(bf16[144,1152]{1,0:T(8,128)(2,1)S(1)} %copy.169) | copy-start | bytes 995332
  780.4 11.4 %all-to-all-start.5 = ((f32[32,1,128]{2,1,0:T(1,128)}), f32[32,1,128]{2,1,0:T(1,128)}, u32[]{:S(2)}, u32[]{:S(2)}) async-start(f32[32,1,128]{2,1,0:T(1,128)} %broadcast_in_dim.18), calls=%async_computation.9 | async-start | bytes 32768 | tf_op jit(solution)/shard_map/all_to_all | solution.py:510
  (29 other events, 298.0 us)
Sparse Core Ops, SparseCore 0:
  132.5 68.0 all-gather.3
  202.6 63.8 all-gather.5
  273.7 81.6 reduce-scatter.16
  380.9 43.3 reduce-scatter.12
  461.0 73.6 reduce-scatter.10
  538.1 82.1 reduce-scatter.14
  622.6 81.4 reduce-scatter.20
  707.0 64.3 reduce-scatter.18

commit v4 on v3

--- a/solution.py
+++ b/solution.py
@@ -448,6 +448,254 @@
     )(wide, tall, tokens)
 
 
+def add_low(left, right):
+    return (left.astype(jnp.float32) + right.astype(jnp.float32)).astype(jnp.bfloat16)
+
+
+def tail_kernel(
+    qkv_ref, out_ref, up_ref, down_ref, rows_ref,
+    wide_ref, tall_ref, back_ref,
+    own, from_core, first_x, first_y, last_x, last_y, turned, held, tall, held_in, tall_in,
+    core_send, core_recv, flat_send, flat_recv, line_send, line_recv, row_send, row_recv, local_sem,
+    *, bands, early,
+):
+    img, band = lax.axis_index("img"), lax.axis_index("band")
+    qkv_part, out_part = own.shape[1], out_ref.shape[0]
+    width = turned.shape[0]
+    depth, tall_width = wide_ref.shape[0], tall_ref.shape[1]
+    row_block = back_ref.shape[1]
+    half = first_x.shape[1]
+    lanes = 128
+    first = -(-(qkv_part + out_part) // lanes) * lanes
+    beside_x, beside_y, sibling = flip(img, 2), flip(img, 4), flip(img, 1)
+    chips = (img, beside_x, beside_y, flip(beside_x, 4))
+    upper, lower = pl.ds(0, half), pl.ds(half, qkv_part - half)
+
+    barrier = pltpu.get_barrier_semaphore()
+    for other in (beside_x, beside_y, sibling):
+        pl.semaphore_signal(barrier, inc=1, device_id={"img": other}, device_id_type=MESH)
+    for step in range(1, bands):
+        pl.semaphore_signal(
+            barrier, inc=1, device_id={"band": lax.rem(band + step, bands)}, device_id_type=MESH
+        )
+    pl.semaphore_wait(barrier, 3 + bands - 1)
+
+    def qkv_rows(owner):
+        return qkv_ref.at[pl.ds(pl.multiple_of(owner * qkv_part, 16), qkv_part), :]
+
+    def core_copy(at):
+        return pltpu.make_async_remote_copy(
+            src_ref=qkv_rows(flip(chips[at], 1)), dst_ref=from_core.at[at],
+            send_sem=core_send.at[at], recv_sem=core_recv.at[at],
+            device_id={"img": sibling}, device_id_type=MESH,
+        )
+
+    def own_copy(at):
+        return pltpu.make_async_copy(qkv_rows(chips[at]), own.at[at], local_sem.at[at])
+
+    plan = (
+        (own.at[1, upper], first_x.at[0], beside_x),
+        (own.at[3, upper], first_x.at[1], beside_x),
+        (own.at[2, lower], first_y.at[0], beside_y),
+        (own.at[3, lower], first_y.at[1], beside_y),
+        (own.at[2, upper], last_y, beside_y),
+        (own.at[1, lower], last_x, beside_x),
+    )
+
+    def flat_copy(at):
+        source, target, toward = plan[at]
+        return pltpu.make_async_remote_copy(
+            src_ref=source, dst_ref=target, send_sem=flat_send.at[at], recv_sem=flat_recv.at[at],
+            device_id={"img": toward}, device_id_type=MESH,
+        )
+
+    def row_span(owner):
+        return pl.ds(pl.multiple_of(owner * row_block, 16), row_block)
+
+    def row_copy(step):
+        target = lax.rem(band + step, bands)
+        return pltpu.make_async_remote_copy(
+            src_ref=rows_ref.at[row_span(target), :], dst_ref=back_ref.at[band],
+            send_sem=row_send.at[step - 1], recv_sem=row_recv.at[step - 1],
+            device_id={"band": target}, device_id_type=MESH,
+        )
+
+    def row_arrival(step):
+        source = lax.rem(band + bands - step, bands)
+        return pltpu.make_async_remote_copy(
+            src_ref=back_ref.at[source], dst_ref=back_ref.at[source],
+            send_sem=row_send.at[step - 1], recv_sem=row_recv.at[step - 1],
+            device_id={"band": source}, device_id_type=MESH,
+        )
+
+    def piece(part, owner, way=None):
+        if part == 2:
+            span = pl.ds(pl.multiple_of(owner * tall_width, lanes), tall_width)
+            return tall.at[:, span] if way is None else tall_in.at[way, :, span]
+        span = pl.ds(0, first) if part == 0 else pl.ds(first, width - first)
+        down = pl.ds(pl.multiple_of(owner * depth, 16), depth)
+        return held.at[down, span] if way is None else held_in.at[way, down, span]
+
+    def line_copy(part, way, owner, toward):
+        return pltpu.make_async_remote_copy(
+            src_ref=piece(part, owner), dst_ref=piece(part, owner, way),
+            send_sem=line_send.at[part, way, owner], recv_sem=line_recv.at[part, way, owner],
+            device_id={"band": toward}, device_id_type=MESH,
+        )
+
+    def line_ends(part):
+        for step in range(bands - 1):
+
+            @pl.when(band == 0)
+            def _():
+                line_copy(part, 0, bands - 1 - step, band + 1).start()
+
+            @pl.when(band == bands - 1)
+            def _():
+                line_copy(part, 1, step, band - 1).start()
+
+    def line_round(part, step):
+        for way, owner, sign in ((0, bands - 1 - step, 1), (1, step, -1)):
+
+            @pl.when((sign * (owner - band) > 0) & (band > 0) & (band < bands - 1))
+            def _():
+                copy = line_copy(part, way, owner, band + sign)
+                copy.wait_recv()
+                mine = piece(part, owner)
+                mine[...] = add_low(mine[...], piece(part, owner, way)[...])
+                copy.start()
+
+    def line_finish(part, target, span):
+        total = piece(part, band)[...].astype(jnp.float32)
+        target[:, span] = total
+        for way, sign in ((0, 1), (1, -1)):
+
+            @pl.when((band - sign >= 0) & (band - sign < bands))
+            def _():
+                line_copy(part, way, band, band - sign).wait_recv()
+                target[:, span] += piece(part, band, way)[...].astype(jnp.float32)
+
+    def line_sent(part):
+        for way, sign in ((0, 1), (1, -1)):
+            for owner in range(bands):
+
+                @pl.when(sign * (owner - band) > 0)
+                def _():
+                    line_copy(part, way, owner, band + sign).wait_send()
+
+    def turn(tile):
+        span = pl.ds(pl.multiple_of(tile * lanes, lanes), lanes)
+        held[:, span] = turned[span, :].astype(jnp.float32).T.astype(jnp.bfloat16)
+
+    order = (3, 1, 2, 0)
+    for at in order:
+        core_copy(at).start()
+    for at in order:
+        own_copy(at).start()
+    turned[pl.ds(qkv_part, out_part), :] = out_ref[...]
+    turned[pl.ds(qkv_part + out_part, width - qkv_part - out_part), :] = up_ref[...]
+    pl.loop(first // lanes, width // lanes)(turn)
+    tall[...] = down_ref[...]
+    line_ends(1)
+    line_ends(2)
+    keep = pltpu.make_async_copy(rows_ref.at[row_span(band), :], back_ref.at[band], local_sem.at[4])
+    keep.start()
+    for step in range(1, bands):
+        row_copy(step).start()
+    for at in order:
+        own_copy(at).wait()
+        core_copy(at).wait_recv()
+        own[at] = add_low(own[at], from_core[at])
+        for ready in {3: (1, 3), 1: (0,), 2: (2,), 0: ()}[at]:
+            flat_copy(ready).start()
+    flat_copy(1).wait_recv()
+    own[2, upper] = add_low(own[2, upper], first_x[1])
+    flat_copy(4).start()
+    flat_copy(3).wait_recv()
+    own[1, lower] = add_low(own[1, lower], first_y[1])
+    flat_copy(5).start()
+    for part in early:
+        line_round(part, 0)
+    flat_copy(0).wait_recv()
+    flat_copy(2).wait_recv()
+    flat_copy(4).wait_recv()
+    flat_copy(5).wait_recv()
+    turned[upper, :] = (
+        own[0, upper].astype(jnp.float32)
+        + first_x[0].astype(jnp.float32)
+        + last_y[...].astype(jnp.float32)
+    ).astype(jnp.bfloat16)
+    turned[lower, :] = (
+        own[0, lower].astype(jnp.float32)
+        + first_y[0].astype(jnp.float32)
+        + last_x[...].astype(jnp.float32)
+    ).astype(jnp.bfloat16)
+    pl.loop(0, first // lanes)(turn)
+    line_ends(0)
+    for step in range(bands - 1):
+        for part in (1, 2, 0):
+            if step > 0 or part not in early:
+                line_round(part, step)
+    line_finish(1, wide_ref, pl.ds(first, width - first))
+    line_finish(2, tall_ref, pl.ds(0, tall_width))
+    line_finish(0, wide_ref, pl.ds(0, first))
+    for part in range(3):
+        line_sent(part)
+    for at in range(4):
+        core_copy(at).wait_send()
+    for at in range(6):
+        flat_copy(at).wait_send()
+    for step in range(1, bands):
+        row_copy(step).wait_send()
+        row_arrival(step).wait_recv()
+    keep.wait()
+
+
+def tail_exchange(qkv_grad, out_sum, up_sum, down_sum, rows, bands, imgs):
+    low = jnp.bfloat16
+    qkv_part, features = qkv_grad.shape[0] // imgs, qkv_grad.shape[1]
+    out_part, up_part = out_sum.shape[0], up_sum.shape[0]
+    width = qkv_part + out_part + up_part
+    tall_rows, tall_width = down_sum.shape[0], down_sum.shape[1] // bands
+    half = -(-qkv_part // 32) * 16
+    anywhere, vmem = pl.BlockSpec(memory_space=pl.ANY), pl.BlockSpec(memory_space=pltpu.VMEM)
+    return pl.pallas_call(
+        functools.partial(tail_kernel, bands=bands, early=(1, 2)),
+        out_shape=(
+            jax.ShapeDtypeStruct((features // bands, width), jnp.float32),
+            jax.ShapeDtypeStruct((tall_rows, tall_width), jnp.float32),
+            jax.ShapeDtypeStruct((bands, rows.shape[0] // bands, features), low),
+        ),
+        in_specs=[anywhere, vmem, vmem, vmem, anywhere],
+        out_specs=(vmem, vmem, anywhere),
+        scratch_shapes=[
+            pltpu.VMEM((4, qkv_part, features), low),
+            pltpu.VMEM((4, qkv_part, features), low),
+            pltpu.VMEM((2, half, features), low),
+            pltpu.VMEM((2, qkv_part - half, features), low),
+            pltpu.VMEM((qkv_part - half, features), low),
+            pltpu.VMEM((half, features), low),
+            pltpu.VMEM((width, features), low),
+            pltpu.VMEM((features, width), low),
+            pltpu.VMEM((tall_rows, tall_width * bands), low),
+            pltpu.VMEM((2, features, width), low),
+            pltpu.VMEM((2, tall_rows, tall_width * bands), low),
+            pltpu.SemaphoreType.DMA((4,)),
+            pltpu.SemaphoreType.DMA((4,)),
+            pltpu.SemaphoreType.DMA((6,)),
+            pltpu.SemaphoreType.DMA((6,)),
+            pltpu.SemaphoreType.DMA((3, 2, bands)),
+            pltpu.SemaphoreType.DMA((3, 2, bands)),
+            pltpu.SemaphoreType.DMA((bands - 1,)),
+            pltpu.SemaphoreType.DMA((bands - 1,)),
+            pltpu.SemaphoreType.DMA((5,)),
+        ],
+        compiler_params=pltpu.CompilerParams(
+            collective_id=1, has_side_effects=True, vmem_limit_bytes=50 * 2**20
+        ),
+    )(qkv_grad, out_sum, up_sum, down_sum, rows)
+
+
 def body(
     inputs,
     condition,
@@ -639,7 +887,7 @@
     up_grad = jnp.einsum(
         "irf,ird->fd", pre_grad, second_in, preferred_element_type=jnp.float32
     ).astype(low_type)
-    up_sum = lax.psum_scatter(up_grad, "img", scatter_dimension=0, tiled=True)
+    up_sum = lax.psum_scatter(after(up_grad, down_sum), "img", scatter_dimension=0, tiled=True)
     second_grad = jnp.einsum("irf,fd->ird", after(pre_grad, up_grad), up_full, preferred_element_type=jnp.float32)
     shift_two_grad = jnp.sum(second_grad, axis=1)
     scale_two_grad = jnp.sum(second_grad * normed_two, axis=1)
@@ -651,7 +899,7 @@
     out_grad = jnp.einsum(
         "ire,ird->ed", attended_grad, mixed, preferred_element_type=jnp.float32
     ).astype(low_type)
-    out_sum = lax.psum_scatter(out_grad, "img", scatter_dimension=0, tiled=True)
+    out_sum = lax.psum_scatter(after(out_grad, up_sum), "img", scatter_dimension=0, tiled=True)
     mixed_grad = jnp.einsum(
         "ire,ed->ird", after(attended_grad, out_grad), out_full, preferred_element_type=jnp.float32
     ).astype(jnp.bfloat16)
@@ -679,16 +927,12 @@
     qkv_weight_grad = jnp.einsum(
         "ire,ird->ed", qkv_grad, first_in, preferred_element_type=jnp.float32
     ).astype(low_type)
-    qkv_sum = lax.psum_scatter(qkv_weight_grad, "img", scatter_dimension=0, tiled=True)
     first_grad = jnp.einsum("ire,ed->ird", after(qkv_grad, qkv_weight_grad), qkv_full, preferred_element_type=jnp.float32)
     shift_one_grad = jnp.sum(first_grad, axis=1)
     scale_one_grad = jnp.sum(first_grad * normed_one, axis=1)
-    input_grad = to_bands(
-        (
-            middle_grad
-            + normalize_back(normed_one, inverse_one, first_grad * (1.0 + scale_one))
-        ).astype(low_type)
-    ).astype(jnp.float32)
+    input_grad_low = (
+        middle_grad + normalize_back(normed_one, inverse_one, first_grad * (1.0 + scale_one))
+    ).astype(low_type)
     mod_grad = jnp.stack(
         [
             shift_one_grad,
@@ -737,15 +981,24 @@
         precision=lax.Precision.HIGHEST,
     )
     bias_total = jnp.sum(got[:, own * ada_columns :], axis=0).reshape(bias_rows, bias_columns)
-    down_shard = lax.psum_scatter(down_sum, "band", scatter_dimension=1, tiled=True).T.astype(
-        jnp.float32
-    )
-    wide_shard = lax.psum_scatter(
-        jnp.concatenate([qkv_sum, out_sum, up_sum], axis=0).T,
-        "band",
-        scatter_dimension=0,
-        tiled=True,
-    ).astype(jnp.float32)
+    if img_count == 8 and own == 1 and split == 1:
+        wide_shard, tall_shard, input_grad_low = tail_exchange(
+            qkv_weight_grad, out_sum, up_sum, down_sum, input_grad_low[0], band_count, img_count
+        )
+    else:
+        qkv_sum = lax.psum_scatter(qkv_weight_grad, "img", scatter_dimension=0, tiled=True)
+        tall_shard = lax.psum_scatter(down_sum, "band", scatter_dimension=1, tiled=True).astype(
+            jnp.float32
+        )
+        wide_shard = lax.psum_scatter(
+            jnp.concatenate([qkv_sum, out_sum, up_sum], axis=0).T,
+            "band",
+            scatter_dimension=0,
+            tiled=True,
+        ).astype(jnp.float32)
+        input_grad_low = to_bands(input_grad_low)
+    input_grad = input_grad_low.astype(jnp.float32)
+    down_shard = tall_shard.T
     qkv_shard = wide_shard[:, :qkv_part]
     out_shard = wide_shard[:, qkv_part : qkv_part + out_part]
     up_shard = wide_shard[:, qkv_part + out_part :]

time: 838 us -> 762 us (0.909)
  waiting for transfers between devices: 238 us -> 50.7 us
  Pallas kernels: 208 us -> 349 us
  local copies, waits for them, and re-layouts: 51.8 us -> 30 us
  other arithmetic: 51.6 us -> 41.6 us
    pallas_call x0 -> x1, Pallas kernels: none -> 141 us  [tail_exchange(): pl.pallas_call(functools.partial(tail_kernel, bands=bands, early=(1, 2)),...]
    unnamed x10 -> x5, waiting for transfers between devices: 126 us -> 0.76 us
    reduce_scatter x3 -> x2, waiting for transfers between devices: 106 us -> 17.4 us  [the longest x1 17.3 us: body(): lax.psum_scatter(after(out_grad, up_sum), 'img', scatter_dimension=0, til...]
    reduce_scatter x1, waiting for transfers between devices: 0.02 us -> 29.5 us  [body(): lax.psum_scatter(down_grad, 'img', scatter_dimension=0, tiled=True)]
    unnamed x110 -> x114, local copies, waits for them, and re-layouts: 46.4 us -> 24 us
    all_to_all x1, starting transfers between devices: 4.42 us -> 16.2 us  [sum_everywhere(): lax.all_to_all(sent, ('img', 'band'), split_axis=0, concat_axis=0, tiled=...]
  transfers between devices with their start and end apart: 13 -> 9, of which waited for: 6 -> 3; matrix products, arithmetic and copies ran while one was open for 32% -> 31% of each run, Pallas kernels for 11% -> 31%
where the time goes in v4:
time: 762 us; the launch traced here: 756 us
  Pallas kernels  349 us (46%)
  matrix products  206 us (27%)
  waiting for transfers between devices  50.7 us (7%)
  other arithmetic  41.6 us (5%)
  starting transfers between devices  33.3 us (4%)
  local copies, waits for them, and re-layouts  30 us (4%)
  blocking collectives  25.5 us (3%)
  between operations  20.9 us (3%)
    pallas_call x1, Pallas kernels, tail_exchange(): pl.pallas_call(functools.partial(tail_kernel, bands=bands, early=(1, 2)),...  141 us
    pallas_call x1, Pallas kernels, start_exchange(): pl.pallas_call(functools.partial(start_kernel, bands=bands, qkv_part=qkv_...  115 us
    pallas_call x1, Pallas kernels, attention_backward(): pl.pallas_call(shared_kernel, out_shape=jax.ShapeDtypeStruct((rows, 3 * f...  56.4 us
    pallas_call x1, Pallas kernels, attention_forward(): pl.pallas_call(functools.partial(attention_forward_kernel, features=featu...  36.8 us
    reduce_scatter x1, waiting for transfers between devices, body(): lax.psum_scatter(down_grad, 'img', scatter_dimension=0, tiled=True)  29.5 us
    dot_general x1, matrix products, body(): jnp.einsum('ird,df->irf', after(branch_grad, down_grad), down_full, prefe...  28.1 us
    dot_general x1, matrix products, body(): jnp.einsum('irf,df->ird', hidden_low, down_full, preferred_element_type=j...  24.7 us
    unnamed x114, local copies, waits for them, and re-layouts  24 us
  transfers between devices with their start and end apart: 9, of which 3 were waited for; matrix products, arithmetic and copies ran while one was open for 31% of the time, Pallas kernels for 31%

profile of v4, /device:TPU:0, one launch (start us, length us, event | category | flops | bytes accessed | tf_op | source)
XLA Modules:
  0.0 756.4 jit_solution(8450232628137667195)
XLA Ops:
  14.0 114.5 %shard_map.381 = (bf16[3456,1152]{1,0:T(8,128)(2,1)}, bf16[1152,1152]{1,0:T(8,128)(2,1)S(1)}, bf16[576,1152]{1,0:T(8,128)(2,1)S(1)}, bf16[144,4608]{1,0:T(8,128)(2,1)S(1)}, bf16[1024,1152]{1,0:T(8,128)(2,1)S(1)}) custom-call(bf16[288,1152]{1,0:T(8,128)(2,1)S(1)} %concatenate.29.wide_ref, bf16[144,1152]{1,0:T(8,128)(2,1)S(1)} %convert_bitcast_fusion.tall_ref, ...), custom_call_target="tpu_custom_call" | custom-call | tf_op jit(solution)/shard_map/pallas_call | solution.py:423
  133.1 9.3 %all-gather = bf16[8,1,6624]{2,1,0:T(2,128)(2,1)S(1)} all-gather(bf16[1,1,6624]{2,1,0:T(2,128)(2,1)S(1)} %maximum_bitcast_fusion), channel_id=1, replica_groups=mesh['img'=8,'band'=4] {'img'}, dimensions={0}, use_global_device_ids=true | all-gather | bytes 119232 | tf_op jit(solution)/shard_map/all_gather | solution.py:764
  145.1 7.4 all-to-all-start
  160.8 4.5 all-to-all-start.2
  166.2 16.9 %add_convert_fusion.query_ref.keyval_ref.both_ref = bf16[1024,3456]{1,0:T(8,128)(2,1)} fusion(bf16[3456,1152]{1,0:T(8,128)(2,1)} %get-tuple-element.40, f32[3456]{0:T(1024)S(1)} %pad_maximum_fusion.1, bf16[1024,1152]{1,0:T(8,128)(2,1)S(1)} %get-tuple-element.39, f32[1152]{0:T(1024)S(1)} %get-tuple-element.225, f32[1152]{0:T(1024)S(1)} %get-tuple-element.226, ...), kind=kOutput, calls=%fused_computation.15 | convolution fusion | flops 8167882752 | bytes 17431040 | tf_op jit(solution)/shard_map/ird,ed->ire/dot_general | solution.py:836
  183.1 36.8 %shard_map.382 = (bf16[1024,1152]{1,0:T(8,128)(2,1)}, f32[16,1024]{1,0:T(8,128)}) custom-call(bf16[1024,3456]{1,0:T(8,128)(2,1)} %add_convert_fusion.query_ref.keyval_ref.both_ref, bf16[1024,3456]{1,0:T(8,128)(2,1)} %add_convert_fusion.query_ref.keyval_ref.both_ref, f32[1024,1]{1,0:T(8,128)} %fusion.38.bias_ref), custom_call_target="tpu_custom_call" | custom-call | tf_op jit(solution)/shard_map/pallas_call | solution.py:119
  220.0 7.5 fusion.58
  232.6 22.5 %fusion.49 = f32[1024,4608]{1,0:T(8,128)} fusion(bf16[4608,1152]{1,0:T(8,128)(2,1)} %all-gather.4.cloned.1.call-done, f32[1024,1152]{1,0:T(8,128)} %copy-done.11, f32[1152]{0:T(1024)S(1)} %get-tuple-element.223, f32[1152]{0:T(1024)S(1)} %get-tuple-element.224, f32[1024]{0:T(1024)S(1)} %add_rsqrt_fusion, f32[1024]{0:T(1024)S(1)} %broadcast_multiply_fusion.5), kind=kOutput, calls=%fused_computation.147 | convolution fusion | flops 10877534208 | bytes 34227200 | tf_op jit(solution)/shard_map/ird,fd->irf/dot_general | solution.py:864
  255.1 18.2 %convolution_convert_fusion.1 = bf16[1152,4608]{1,0:T(8,128)(2,1)} fusion(bf16[1024,1152]{1,0:T(8,128)(2,1)S(1)} %multiply_convert_fusion.2, f32[1024,4608]{1,0:T(8,128)} %fusion.49, f32[4608]{0:T(1024)S(1)} %add.277), kind=kOutput, calls=%fused_computation.3 | convolution fusion | flops 10924130304 | bytes 31868928 | tf_op jit(solution)/shard_map/ird,irf->df/dot_general | solution.py:876
  276.0 28.1 %convert_reduce_fusion = (f32[4608]{0:T(1024)S(1)}, bf16[1024,4608]{1,0:T(8,128)(2,1)S(1)}) fusion(f32[1024,4608]{1,0:T(8,128)} %fusion.49, f32[4608]{0:T(1024)S(1)} %add.277, bf16[1152,4608]{1,0:T(8,128)(2,1)} %all-gather.6.cloned.1.call-done, bf16[1,1024,1152]{2,1,0:T(8,128)(2,1)S(1)} %get-tuple-element.46), kind=kOutput, calls=%fused_computation.11 | convolution fusion | flops 10980159488 | bytes 41324544 | tf_op jit(solution)/shard_map/ird,df->irf/dot_general | solution.py:880
  307.6 18.0 %convolution_convert_fusion = bf16[4608,1152]{1,0:T(8,128)(2,1)} fusion(bf16[1024,4608]{1,0:T(8,128)(2,1)S(1)} %get-tuple-element.266, f32[1024,1152]{1,0:T(8,128)} %copy-done.11, f32[1152]{0:T(1024)S(1)} %get-tuple-element.223, f32[1152]{0:T(1024)S(1)} %get-tuple-element.224, f32[1024]{0:T(1024)S(1)} %add_rsqrt_fusion, f32[1024]{0:T(1024)S(1)} %broadcast_multiply_fusion.5), kind=kOutput, calls=%fused_computation.2 | convolution fusion | flops 10882842624 | bytes 24790016 | tf_op jit(solution)/shard_map/irf,ird->fd/dot_general | solution.py:887
  325.6 29.5 %reduce-scatter.4.cloned.1.call-done.down_ref = bf16[144,4608]{1,0:T(8,128)(2,1)} async-done(((bf16[1152,4608]{1,0:T(8,128)(2,1)}), bf16[144,4608]{1,0:T(8,128)(2,1)}) %reduce-scatter.4.cloned.1.call-update) | async-done | bytes 1327120 | tf_op jit(solution)/shard_map/reduce_scatter | solution.py:879
  355.4 20.9 %multiply_reduce_fusion.1 = (f32[1152]{0:T(1024)S(1)}, f32[1024]{0:T(1024)S(1)}, f32[1024]{0:T(1024)S(1)}, f32[1152]{0:T(1024)S(1)}, f32[1024,1152]{1,0:T(8,128)}) fusion(f32[1024,1152]{1,0:T(8,128)} %copy-done.11, f32[1024]{0:T(1024)S(1)} %add_rsqrt_fusion, f32[1024]{0:T(1024)S(1)} %broadcast_multiply_fusion.5, f32[1152]{0:T(1024)S(1)} %get-tuple-element.224, ...), kind=kOutput, calls=%fused_computation.47 | convolution fusion | flops 10882248704 | bytes 29521408 | tf_op jit(solution)/shard_map/irf,fd->ird/dot_general | solution.py:891
  376.3 24.7 %multiply_reduce_fusion = (f32[1152]{0:T(1024)S(1)}, bf16[1024,1152]{1,0:T(8,128)(2,1)}, f32[1152]{0:T(1024)S(1)}, bf16[1024,1152]{1,0:T(8,128)(2,1)}, f32[1024,1152]{1,0:T(8,128)}) fusion(bf16[4,256,1152]{2,1,0:T(8,128)(2,1)} %all-to-all-done.2, f32[1024]{0:T(1024)S(1)} %fusion.46, f32[1024,1152]{1,0:T(8,128)} %copy-done.11, ...), kind=kOutput, calls=%fused_computation.46 | convolution fusion | flops 10942412800 | bytes 50791424 | tf_op jit(solution)/shard_map/irf,df->ird/dot_general | solution.py:870
  401.4 7.5 convolution_convert_fusion.3
  408.9 6.6 convolution_convert_fusion.4.grad_ref
  415.6 56.4 %shard_map.383 = bf16[1024,3456]{1,0:T(8,128)(2,1)} custom-call(bf16[1024,3456]{1,0:T(8,128)(2,1)} %add_convert_fusion.query_ref.keyval_ref.both_ref, f32[1024,1]{1,0:T(8,128)} %fusion.38.bias_ref, bf16[1024,1152]{1,0:T(8,128)(2,1)} %get-tuple-element.41.mixed_ref, bf16[1024,1152]{1,0:T(8,128)(2,1)} %convolution_convert_fusion.4.grad_ref, ...), custom_call_target="tpu_custom_call" | custom-call | tf_op jit(solution)/shard_map/pallas_call | solution.py:211
  472.1 16.4 %convolution_convert_fusion.2.qkv_ref = bf16[3456,1152]{1,0:T(8,128)(2,1)} fusion(bf16[1024,3456]{1,0:T(8,128)(2,1)} %shard_map.383, bf16[1024,1152]{1,0:T(8,128)(2,1)S(1)} %copy-done.1, f32[1152]{0:T(1024)S(1)} %copy-done.38, f32[1152]{0:T(1024)S(1)} %copy-done.30, f32[1024]{0:T(1024)S(1)} %copy-done.33, f32[1024]{0:T(1024)S(1)} %copy-done.28), kind=kOutput, calls=%fused_computation.13 | convolution fusion | flops 8164786176 | bytes 17417216 | tf_op jit(solution)/shard_map/ire,ird->ed/dot_general | solution.py:927
  488.5 13.5 %fusion.24 = (f32[1152]{0:T(1024)S(1)}, f32[1024]{0:T(1024)S(1)}, f32[1024]{0:T(1024)S(1)}, f32[1152]{0:T(1024)S(1)}, f32[1024,1152]{1,0:T(8,128)S(1)}) fusion(bf16[1024,1152]{1,0:T(8,128)(2,1)S(1)} %copy-done.1, f32[1024]{0:T(1024)S(1)} %copy-done.33, f32[1024]{0:T(1024)S(1)} %copy-done.28, f32[1152]{0:T(1024)S(1)} %copy-done.30, ...), kind=kOutput, calls=%fused_computation.38 | convolution fusion | flops 8165519360 | bytes 22148608 | tf_op jit(solution)/shard_map/ire,ed->ird/dot_general | solution.py:930
  511.1 16.2 %all_to_all.44 = f32[32,1,2880]{2,1,0:T(1,128)S(1)} all-to-all(f32[32,1,2880]{2,1,0:T(1,128)S(1)} %all_to_all.34), channel_id=1, replica_groups=mesh['img'=8,'band'=4] {'img','band'}, dimensions={0} | all-to-all | bytes 737280 | tf_op jit(solution)/shard_map/all_to_all | solution.py:972
  527.3 4.8 all-to-all-start.1
  537.3 17.3 %reduce-scatter.8.cloned.1.call-done.out_ref = bf16[144,1152]{1,0:T(8,128)(2,1)} async-done(((bf16[1152,1152]{1,0:T(8,128)(2,1)}), bf16[144,1152]{1,0:T(8,128)(2,1)}) %reduce-scatter.8.cloned.1.call-update) | async-done | bytes 331792 | tf_op jit(solution)/shard_map/reduce_scatter | solution.py:902
  555.6 140.9 %shard_map.384 = (f32[288,1152]{1,0:T(8,128)S(1)}, f32[144,1152]{1,0:T(8,128)S(1)}, bf16[4,256,1152]{2,1,0:T(8,128)(2,1)}) custom-call(bf16[3456,1152]{1,0:T(8,128)(2,1)} %convolution_convert_fusion.2.qkv_ref, bf16[144,1152]{1,0:T(8,128)(2,1)S(1)} %copy-done.6, bf16[576,1152]{1,0:T(8,128)(2,1)S(1)} %copy-done.3, ...), custom_call_target="tpu_custom_call" | custom-call | tf_op jit(solution)/shard_map/pallas_call | solution.py:662
  703.0 16.2 %all-to-all-start.4 = ((f32[32,1,128]{2,1,0:T(1,128)}), f32[32,1,128]{2,1,0:T(1,128)S(1)}, u32[]{:S(2)}, u32[]{:S(2)}) async-start(f32[32,1,128]{2,1,0:T(1,128)} %broadcast_in_dim.18), calls=%async_computation.7 | async-start | bytes 32768 | tf_op jit(solution)/shard_map/all_to_all | solution.py:758
  (230 shorter events, 80.7 us)
Async XLA Ops:
  7.2 225.4 %all-gather.4.cloned.1.call-start = ((), (), s32[]{:S(2)}) async-start(), calls=%async_computation.8 | async-start | bytes 11943936 | tf_op jit(solution)/shard_map/all_gather | solution.py:794
  9.4 123.5 %copy-start.25 = (f32[14,144]{1,0:T(8,128)S(1)}, f32[14,144]{1,0:T(8,128)}, u32[]{:S(2)}) copy-start(f32[14,144]{1,0:T(8,128)} %param.31) | copy-start | bytes 24196
  9.4 123.6 %copy-start.36 = (bf16[4,1152]{1,0:T(4,128)(2,1)S(1)}, bf16[4,1152]{1,0:T(4,128)(2,1)}, u32[]{:S(2)}) copy-start(bf16[4,1152]{1,0:T(4,128)(2,1)} %param.23) | copy-start | bytes 27652
  14.0 139.8 %copy-start.41 = (s32[4]{0:T(128)S(1)}, s32[4]{0:T(128)}, u32[]{:S(2)}) copy-start(s32[4]{0:T(128)} %param.24) | copy-start | bytes 52
  132.2 87.8 %copy-start = (bf16[1024,1152]{1,0:T(8,128)(2,1)}, bf16[1024,1152]{1,0:T(8,128)(2,1)S(1)}, u32[]{:S(2)}) copy-start(bf16[1024,1152]{1,0:T(8,128)(2,1)S(1)} %get-tuple-element.39) | copy-start | bytes 7077892
  132.2 143.8 %all-gather.6.cloned.1.call-start = ((), (), s32[]{:S(2)}) async-start(), calls=%async_computation.9 | async-start | bytes 11943936 | tf_op jit(solution)/shard_map/all_gather | solution.py:795
  145.1 15.7 %all-to-all-start = ((f32[32,1,864]{2,1,0:T(1,128)}), f32[32,1,864]{2,1,0:T(1,128)S(1)}, u32[]{:S(2)}, u32[]{:S(2)}) async-start(f32[32,1,864]{2,1,0:T(1,128)} %copy.108), calls=%async_computation | async-start | bytes 229376 | tf_op jit(solution)/shard_map/all_to_all | solution.py:807
  160.8 69.5 %all-to-all-start.2 = ((bf16[4,256,1152]{2,1,0:T(8,128)(2,1)}), bf16[4,256,1152]{2,1,0:T(8,128)(2,1)}, u32[]{:S(2)}, u32[]{:S(2)}) async-start(bf16[4,256,1152]{2,1,0:T(8,128)(2,1)} %param.25), calls=%async_computation.2 | async-start | bytes 4718592 | tf_op jit(solution)/shard_map/all_to_all | solution.py:744
  165.3 189.8 %reduce-scatter.4.cloned.1.call-start = ((), (), s32[]{:S(2)}) async-start(), calls=%async_computation.10 | async-start | bytes 11943936 | tf_op jit(solution)/shard_map/reduce_scatter | solution.py:879
  166.2 53.8 %copy-start.39 = (f32[1152]{0:T(1024)}, f32[1152]{0:T(1024)S(1)}, u32[]{:S(2)}) copy-start(f32[1152]{0:T(1024)S(1)} %get-tuple-element.227) | copy-start | bytes 13828
  183.1 36.9 %copy-start.8 = (bf16[1152,1152]{1,0:T(8,128)(2,1)S(1)}, bf16[1152,1152]{1,0:T(8,128)(2,1)}, u32[]{:S(2)}) copy-start(bf16[1152,1152]{1,0:T(8,128)(2,1)} %copy-done.7) | copy-start | bytes 7962628
  273.3 237.2 %reduce-scatter.6.cloned.1.call-start = ((), (), s32[]{:S(2)}) async-start(), calls=%async_computation.11 | async-start | bytes 11943936 | tf_op jit(solution)/shard_map/reduce_scatter | solution.py:890
  355.1 199.5 %reduce-scatter.8.cloned.1.call-start = ((), (), s32[]{:S(2)}) async-start(), calls=%async_computation.12 | async-start | bytes 2985984 | tf_op jit(solution)/shard_map/reduce_scatter | solution.py:902
  415.5 56.5 %copy-start.1 = (bf16[1024,1152]{1,0:T(8,128)(2,1)S(1)}, bf16[1024,1152]{1,0:T(8,128)(2,1)}, u32[]{:S(2)}) copy-start(bf16[1024,1152]{1,0:T(8,128)(2,1)} %copy-done) | copy-start | bytes 7077892
  415.5 56.5 %copy-start.28 = (f32[1024]{0:T(1024)S(1)}, f32[1024]{0:T(1024)}, u32[]{:S(2)}) copy-start(f32[1024]{0:T(1024)} %copy-done.27) | copy-start | bytes 12292
  415.5 56.5 %copy-start.30 = (f32[1152]{0:T(1024)S(1)}, f32[1152]{0:T(1024)}, u32[]{:S(2)}) copy-start(f32[1152]{0:T(1024)} %copy-done.29) | copy-start | bytes 13828
  415.5 56.5 %copy-start.33 = (f32[1024]{0:T(1024)S(1)}, f32[1024]{0:T(1024)}, u32[]{:S(2)}) copy-start(f32[1024]{0:T(1024)} %copy-done.32) | copy-start | bytes 12292
  415.6 56.5 %copy-start.38 = (f32[1152]{0:T(1024)S(1)}, f32[1152]{0:T(1024)}, u32[]{:S(2)}) copy-start(f32[1152]{0:T(1024)} %copy-done.37) | copy-start | bytes 13828
  472.0 30.0 %slice-start = ((s8[4718592]{0:T(1024)(128)(4,1)}), s8[4194304]{0:T(1024)(128)(4,1)S(1)}, s32[]{:S(2)}) async-start(s8[4718592]{0:T(1024)(128)(4,1)} %bitcast.85), calls=%async_computation.13 | async-start | bytes 8388608
  472.0 30.0 %slice-start.2 = ((s8[4718592]{0:T(1024)(128)(4,1)}), s8[4194304]{0:T(1024)(128)(4,1)S(1)}, s32[]{:S(2)}) async-start(s8[4718592]{0:T(1024)(128)(4,1)} %bitcast.87), calls=%async_computation.15 | async-start | bytes 8388608
  510.5 44.1 %copy-start.3 = (bf16[576,1152]{1,0:T(8,128)(2,1)S(1)}, bf16[576,1152]{1,0:T(8,128)(2,1)}, u32[]{:S(2)}) copy-start(bf16[576,1152]{1,0:T(8,128)(2,1)} %reduce-scatter.6.cloned.1.call-done.up_ref) | copy-start | bytes 3981316
  527.3 175.0 %all-to-all-start.1 = ((bf16[4,1,256,1152]{3,2,1,0:T(8,128)(2,1)}), bf16[4,1,256,1152]{3,2,1,0:T(8,128)(2,1)}, u32[]{:S(2)}, u32[]{:S(2)}) async-start(bf16[4,1,256,1152]{3,2,1,0:T(8,128)(2,1)} %bitcast.89), calls=%async_computation.1 | async-start | bytes 4718592 | tf_op jit(solution)/shard_map/all_to_all | solution.py:748
  555.6 163.5 %copy-start.19 = (f32[288,144]{0,1:T(8,128)S(1)}, f32[288,144]{0,1:T(8,128)}, u32[]{:S(2)}) copy-start(f32[288,144]{0,1:T(8,128)} %param.28) | copy-start | bytes 497668
  703.0 23.5 %all-to-all-start.4 = ((f32[32,1,128]{2,1,0:T(1,128)}), f32[32,1,128]{2,1,0:T(1,128)S(1)}, u32[]{:S(2)}, u32[]{:S(2)}) async-start(f32[32,1,128]{2,1,0:T(1,128)} %broadcast_in_dim.18), calls=%async_computation.7 | async-start | bytes 32768 | tf_op jit(solution)/shard_map/all_to_all | solution.py:758
  (32 other events, 282.8 us)
Sparse Core Ops, SparseCore 0:
  132.3 68.1 all-gather.3
  202.4 63.7 all-gather.5
  273.4 81.6 reduce-scatter.3
  358.5 82.2 reduce-scatter.5
  510.6 43.9 reduce-scatter.7

commit v5 on v4

--- a/solution.py
+++ b/solution.py
@@ -54,6 +54,14 @@
 WINDOW = 256
 CONTRACT_LAST = (((1,), (1,)), ((), ()))
 LOG2_E = 1.4426950408889634
+
+
+FORWARD_US, BACKWARD_US, START_US, TAIL_US = 37, 57, 115, 110
+
+
+def expected(microseconds):
+    moved = int(microseconds * 3.2e6)
+    return pl.CostEstimate(flops=0, bytes_accessed=moved, transcendentals=0)
 
 
 def head_window(head, features):
@@ -127,8 +135,52 @@
             pltpu.VMEM((features, length), jnp.float32),
             pltpu.VMEM((features, rows), jnp.float32),
         ],
+        cost_estimate=expected(FORWARD_US),
         compiler_params=pltpu.CompilerParams(vmem_limit_bytes=56 * 2**20),
     )(query, keyval, key_bias)
+
+
+MESH = pl.DeviceIdType.MESH
+
+
+def exchange_rows(rows_ref, back_ref, send, recv, local_sem, *, bands):
+    band = lax.axis_index("band")
+    block = back_ref.shape[1]
+    barrier = pltpu.get_barrier_semaphore()
+    for step in range(1, bands):
+        pl.semaphore_signal(
+            barrier, inc=1, device_id={"band": lax.rem(band + step, bands)}, device_id_type=MESH
+        )
+    pl.semaphore_wait(barrier, bands - 1)
+
+    def span(owner):
+        return rows_ref.at[pl.ds(pl.multiple_of(owner * block, 16), block), :]
+
+    def sent(step):
+        target = lax.rem(band + step, bands)
+        return pltpu.make_async_remote_copy(
+            src_ref=span(target), dst_ref=back_ref.at[band],
+            send_sem=send.at[step], recv_sem=recv.at[step],
+            device_id={"band": target}, device_id_type=MESH,
+        )
+
+    keep = pltpu.make_async_copy(span(band), back_ref.at[band], local_sem)
+    keep.start()
+    for step in range(1, bands):
+        sent(step).start()
+
+    def finish():
+        keep.wait()
+        for step in range(1, bands):
+            sent(step).wait_send()
+            source = lax.rem(band + bands - step, bands)
+            pltpu.make_async_remote_copy(
+                src_ref=back_ref.at[source], dst_ref=back_ref.at[source],
+                send_sem=send.at[step], recv_sem=recv.at[step],
+                device_id={"band": source}, device_id_type=MESH,
+            ).wait_recv()
+
+    return finish
 
 
 def attention_backward_kernel(
@@ -191,9 +243,11 @@
         out_ref[:, columns] = wide_t[columns, :].T.astype(jnp.bfloat16)
 
 
-def attention_backward(query, keyval, key_bias, mixed, grad, log_total, features, block):
+def attention_backward(
+    query, keyval, key_bias, mixed, grad, log_total, features, block, exchanged, known, bands
+):
     rows, length = query.shape[0], keyval.shape[0]
-    shared = query is keyval
+    shared = exchanged is not None
     scratch = [
         pltpu.VMEM((rows, features), jnp.bfloat16),
         pltpu.VMEM((features, length), jnp.float32),
@@ -202,18 +256,36 @@
     params = pltpu.CompilerParams(vmem_limit_bytes=56 * 2**20)
     if shared:
 
-        def shared_kernel(both_ref, bias_ref, mixed_ref, grad_ref, log_ref, out_ref, *held):
+        def shared_kernel(both_ref, bias_ref, mixed_ref, grad_ref, log_ref, rows_ref, known_ref, out_ref, back_ref, kept_ref, *held):
+            kept_ref[...] = known_ref[...]
+            finish = exchange_rows(rows_ref, back_ref, *held[3:], bands=bands)
             attention_backward_kernel(
-                both_ref, both_ref, bias_ref, mixed_ref, grad_ref, log_ref, out_ref, out_ref, *held,
+                both_ref, both_ref, bias_ref, mixed_ref, grad_ref, log_ref, out_ref, out_ref, *held[:3],
                 features=features, shift=features, out_shift=features, block=block,
             )
-
+            finish()
+
+        anywhere, vmem = pl.BlockSpec(memory_space=pl.ANY), pl.BlockSpec(memory_space=pltpu.VMEM)
         return pl.pallas_call(
             shared_kernel,
-            out_shape=jax.ShapeDtypeStruct((rows, 3 * features), jnp.bfloat16),
-            scratch_shapes=scratch,
-            compiler_params=params,
-        )(query, key_bias, mixed, grad, log_total)
+            out_shape=(
+                jax.ShapeDtypeStruct((rows, 3 * features), jnp.bfloat16),
+                jax.ShapeDtypeStruct((bands, rows // bands, features), jnp.bfloat16),
+                jax.ShapeDtypeStruct(known.shape, jnp.float32),
+            ),
+            in_specs=[vmem] * 5 + [anywhere, vmem],
+            out_specs=(vmem, anywhere, vmem),
+            scratch_shapes=scratch
+            + [
+                pltpu.SemaphoreType.DMA((bands,)),
+                pltpu.SemaphoreType.DMA((bands,)),
+                pltpu.SemaphoreType.DMA(()),
+            ],
+            cost_estimate=expected(BACKWARD_US),
+            compiler_params=pltpu.CompilerParams(
+                collective_id=2, has_side_effects=True, vmem_limit_bytes=56 * 2**20
+            ),
+        )(query, key_bias, mixed, grad, log_total, exchanged, known)
     return pl.pallas_call(
         functools.partial(
             attention_backward_kernel, features=features, shift=0, out_shift=0, block=block
@@ -225,9 +297,6 @@
         scratch_shapes=scratch,
         compiler_params=params,
     )(query, keyval, key_bias, mixed, grad, log_total)
-
-
-MESH = pl.DeviceIdType.MESH
 
 
 def flip(index, bit):
@@ -442,6 +511,7 @@
             pltpu.SemaphoreType.DMA((16,)),
             pltpu.SemaphoreType.DMA((3,)),
         ],
+        cost_estimate=expected(START_US),
         compiler_params=pltpu.CompilerParams(
             collective_id=0, has_side_effects=True, vmem_limit_bytes=40 * 2**20
         ),
@@ -453,45 +523,50 @@
 
 
 def tail_kernel(
-    qkv_ref, out_ref, up_ref, down_ref, rows_ref,
-    wide_ref, tall_ref, back_ref,
-    own, from_core, first_x, first_y, last_x, last_y, turned, held, tall, held_in, tall_in,
+    qkv_ref, out_ref, up_ref, rows_ref, pieces_ref, silu_ref, known_ref,
+    wide_ref, back_ref, ada_ref, bias_ref, squares_ref,
+    pieces, terms, square_flat, square_line, small_send, small_recv,
+    own, from_core, first_x, first_y, last_x, last_y, turned, held, held_in,
     core_send, core_recv, flat_send, flat_recv, line_send, line_recv, row_send, row_recv, local_sem,
-    *, bands, early,
+    *, imgs, bands,
 ):
     img, band = lax.axis_index("img"), lax.axis_index("band")
-    qkv_part, out_part = own.shape[1], out_ref.shape[0]
-    width = turned.shape[0]
-    depth, tall_width = wide_ref.shape[0], tall_ref.shape[1]
+    qkv_part, out_part = qkv_ref.shape[0] // imgs, out_ref.shape[0] // imgs
+    both = own.shape[1]
+    depth, width = wide_ref.shape
     row_block = back_ref.shape[1]
     half = first_x.shape[1]
     lanes = 128
-    first = -(-(qkv_part + out_part) // lanes) * lanes
     beside_x, beside_y, sibling = flip(img, 2), flip(img, 4), flip(img, 1)
     chips = (img, beside_x, beside_y, flip(beside_x, 4))
-    upper, lower = pl.ds(0, half), pl.ds(half, qkv_part - half)
+    upper, lower = pl.ds(0, half), pl.ds(half, both - half)
+    spans = (pl.ds(0, qkv_part), pl.ds(qkv_part, out_part))
 
     barrier = pltpu.get_barrier_semaphore()
-    for other in (beside_x, beside_y, sibling):
+    for step in range(1, imgs):
+        other = lax.rem(img + step, imgs)
         pl.semaphore_signal(barrier, inc=1, device_id={"img": other}, device_id_type=MESH)
     for step in range(1, bands):
         pl.semaphore_signal(
             barrier, inc=1, device_id={"band": lax.rem(band + step, bands)}, device_id_type=MESH
         )
-    pl.semaphore_wait(barrier, 3 + bands - 1)
-
-    def qkv_rows(owner):
-        return qkv_ref.at[pl.ds(pl.multiple_of(owner * qkv_part, 16), qkv_part), :]
-
-    def core_copy(at):
+    pl.semaphore_wait(barrier, imgs + bands - 2)
+
+    def grad_rows(kind, owner):
+        source, count = ((qkv_ref, qkv_part), (out_ref, out_part))[kind]
+        return source.at[pl.ds(pl.multiple_of(owner * count, 16), count), :]
+
+    def core_copy(kind, at):
         return pltpu.make_async_remote_copy(
-            src_ref=qkv_rows(flip(chips[at], 1)), dst_ref=from_core.at[at],
-            send_sem=core_send.at[at], recv_sem=core_recv.at[at],
+            src_ref=grad_rows(kind, flip(chips[at], 1)), dst_ref=from_core.at[at, spans[kind]],
+            send_sem=core_send.at[kind, at], recv_sem=core_recv.at[kind, at],
             device_id={"img": sibling}, device_id_type=MESH,
         )
 
-    def own_copy(at):
-        return pltpu.make_async_copy(qkv_rows(chips[at]), own.at[at], local_sem.at[at])
+    def own_copy(kind, at):
+        return pltpu.make_async_copy(
+            grad_rows(kind, chips[at]), own.at[at, spans[kind]], local_sem.at[4 * kind + at]
+        )
 
     plan = (
         (own.at[1, upper], first_x.at[0], beside_x),
@@ -528,13 +603,12 @@
             device_id={"band": source}, device_id_type=MESH,
         )
 
+    first = -(-both // lanes) * lanes
+    parts = (pl.ds(0, first), pl.ds(first, width - first))
+
     def piece(part, owner, way=None):
-        if part == 2:
-            span = pl.ds(pl.multiple_of(owner * tall_width, lanes), tall_width)
-            return tall.at[:, span] if way is None else tall_in.at[way, :, span]
-        span = pl.ds(0, first) if part == 0 else pl.ds(first, width - first)
         down = pl.ds(pl.multiple_of(owner * depth, 16), depth)
-        return held.at[down, span] if way is None else held_in.at[way, down, span]
+        return held.at[down, parts[part]] if way is None else held_in.at[way, down, parts[part]]
 
     def line_copy(part, way, owner, toward):
         return pltpu.make_async_remote_copy(
@@ -565,15 +639,15 @@
                 mine[...] = add_low(mine[...], piece(part, owner, way)[...])
                 copy.start()
 
-    def line_finish(part, target, span):
-        total = piece(part, band)[...].astype(jnp.float32)
-        target[:, span] = total
+    def line_finish(part):
+        span = parts[part]
+        wide_ref[:, span] = piece(part, band)[...].astype(jnp.float32)
         for way, sign in ((0, 1), (1, -1)):
 
             @pl.when((band - sign >= 0) & (band - sign < bands))
             def _():
                 line_copy(part, way, band, band - sign).wait_recv()
-                target[:, span] += piece(part, band, way)[...].astype(jnp.float32)
+                wide_ref[:, span] += piece(part, band, way)[...].astype(jnp.float32)
 
     def line_sent(part):
         for way, sign in ((0, 1), (1, -1)):
@@ -587,24 +661,60 @@
         span = pl.ds(pl.multiple_of(tile * lanes, lanes), lanes)
         held[:, span] = turned[span, :].astype(jnp.float32).T.astype(jnp.bfloat16)
 
+    def small_copy(source, target, kind, step, axis, toward):
+        return pltpu.make_async_remote_copy(
+            src_ref=source, dst_ref=target,
+            send_sem=small_send.at[kind, step], recv_sem=small_recv.at[kind, step],
+            device_id={axis: toward}, device_id_type=MESH,
+        )
+
+    def piece_flat(step):
+        other = lax.rem(img + step, imgs)
+        return small_copy(pieces_ref.at[other], pieces.at[band, img], 0, step, "img", other)
+
+    def piece_line(step):
+        other = lax.rem(band + step, bands)
+        return small_copy(pieces.at[band], pieces.at[band], 1, step, "band", other)
+
+    def square_one(step):
+        other = lax.rem(img + step, imgs)
+        return small_copy(square_flat.at[img], square_flat.at[img], 2, step, "img", other)
+
+    def square_two(step):
+        other = lax.rem(band + step, bands)
+        return small_copy(square_line.at[band], square_line.at[band], 3, step, "band", other)
+
+    def arrival(view, kind, step, axis):
+        me, count = (img, imgs) if axis == "img" else (band, bands)
+        small_copy(view, view, kind, step, axis, lax.rem(me + count - step, count)).wait_recv()
+
     order = (3, 1, 2, 0)
+    for step in range(1, imgs):
+        piece_flat(step).start()
+    keep_piece = pltpu.make_async_copy(pieces_ref.at[img], pieces.at[band, img], local_sem.at[9])
+    keep_piece.start()
     for at in order:
-        core_copy(at).start()
+        core_copy(0, at).start()
+        core_copy(1, at).start()
     for at in order:
-        own_copy(at).start()
-    turned[pl.ds(qkv_part, out_part), :] = out_ref[...]
-    turned[pl.ds(qkv_part + out_part, width - qkv_part - out_part), :] = up_ref[...]
+        own_copy(0, at).start()
+        own_copy(1, at).start()
+    keep = pltpu.make_async_copy(rows_ref.at[row_span(band), :], back_ref.at[band], local_sem.at[8])
+    keep.start()
+    turned[pl.ds(both, width - both), :] = up_ref[...]
     pl.loop(first // lanes, width // lanes)(turn)
-    tall[...] = down_ref[...]
     line_ends(1)
-    line_ends(2)
-    keep = pltpu.make_async_copy(rows_ref.at[row_span(band), :], back_ref.at[band], local_sem.at[4])
-    keep.start()
+    keep_piece.wait()
+    for step in range(1, imgs):
+        arrival(pieces.at[band, lax.rem(img + imgs - step, imgs)], 0, step, "img")
+    for step in range(1, bands):
+        piece_line(step).start()
     for step in range(1, bands):
         row_copy(step).start()
     for at in order:
-        own_copy(at).wait()
-        core_copy(at).wait_recv()
+        for kind in range(2):
+            own_copy(kind, at).wait()
+            core_copy(kind, at).wait_recv()
         own[at] = add_low(own[at], from_core[at])
         for ready in {3: (1, 3), 1: (0,), 2: (2,), 0: ()}[at]:
             flat_copy(ready).start()
@@ -614,8 +724,7 @@
     flat_copy(3).wait_recv()
     own[1, lower] = add_low(own[1, lower], first_y[1])
     flat_copy(5).start()
-    for part in early:
-        line_round(part, 0)
+    line_round(1, 0)
     flat_copy(0).wait_recv()
     flat_copy(2).wait_recv()
     flat_copy(4).wait_recv()
@@ -632,17 +741,60 @@
     ).astype(jnp.bfloat16)
     pl.loop(0, first // lanes)(turn)
     line_ends(0)
+    for step in range(1, bands):
+        arrival(pieces.at[lax.rem(band + bands - step, bands)], 1, step, "band")
+    for image in range(imgs):
+        for at in range(bands):
+            terms[pl.ds(image * bands + at, 1), :] = pieces[at, image]
+    columns = ada_ref.shape[1]
+    ada = lax.dot_general(
+        silu_ref[...], terms[:, pl.ds(0, columns)], (((1,), (0,)), ((), ())),
+        precision=lax.Precision.HIGHEST, preferred_element_type=jnp.float32,
+    )
+    ada_ref[...] = ada
+    bias_rows, bias_columns = bias_ref.shape
+    bias = jnp.sum(terms[:, pl.ds(columns, bias_rows * bias_columns)], axis=0, keepdims=True)
+    for at in range(bias_rows):
+        bias_ref[pl.ds(at, 1), :] = bias[:, at * bias_columns : (at + 1) * bias_columns]
+    squares = jnp.sum(ada * ada, axis=0, keepdims=True)
+    squares = jnp.sum(squares, axis=1, keepdims=True)
+    squares += jnp.sum(bias * bias, axis=1, keepdims=True) / bands
     for step in range(bands - 1):
-        for part in (1, 2, 0):
-            if step > 0 or part not in early:
-                line_round(part, step)
-    line_finish(1, wide_ref, pl.ds(first, width - first))
-    line_finish(2, tall_ref, pl.ds(0, tall_width))
-    line_finish(0, wide_ref, pl.ds(0, first))
-    for part in range(3):
-        line_sent(part)
+        line_round(0, step)
+        if step > 0:
+            line_round(1, step)
+    line_finish(1)
+    line_finish(0)
+    rows = jnp.sum(wide_ref[...] * wide_ref[...], axis=0, keepdims=True)
+    squares += jnp.sum(rows, axis=1, keepdims=True) + known_ref[0:1, 0:1]
+    square_flat[img] = jnp.broadcast_to(squares, square_flat.shape[1:])
+    for step in range(1, imgs):
+        square_one(step).start()
+    for step in range(1, imgs):
+        arrival(square_flat.at[lax.rem(img + imgs - step, imgs)], 2, step, "img")
+    total = square_flat[0]
+    for at in range(1, imgs):
+        total += square_flat[at]
+    square_line[band] = total
+    for step in range(1, bands):
+        square_two(step).start()
+    for step in range(1, bands):
+        arrival(square_line.at[lax.rem(band + bands - step, bands)], 3, step, "band")
+    total = square_line[0]
+    for at in range(1, bands):
+        total += square_line[at]
+    squares_ref[...] = total
+    line_sent(0)
+    line_sent(1)
+    for step in range(1, imgs):
+        piece_flat(step).wait_send()
+        square_one(step).wait_send()
+    for step in range(1, bands):
+        piece_line(step).wait_send()
+        square_two(step).wait_send()
     for at in range(4):
-        core_copy(at).wait_send()
+        core_copy(0, at).wait_send()
+        core_copy(1, at).wait_send()
     for at in range(6):
         flat_copy(at).wait_send()
     for step in range(1, bands):
@@ -651,49 +803,108 @@
     keep.wait()
 
 
-def tail_exchange(qkv_grad, out_sum, up_sum, down_sum, rows, bands, imgs):
+def tail_exchange(qkv_grad, out_grad, up_sum, rows, pieces, silu, known, bias_shape, bands, imgs):
     low = jnp.bfloat16
-    qkv_part, features = qkv_grad.shape[0] // imgs, qkv_grad.shape[1]
-    out_part, up_part = out_sum.shape[0], up_sum.shape[0]
-    width = qkv_part + out_part + up_part
-    tall_rows, tall_width = down_sum.shape[0], down_sum.shape[1] // bands
-    half = -(-qkv_part // 32) * 16
+    features = qkv_grad.shape[1]
+    both = (qkv_grad.shape[0] + out_grad.shape[0]) // imgs
+    width = both + up_sum.shape[0]
+    half = -(-both // 32) * 16
+    ada_columns = pieces.shape[2] - bias_shape[0] * bias_shape[1]
     anywhere, vmem = pl.BlockSpec(memory_space=pl.ANY), pl.BlockSpec(memory_space=pltpu.VMEM)
     return pl.pallas_call(
-        functools.partial(tail_kernel, bands=bands, early=(1, 2)),
+        functools.partial(tail_kernel, imgs=imgs, bands=bands),
         out_shape=(
             jax.ShapeDtypeStruct((features // bands, width), jnp.float32),
-            jax.ShapeDtypeStruct((tall_rows, tall_width), jnp.float32),
             jax.ShapeDtypeStruct((bands, rows.shape[0] // bands, features), low),
+            jax.ShapeDtypeStruct((silu.shape[0], ada_columns), jnp.float32),
+            jax.ShapeDtypeStruct(bias_shape, jnp.float32),
+            jax.ShapeDtypeStruct((8, 128), jnp.float32),
         ),
-        in_specs=[anywhere, vmem, vmem, vmem, anywhere],
-        out_specs=(vmem, vmem, anywhere),
+        in_specs=[anywhere, anywhere, vmem, anywhere, vmem, vmem, vmem],
+        out_specs=(vmem, anywhere, vmem, vmem, vmem),
         scratch_shapes=[
-            pltpu.VMEM((4, qkv_part, features), low),
-            pltpu.VMEM((4, qkv_part, features), low),
+            pltpu.VMEM((bands,) + pieces.shape, jnp.float32),
+            pltpu.VMEM((bands * imgs, pieces.shape[2]), jnp.float32),
+            pltpu.VMEM((imgs, 8, 128), jnp.float32),
+            pltpu.VMEM((bands, 8, 128), jnp.float32),
+            pltpu.SemaphoreType.DMA((4, imgs)),
+            pltpu.SemaphoreType.DMA((4, imgs)),
+            pltpu.VMEM((4, both, features), low),
+            pltpu.VMEM((4, both, features), low),
             pltpu.VMEM((2, half, features), low),
-            pltpu.VMEM((2, qkv_part - half, features), low),
-            pltpu.VMEM((qkv_part - half, features), low),
+            pltpu.VMEM((2, both - half, features), low),
+            pltpu.VMEM((both - half, features), low),
             pltpu.VMEM((half, features), low),
             pltpu.VMEM((width, features), low),
             pltpu.VMEM((features, width), low),
-            pltpu.VMEM((tall_rows, tall_width * bands), low),
             pltpu.VMEM((2, features, width), low),
-            pltpu.VMEM((2, tall_rows, tall_width * bands), low),
-            pltpu.SemaphoreType.DMA((4,)),
-            pltpu.SemaphoreType.DMA((4,)),
+            pltpu.SemaphoreType.DMA((2, 4)),
+            pltpu.SemaphoreType.DMA((2, 4)),
             pltpu.SemaphoreType.DMA((6,)),
             pltpu.SemaphoreType.DMA((6,)),
-            pltpu.SemaphoreType.DMA((3, 2, bands)),
-            pltpu.SemaphoreType.DMA((3, 2, bands)),
+            pltpu.SemaphoreType.DMA((2, 2, bands)),
+            pltpu.SemaphoreType.DMA((2, 2, bands)),
             pltpu.SemaphoreType.DMA((bands - 1,)),
             pltpu.SemaphoreType.DMA((bands - 1,)),
-            pltpu.SemaphoreType.DMA((5,)),
+            pltpu.SemaphoreType.DMA((10,)),
         ],
+        cost_estimate=expected(TAIL_US),
         compiler_params=pltpu.CompilerParams(
             collective_id=1, has_side_effects=True, vmem_limit_bytes=50 * 2**20
         ),
-    )(qkv_grad, out_sum, up_sum, down_sum, rows)
+    )(qkv_grad, out_grad, up_sum, rows, pieces, silu, known)
+
+
+def adam_kernel(*refs):
+    squares_ref, wide_ref, tall_ref, ada_ref, bias_ref = refs[:5]
+    sources, results = refs[5:23], refs[23:]
+    norm = jnp.sqrt(squares_ref[0:1, 0:1])
+    factor = clip_norm / jnp.maximum(norm, clip_norm)
+    qkv_part = sources[3].shape[1]
+    both = qkv_part + sources[6].shape[1]
+    rates = (learn_rate, learn_rate, out_rate, learn_rate, learn_rate, bias_rate)
+
+    def update(which, rows, gradient):
+        weight_ref, first_ref, second_ref = sources[3 * which : 3 * which + 3]
+        new = adam_update(
+            weight_ref[rows, :], first_ref[rows, :], second_ref[rows, :], gradient, factor, rates[which]
+        )
+        for into, value in zip(results[3 * which : 3 * which + 3], new):
+            into[rows, :] = value
+
+    depth = wide_ref.shape[0]
+    block = next(rows for rows in (32, 16, 8) if depth % rows == 0)
+
+    @pl.loop(0, depth // block)
+    def _(step):
+        rows = pl.ds(pl.multiple_of(step * block, block), block)
+        update(0, rows, ada_ref[rows, :])
+        update(1, rows, wide_ref[rows, :qkv_part])
+        update(2, rows, wide_ref[rows, qkv_part:both])
+        update(3, rows, wide_ref[rows, both:])
+
+    tall_width = sources[12].shape[0]
+    whole = tall_width // 128 * 128
+
+    @pl.loop(0, tall_width // 128)
+    def _(step):
+        rows = pl.ds(pl.multiple_of(step * 128, 128), 128)
+        update(4, rows, tall_ref[:, rows].T)
+
+    if whole < tall_width:
+        update(4, pl.ds(whole, tall_width - whole), tall_ref[:, whole:].T)
+    update(5, slice(None), bias_ref[...])
+    results[18][...] = bias_ref[pl.ds(13, 1), :] * factor
+
+
+def adam_all(squares, wide, tall, ada, bias, groups):
+    flat = [array for group in groups for array in group]
+    return pl.pallas_call(
+        adam_kernel,
+        out_shape=[jax.ShapeDtypeStruct(array.shape, jnp.float32) for array in flat]
+        + [jax.ShapeDtypeStruct((1, bias.shape[1]), jnp.float32)],
+        compiler_params=pltpu.CompilerParams(vmem_limit_bytes=50 * 2**20),
+    )(squares, wide, tall, ada, bias, *flat)
 
 
 def body(
@@ -870,7 +1081,7 @@
         jnp.einsum("irf,df->ird", hidden_low, down_full, preferred_element_type=jnp.float32)
         + bias_vals[13]
     )
-    output = to_bands((middle + gate_two * branch).astype(jnp.bfloat16))
+    output_low = (middle + gate_two * branch).astype(jnp.bfloat16)
     branch_grad = (gate_two * grad_out).astype(jnp.bfloat16)
     gate_two_grad = jnp.sum(grad_out * branch, axis=1)
     down_grad = jnp.einsum(
@@ -887,7 +1098,7 @@
     up_grad = jnp.einsum(
         "irf,ird->fd", pre_grad, second_in, preferred_element_type=jnp.float32
     ).astype(low_type)
-    up_sum = lax.psum_scatter(after(up_grad, down_sum), "img", scatter_dimension=0, tiled=True)
+    up_sum = lax.psum_scatter(up_grad, "img", scatter_dimension=0, tiled=True)
     second_grad = jnp.einsum("irf,fd->ird", after(pre_grad, up_grad), up_full, preferred_element_type=jnp.float32)
     shift_two_grad = jnp.sum(second_grad, axis=1)
     scale_two_grad = jnp.sum(second_grad * normed_two, axis=1)
@@ -899,17 +1110,27 @@
     out_grad = jnp.einsum(
         "ire,ird->ed", attended_grad, mixed, preferred_element_type=jnp.float32
     ).astype(low_type)
-    out_sum = lax.psum_scatter(after(out_grad, up_sum), "img", scatter_dimension=0, tiled=True)
     mixed_grad = jnp.einsum(
         "ire,ed->ird", after(attended_grad, out_grad), out_full, preferred_element_type=jnp.float32
     ).astype(jnp.bfloat16)
+    tall_cut = down_sum.reshape(down_sum.shape[0], band_count, -1).transpose(1, 0, 2)
+    tall_shard = jnp.sum(
+        lax.all_to_all(tall_cut, "band", split_axis=0, concat_axis=0, tiled=True).astype(jnp.float32),
+        axis=0,
+    )
+    hosted = img_count == 8 and own == 1 and split == 1
+    tall_squares = jnp.broadcast_to(jnp.sum(tall_shard * tall_shard), (8, 128))
     attention_grads = [
         attention_backward(
             queries[i], keys_values[i], key_bias[i], mixed_parts[i], mixed_grad[i], log_total[i],
-            features, 512,
+            features, 512, output_low[i] if hosted else None, tall_squares, band_count,
         )
         for i in range(own)
     ]
+    if hosted:
+        output, tall_squares = attention_grads[0][1:]
+    else:
+        output = to_bands(output_low)
     if split > 1:
         shared_grads = lax.psum_scatter(
             jnp.stack([pair[1] for pair in attention_grads]),
@@ -921,8 +1142,10 @@
         qkv_grad = jnp.concatenate(
             [jnp.stack([pair[0] for pair in attention_grads]), shared_grads], axis=-1
         )
+    elif hosted:
+        qkv_grad = attention_grads[0][0][None]
     else:
-        qkv_grad = jnp.stack(attention_grads)
+        qkv_grad = jnp.stack([jnp.concatenate(pair, axis=-1) for pair in attention_grads])
     qkv_sums = jnp.sum(qkv_grad.astype(jnp.float32), axis=(0, 1))
     qkv_weight_grad = jnp.einsum(
         "ire,ird->ed", qkv_grad, first_in, preferred_element_type=jnp.float32
@@ -966,30 +1189,36 @@
         ],
         axis=1,
     )
-    sent = jnp.broadcast_to(pieces[:, None], (img_count, band_count, pieces.shape[1])).reshape(
-        img_count * band_count, -1
-    )
-    got = lax.all_to_all(sent, ("img", "band"), split_axis=0, concat_axis=0, tiled=True)
-    mod_columns = got[:, : own * ada_columns].reshape(-1, ada_columns)
     silu_terms = jnp.tile(
         silu_rows.astype(jnp.float32).reshape(img_count, 1, images, ada_rows), (1, split, 1, 1)
     ).reshape(img_count * band_count * own, ada_rows)
-    ada_shard = jnp.einsum(
-        "id,ie->de",
-        silu_terms,
-        mod_columns,
-        precision=lax.Precision.HIGHEST,
-    )
-    bias_total = jnp.sum(got[:, own * ada_columns :], axis=0).reshape(bias_rows, bias_columns)
     if img_count == 8 and own == 1 and split == 1:
-        wide_shard, tall_shard, input_grad_low = tail_exchange(
-            qkv_weight_grad, out_sum, up_sum, down_sum, input_grad_low[0], band_count, img_count
+        wide_shard, input_grad_low, ada_shard, bias_total, squares_total = tail_exchange(
+            qkv_weight_grad,
+            out_grad,
+            up_sum,
+            input_grad_low[0],
+            pieces[:, None],
+            silu_terms.T,
+            tall_squares,
+            biases.shape,
+            band_count,
+            img_count,
         )
     else:
+        sent = jnp.broadcast_to(
+            pieces[:, None], (img_count, band_count, pieces.shape[1])
+        ).reshape(img_count * band_count, -1)
+        got = lax.all_to_all(sent, ("img", "band"), split_axis=0, concat_axis=0, tiled=True)
+        ada_shard = jnp.einsum(
+            "id,ie->de",
+            silu_terms,
+            got[:, : own * ada_columns].reshape(-1, ada_columns),
+            precision=lax.Precision.HIGHEST,
+        )
+        bias_total = jnp.sum(got[:, own * ada_columns :], axis=0).reshape(bias_rows, bias_columns)
         qkv_sum = lax.psum_scatter(qkv_weight_grad, "img", scatter_dimension=0, tiled=True)
-        tall_shard = lax.psum_scatter(down_sum, "band", scatter_dimension=1, tiled=True).astype(
-            jnp.float32
-        )
+        out_sum = lax.psum_scatter(out_grad, "img", scatter_dimension=0, tiled=True)
         wide_shard = lax.psum_scatter(
             jnp.concatenate([qkv_sum, out_sum, up_sum], axis=0).T,
             "band",
@@ -997,37 +1226,28 @@
             tiled=True,
         ).astype(jnp.float32)
         input_grad_low = to_bands(input_grad_low)
+        squares = tall_squares[0, 0] + jnp.sum(bias_total * bias_total) / band_count
+        for shard_grad in (ada_shard, wide_shard):
+            squares = squares + jnp.sum(shard_grad * shard_grad)
+        squares_total = jnp.broadcast_to(sum_everywhere(squares), (8, 128))
     input_grad = input_grad_low.astype(jnp.float32)
-    down_shard = tall_shard.T
-    qkv_shard = wide_shard[:, :qkv_part]
-    out_shard = wide_shard[:, qkv_part : qkv_part + out_part]
-    up_shard = wide_shard[:, qkv_part + out_part :]
-    shards = (ada_shard, qkv_shard, out_shard, up_shard, down_shard)
-    squares = jnp.sum(bias_total * bias_total) / band_count
-    for shard_grad in shards:
-        squares = squares + jnp.sum(shard_grad * shard_grad)
-    squares_total = sum_everywhere(squares)
-    grad_norm = jnp.sqrt(squares_total)
-    factor = clip_norm / jnp.maximum(grad_norm, clip_norm)
-    ada_new, ada_first_new, ada_second_new = adam_update(
-        ada_weight, ada_first, ada_second, shards[0], factor, learn_rate
-    )
-    qkv_new, qkv_first_new, qkv_second_new = adam_update(
-        qkv_weight, qkv_first, qkv_second, shards[1], factor, learn_rate
-    )
-    out_new, out_first_new, out_second_new = adam_update(
-        out_weight, out_first, out_second, shards[2], factor, out_rate
-    )
-    up_new, up_first_new, up_second_new = adam_update(
-        up_weight, up_first, up_second, shards[3], factor, learn_rate
-    )
-    down_new, down_first_new, down_second_new = adam_update(
-        down_weight, down_first, down_second, shards[4], factor, learn_rate
-    )
-    bias_new, bias_first_new, bias_second_new = adam_update(
-        biases, bias_first, bias_second, bias_total, factor, bias_rate
-    )
-    branch_bias_grad = bias_total[13] * factor
+    grad_norm = jnp.sqrt(squares_total[0, 0])
+    groups = (
+        (ada_weight, ada_first, ada_second),
+        (qkv_weight, qkv_first, qkv_second),
+        (out_weight, out_first, out_second),
+        (up_weight, up_first, up_second),
+        (down_weight, down_first, down_second),
+        (biases, bias_first, bias_second),
+    )
+    updated = adam_all(squares_total, wide_shard, tall_shard, ada_shard, bias_total, groups)
+    ada_new, ada_first_new, ada_second_new = updated[0:3]
+    qkv_new, qkv_first_new, qkv_second_new = updated[3:6]
+    out_new, out_first_new, out_second_new = updated[6:9]
+    up_new, up_first_new, up_second_new = updated[9:12]
+    down_new, down_first_new, down_second_new = updated[12:15]
+    bias_new, bias_first_new, bias_second_new = updated[15:18]
+    branch_bias_grad = updated[18][0]
     return (
         output,
         input_grad,

time: 762 us -> 676 us (0.89)
  waiting for transfers between devices: 50.7 us -> 4.37 us
  blocking collectives: 25.5 us -> 9.32 us
  starting transfers between devices: 33.3 us -> 17.5 us
  other arithmetic: 41.6 us -> 28 us
  local copies, waits for them, and re-layouts: 30 us -> 41.4 us
    reduce_scatter x1, waiting for transfers between devices: 29.5 us -> 0.02 us  [body(): lax.psum_scatter(down_grad, 'img', scatter_dimension=0, tiled=True)]
    reduce_scatter x2 -> x1, waiting for transfers between devices: 17.4 us -> 0.02 us  [body(): up_sum = lax.psum_scatter(up_grad, 'img', scatter_dimension=0, tiled=True)]
    all_to_all x1 -> x0, blocking collectives: 16.2 us -> none  [body(): lax.all_to_all(sent, ('img', 'band'), split_axis=0, concat_axis=0, tiled=...]
    all_to_all x2 -> x1, starting transfers between devices: 21 us -> 4.9 us  [body(): lax.all_to_all(tall_cut, 'band', split_axis=0, concat_axis=0, tiled=True)]
    sub x6 -> x0, other arithmetic: 11.2 us -> none  [adam_update(): weight - rate * first_hat / (jnp.sqrt(second_hat) + adam_eps)]
    unnamed x114 -> x122, local copies, waits for them, and re-layouts: 24 us -> 32.2 us
    pallas_call x2 -> x3, Pallas kernels: 197 us -> 197 us  [the longest x1 123 us: tail_exchange(): pl.pallas_call(functools.partial(tail_kernel, imgs=imgs, bands=bands), ou...]
  transfers between devices with their start and end apart: 9 -> 7, of which waited for: 3 -> 1; matrix products, arithmetic and copies ran while one was open for 31% -> 35% of each run, Pallas kernels for 31% -> 15%
where the time goes in v5:
time: 676 us; the launch traced here: 671 us
  Pallas kernels  348 us (51%)
  matrix products  205 us (30%)
  local copies, waits for them, and re-layouts  41.4 us (6%)
  other arithmetic  28 us (4%)
  starting transfers between devices  17.5 us (3%)
  between operations  17 us (3%)
  blocking collectives  9.32 us (1%)
    pallas_call x1, Pallas kernels, tail_exchange(): pl.pallas_call(functools.partial(tail_kernel, imgs=imgs, bands=bands), ou...  123 us
    pallas_call x1, Pallas kernels, start_exchange(): pl.pallas_call(functools.partial(start_kernel, bands=bands, qkv_part=qkv_...  115 us
    pallas_call x1, Pallas kernels, attention_backward(): pl.pallas_call(shared_kernel, out_shape=(jax.ShapeDtypeStruct((rows, 3 *...  60.8 us
    pallas_call x1, Pallas kernels, attention_forward(): pl.pallas_call(functools.partial(attention_forward_kernel, features=featu...  36.8 us
    unnamed x122, local copies, waits for them, and re-layouts  32.2 us
    dot_general x1, matrix products, body(): jnp.einsum('ird,df->irf', after(branch_grad, down_grad), down_full, prefe...  29.2 us
    dot_general x1, matrix products, body(): jnp.einsum('irf,df->ird', hidden_low, down_full, preferred_element_type=j...  27.9 us
    dot_general x1, matrix products, body(): jnp.einsum('ird,fd->irf', second_in, up_full, preferred_element_type=jnp....  22.2 us
  transfers between devices with their start and end apart: 7, of which 1 were waited for; matrix products, arithmetic and copies ran while one was open for 35% of the time, Pallas kernels for 15%

profile of v5, /device:TPU:0, one launch (start us, length us, event | category | flops | bytes accessed | tf_op | source)
XLA Modules:
  0.0 670.7 jit_solution(12321686069581755131)
XLA Ops:
  14.0 114.5 %shard_map.381 = (bf16[3456,1152]{1,0:T(8,128)(2,1)}, bf16[1152,1152]{1,0:T(8,128)(2,1)S(1)}, bf16[576,1152]{1,0:T(8,128)(2,1)S(1)}, bf16[144,4608]{1,0:T(8,128)(2,1)S(1)}, bf16[1024,1152]{1,0:T(8,128)(2,1)S(1)}) custom-call(bf16[288,1152]{1,0:T(8,128)(2,1)S(1)} %concatenate.29.wide_ref, bf16[144,1152]{1,0:T(8,128)(2,1)S(1)} %convert_bitcast_fusion.tall_ref, ...), custom_call_target="tpu_custom_call" | custom-call | bytes 368000000 | tf_op jit(solution)/shard_map/pallas_call | solution.py:492
  133.4 9.3 %all-gather = bf16[8,1,6624]{2,1,0:T(2,128)(2,1)S(1)} all-gather(bf16[1,1,6624]{2,1,0:T(2,128)(2,1)S(1)} %maximum_bitcast_fusion), channel_id=1, replica_groups=mesh['img'=8,'band'=4] {'img'}, dimensions={0}, use_global_device_ids=true | all-gather | bytes 119232 | tf_op jit(solution)/shard_map/all_gather | solution.py:975
  145.4 7.4 %all-to-all-start = ((f32[32,1,864]{2,1,0:T(1,128)}), f32[32,1,864]{2,1,0:T(1,128)S(1)}, u32[]{:S(2)}, u32[]{:S(2)}) async-start(f32[32,1,864]{2,1,0:T(1,128)} %copy.100), calls=%async_computation | async-start | bytes 229376 | tf_op jit(solution)/shard_map/all_to_all | solution.py:1018
  157.5 3.6 all-to-all-done
  161.1 4.5 all-to-all-start.1
  166.6 17.1 %add_convert_fusion.query_ref.keyval_ref.both_ref = bf16[1024,3456]{1,0:T(8,128)(2,1)} fusion(bf16[3456,1152]{1,0:T(8,128)(2,1)} %get-tuple-element.62, f32[3456]{0:T(1024)S(1)} %pad_maximum_fusion.1, bf16[1024,1152]{1,0:T(8,128)(2,1)S(1)} %get-tuple-element.61, f32[1152]{0:T(1024)S(1)} %get-tuple-element.204, f32[1152]{0:T(1024)S(1)} %get-tuple-element.205, ...), kind=kOutput, calls=%fused_computation.15 | convolution fusion | flops 8167882752 | bytes 17431040 | tf_op jit(solution)/shard_map/ird,ed->ire/dot_general | solution.py:1047
  183.7 36.8 %shard_map.382 = (bf16[1024,1152]{1,0:T(8,128)(2,1)}, f32[16,1024]{1,0:T(8,128)}) custom-call(bf16[1024,3456]{1,0:T(8,128)(2,1)} %add_convert_fusion.query_ref.keyval_ref.both_ref, bf16[1024,3456]{1,0:T(8,128)(2,1)} %add_convert_fusion.query_ref.keyval_ref.both_ref, f32[1024,1]{1,0:T(8,128)} %fusion.33.bias_ref), custom_call_target="tpu_custom_call" | custom-call | bytes 118400000 | tf_op jit(solution)/shard_map/pallas_call | solution.py:127
  220.5 7.5 %fusion.42 = (f32[1024]{0:T(1024)S(1)}, f32[1024,1152]{1,0:T(8,128)S(1)}, f32[1024,1152]{1,0:T(8,128)}) fusion(f32[1152]{0:T(1024)S(1)} %get-tuple-element.203, bf16[1024,1152]{1,0:T(8,128)(2,1)S(1)} %get-tuple-element.61, f32[1152]{0:T(1024)S(1)} %add.180, bf16[1024,1152]{1,0:T(8,128)(2,1)} %get-tuple-element.63.mixed_ref, ...), kind=kOutput, calls=%fused_computation.115 | convolution fusion | flops 2723806208 | bytes 16823296 | tf_op jit(solution)/shard_map/ird,ed->ire/dot_general | solution.py:1069
  233.2 22.2 %fusion.40 = f32[1024,4608]{1,0:T(8,128)} fusion(bf16[4608,1152]{1,0:T(8,128)(2,1)} %all-gather.4.cloned.1.call-done, f32[1024,1152]{1,0:T(8,128)} %copy-done.20, f32[1152]{0:T(1024)S(1)} %get-tuple-element.201, f32[1152]{0:T(1024)S(1)} %get-tuple-element.202, f32[1024]{0:T(1024)S(1)} %add_rsqrt_fusion, f32[1024]{0:T(1024)S(1)} %broadcast_multiply_fusion.4), kind=kOutput, calls=%fused_computation.114 | convolution fusion | flops 10877534208 | bytes 34227200 | tf_op jit(solution)/shard_map/ird,fd->irf/dot_general | solution.py:1075
  255.3 18.1 %convolution_convert_fusion.1 = bf16[1152,4608]{1,0:T(8,128)(2,1)} fusion(bf16[1024,1152]{1,0:T(8,128)(2,1)S(1)} %multiply_convert_fusion.2, f32[1024,4608]{1,0:T(8,128)} %fusion.40, f32[4608]{0:T(1024)S(1)} %add.190), kind=kOutput, calls=%fused_computation.3 | convolution fusion | flops 10924130304 | bytes 31868928 | tf_op jit(solution)/shard_map/ird,irf->df/dot_general | solution.py:1087
  282.7 29.2 %convert_reduce_fusion = (f32[4608]{0:T(1024)S(1)}, bf16[1024,4608]{1,0:T(8,128)(2,1)S(1)}) fusion(f32[1024,4608]{1,0:T(8,128)} %fusion.40, f32[4608]{0:T(1024)S(1)} %add.190, bf16[1152,4608]{1,0:T(8,128)(2,1)} %all-gather.6.cloned.1.call-done, bf16[1,1024,1152]{2,1,0:T(8,128)(2,1)S(1)} %get-tuple-element.66), kind=kOutput, calls=%fused_computation.11 | convolution fusion | flops 10980159488 | bytes 41324544 | tf_op jit(solution)/shard_map/ird,df->irf/dot_general | solution.py:1091
  315.4 18.0 %convolution_convert_fusion = bf16[4608,1152]{1,0:T(8,128)(2,1)} fusion(bf16[1024,4608]{1,0:T(8,128)(2,1)S(1)} %get-tuple-element.226, f32[1024,1152]{1,0:T(8,128)} %copy-done.20, f32[1152]{0:T(1024)S(1)} %get-tuple-element.201, f32[1152]{0:T(1024)S(1)} %get-tuple-element.202, f32[1024]{0:T(1024)S(1)} %add_rsqrt_fusion, f32[1024]{0:T(1024)S(1)} %broadcast_multiply_fusion.4), kind=kOutput, calls=%fused_computation.2 | convolution fusion | flops 10882842624 | bytes 24790016 | tf_op jit(solution)/shard_map/irf,ird->fd/dot_general | solution.py:1098
  333.5 21.9 %multiply_reduce_fusion.1 = (f32[1152]{0:T(1024)S(1)}, f32[1024]{0:T(1024)S(1)}, f32[1024]{0:T(1024)S(1)}, f32[1152]{0:T(1024)S(1)}, f32[1024,1152]{1,0:T(8,128)}) fusion(f32[1024,1152]{1,0:T(8,128)} %copy-done.20, f32[1024]{0:T(1024)S(1)} %add_rsqrt_fusion, f32[1024]{0:T(1024)S(1)} %broadcast_multiply_fusion.4, f32[1152]{0:T(1024)S(1)} %get-tuple-element.202, ...), kind=kOutput, calls=%fused_computation.47 | convolution fusion | flops 10882248704 | bytes 29521408 | tf_op jit(solution)/shard_map/irf,fd->ird/dot_general | solution.py:1102
  358.0 4.9 all-to-all-start.2
  362.9 27.9 %multiply_reduce_fusion = (f32[1152]{0:T(1024)S(1)}, bf16[1024,1152]{1,0:T(8,128)(2,1)}, f32[1152]{0:T(1024)S(1)}, bf16[1024,1152]{1,0:T(8,128)(2,1)}, f32[1024,1152]{1,0:T(8,128)}) fusion(bf16[4,256,1152]{2,1,0:T(8,128)(2,1)} %all-to-all-done.1, f32[1024]{0:T(1024)S(1)} %fusion.37, f32[1024,1152]{1,0:T(8,128)} %copy-done.20, ...), kind=kOutput, calls=%fused_computation.46 | convolution fusion | flops 10942412800 | bytes 50791424 | tf_op jit(solution)/shard_map/irf,df->ird/dot_general | solution.py:1081
  391.3 6.6 convolution_convert_fusion.3.out_ref
  397.9 4.7 convolution_convert_fusion.4.grad_ref
  406.5 60.8 %shard_map.383 = (bf16[1024,3456]{1,0:T(8,128)(2,1)}, bf16[4,256,1152]{2,1,0:T(8,128)(2,1)}, f32[8,128]{1,0:T(8,128)}) custom-call(bf16[1024,3456]{1,0:T(8,128)(2,1)} %add_convert_fusion.query_ref.keyval_ref.both_ref, f32[1024,1]{1,0:T(8,128)} %fusion.33.bias_ref, bf16[1024,1152]{1,0:T(8,128)(2,1)} %get-tuple-element.63.mixed_ref, ...), custom_call_target="tpu_custom_call" | custom-call | bytes 182400000 | tf_op jit(solution)/shard_map/pallas_call | solution.py:269
  467.4 16.2 %convolution_convert_fusion.2.qkv_ref = bf16[3456,1152]{1,0:T(8,128)(2,1)} fusion(bf16[1024,3456]{1,0:T(8,128)(2,1)} %get-tuple-element.73, bf16[1024,1152]{1,0:T(8,128)(2,1)S(1)} %copy-done.1, f32[1152]{0:T(1024)S(1)} %copy-done.38, f32[1152]{0:T(1024)S(1)} %copy-done.32, f32[1024]{0:T(1024)S(1)} %copy-done.35, f32[1024]{0:T(1024)S(1)} %copy-done.30), kind=kOutput, calls=%fused_computation.13 | convolution fusion | flops 8164786176 | bytes 17417216 | tf_op jit(solution)/shard_map/ire,ird->ed/dot_general | solution.py:1150
  483.7 13.6 %fusion.24 = (f32[1152]{0:T(1024)S(1)}, f32[1024]{0:T(1024)S(1)}, f32[1024]{0:T(1024)S(1)}, f32[1152]{0:T(1024)S(1)}, f32[1024,1152]{1,0:T(8,128)S(1)}) fusion(bf16[1024,1152]{1,0:T(8,128)(2,1)S(1)} %copy-done.1, f32[1024]{0:T(1024)S(1)} %copy-done.35, f32[1024]{0:T(1024)S(1)} %copy-done.30, f32[1152]{0:T(1024)S(1)} %copy-done.32, ...), kind=kOutput, calls=%fused_computation.38 | convolution fusion | flops 8165519360 | bytes 22148608 | tf_op jit(solution)/shard_map/ire,ed->ird/dot_general | solution.py:1153
  501.1 4.0 convert_reduce_fusion.1
  507.3 122.7 %shard_map.384 = (f32[288,1152]{1,0:T(8,128)S(1)}, bf16[4,256,1152]{2,1,0:T(8,128)(2,1)}, f32[288,864]{1,0:T(8,128)S(1)}, f32[14,144]{1,0:T(8,128)S(1)}, f32[8,128]{1,0:T(8,128)S(1)}) custom-call(bf16[3456,1152]{1,0:T(8,128)(2,1)} %convolution_convert_fusion.2.qkv_ref, bf16[1152,1152]{1,0:T(8,128)(2,1)} %convolution_convert_fusion.3.out_ref, ...), custom_call_target="tpu_custom_call" | custom-call | bytes 352000000 | tf_op jit(solution)/shard_map/pallas_call | solution.py:814
  633.3 4.2 convert_element_type.196
  637.4 13.5 %shard_map.385 = (f32[288,864]{1,0:T(8,128)}, f32[288,864]{1,0:T(8,128)}, f32[288,864]{1,0:T(8,128)}, f32[288,432]{1,0:T(8,128)}, f32[288,432]{1,0:T(8,128)}, /*...) custom-call(f32[8,128]{1,0:T(8,128)S(1)} %get-tuple-element.77.refs_, ...), custom_call_target="tpu_custom_call" | custom-call | tf_op jit(solution)/shard_map/pallas_call | solution.py:902
  (221 shorter events, 64.3 us)
Async XLA Ops:
  7.2 226.0 %all-gather.4.cloned.1.call-start = ((), (), s32[]{:S(2)}) async-start(), calls=%async_computation.5 | async-start | bytes 11943936 | tf_op jit(solution)/shard_map/all_gather | solution.py:1005
  9.4 123.8 %copy-start.11 = (f32[14,144]{1,0:T(8,128)S(1)}, f32[14,144]{1,0:T(8,128)}, u32[]{:S(2)}) copy-start(f32[14,144]{1,0:T(8,128)} %refs_20_.1) | copy-start | bytes 24196
  9.4 123.9 %copy-start.36 = (bf16[4,1152]{1,0:T(4,128)(2,1)S(1)}, bf16[4,1152]{1,0:T(4,128)(2,1)}, u32[]{:S(2)}) copy-start(bf16[4,1152]{1,0:T(4,128)(2,1)} %param.23) | copy-start | bytes 27652
  14.0 139.6 %copy-start.41 = (s32[4]{0:T(128)S(1)}, s32[4]{0:T(128)}, u32[]{:S(2)}) copy-start(s32[4]{0:T(128)} %param.24) | copy-start | bytes 52
  132.4 88.1 %copy-start = (bf16[1024,1152]{1,0:T(8,128)(2,1)}, bf16[1024,1152]{1,0:T(8,128)(2,1)S(1)}, u32[]{:S(2)}) copy-start(bf16[1024,1152]{1,0:T(8,128)(2,1)S(1)} %get-tuple-element.61) | copy-start | bytes 7077892
  132.4 150.2 %all-gather.6.cloned.1.call-start = ((), (), s32[]{:S(2)}) async-start(), calls=%async_computation.6 | async-start | bytes 11943936 | tf_op jit(solution)/shard_map/all_gather | solution.py:1006
  145.4 15.7 %all-to-all-start = ((f32[32,1,864]{2,1,0:T(1,128)}), f32[32,1,864]{2,1,0:T(1,128)S(1)}, u32[]{:S(2)}, u32[]{:S(2)}) async-start(f32[32,1,864]{2,1,0:T(1,128)} %copy.100), calls=%async_computation | async-start | bytes 229376 | tf_op jit(solution)/shard_map/all_to_all | solution.py:1018
  156.7 26.9 %copy-start.29 = (f32[1024]{0:T(1024)}, f32[1024]{0:T(1024)S(1)}, u32[]{:S(2)}) copy-start(f32[1024]{0:T(1024)S(1)} %broadcast_multiply_fusion.5) | copy-start | bytes 12292
  157.5 26.1 %copy-start.34 = (f32[1024]{0:T(1024)}, f32[1024]{0:T(1024)S(1)}, u32[]{:S(2)}) copy-start(f32[1024]{0:T(1024)S(1)} %add_rsqrt_fusion.1) | copy-start | bytes 12292
  161.1 69.8 %all-to-all-start.1 = ((bf16[4,256,1152]{2,1,0:T(8,128)(2,1)}), bf16[4,256,1152]{2,1,0:T(8,128)(2,1)}, u32[]{:S(2)}, u32[]{:S(2)}) async-start(bf16[4,256,1152]{2,1,0:T(8,128)(2,1)} %param.25), calls=%async_computation.1 | async-start | bytes 4718592 | tf_op jit(solution)/shard_map/all_to_all | solution.py:955
  165.6 189.8 %reduce-scatter.3.cloned.1.call-start = ((), (), s32[]{:S(2)}) async-start(), calls=%async_computation.7 | async-start | bytes 11943936 | tf_op jit(solution)/shard_map/reduce_scatter | solution.py:1090
  166.6 54.0 %copy-start.39 = (f32[1152]{0:T(1024)}, f32[1152]{0:T(1024)S(1)}, u32[]{:S(2)}) copy-start(f32[1152]{0:T(1024)S(1)} %get-tuple-element.203) | copy-start | bytes 13828
  183.7 36.9 %copy-start.16 = (bf16[1152,1152]{1,0:T(8,128)(2,1)S(1)}, bf16[1152,1152]{1,0:T(8,128)(2,1)}, u32[]{:S(2)}) copy-start(bf16[1152,1152]{1,0:T(8,128)(2,1)} %copy-done.15) | copy-start | bytes 7962628
  273.5 232.4 %reduce-scatter.5.cloned.1.call-start = ((), (), s32[]{:S(2)}) async-start(), calls=%async_computation.8 | async-start | bytes 11943936 | tf_op jit(solution)/shard_map/reduce_scatter | solution.py:1101
  358.0 44.7 %all-to-all-start.2 = ((bf16[4,144,1152]{2,1,0:T(8,128)(2,1)}), bf16[4,144,1152]{2,1,0:T(8,128)(2,1)}, u32[]{:S(2)}, u32[]{:S(2)}) async-start(bf16[4,144,1152]{2,1,0:T(8,128)(2,1)} %bitcast.77), calls=%async_computation.3 | async-start | bytes 2654208 | tf_op jit(solution)/shard_map/all_to_all | solution.py:1118
  362.9 28.4 %copy-start.22 = (bf16[1024,1152]{1,0:T(8,128)(2,1)S(1)}, bf16[1024,1152]{1,0:T(8,128)(2,1)}, u32[]{:S(2)}) copy-start(bf16[1024,1152]{1,0:T(8,128)(2,1)} %get-tuple-element.63.mixed_ref) | copy-start | bytes 7077892
  404.4 62.9 %copy-start.19 = (f32[144,1152]{1,0:T(8,128)}, f32[144,1152]{1,0:T(8,128)S(1)}, u32[]{:S(2)}) copy-start(f32[144,1152]{1,0:T(8,128)S(1)} %convert_reduce_fusion.5.refs_2_) | copy-start | bytes 1990660
  406.5 60.9 %copy-start.1 = (bf16[1024,1152]{1,0:T(8,128)(2,1)S(1)}, bf16[1024,1152]{1,0:T(8,128)(2,1)}, u32[]{:S(2)}) copy-start(bf16[1024,1152]{1,0:T(8,128)(2,1)} %copy-done) | copy-start | bytes 7077892
  406.5 60.9 %copy-start.30 = (f32[1024]{0:T(1024)S(1)}, f32[1024]{0:T(1024)}, u32[]{:S(2)}) copy-start(f32[1024]{0:T(1024)} %copy-done.29) | copy-start | bytes 12292
  406.5 60.9 %copy-start.32 = (f32[1152]{0:T(1024)S(1)}, f32[1152]{0:T(1024)}, u32[]{:S(2)}) copy-start(f32[1152]{0:T(1024)} %copy-done.31) | copy-start | bytes 13828
  406.5 60.9 %copy-start.35 = (f32[1024]{0:T(1024)S(1)}, f32[1024]{0:T(1024)}, u32[]{:S(2)}) copy-start(f32[1024]{0:T(1024)} %copy-done.34) | copy-start | bytes 12292
  406.5 60.9 %copy-start.38 = (f32[1152]{0:T(1024)S(1)}, f32[1152]{0:T(1024)}, u32[]{:S(2)}) copy-start(f32[1152]{0:T(1024)} %copy-done.37) | copy-start | bytes 13828
  467.4 29.8 %slice-start = ((s8[4718592]{0:T(1024)(128)(4,1)}), s8[4194304]{0:T(1024)(128)(4,1)S(1)}, s32[]{:S(2)}) async-start(s8[4718592]{0:T(1024)(128)(4,1)} %bitcast.81), calls=%async_computation.9 | async-start | bytes 8388608
  467.4 29.8 %slice-start.2 = ((s8[4718592]{0:T(1024)(128)(4,1)}), s8[4194304]{0:T(1024)(128)(4,1)S(1)}, s32[]{:S(2)}) async-start(s8[4718592]{0:T(1024)(128)(4,1)} %bitcast.83), calls=%async_computation.11 | async-start | bytes 8388608
  (31 other events, 172.5 us)
Sparse Core Ops, SparseCore 0:
  132.5 68.0 all-gather.3
  202.6 63.8 all-gather.5
  273.6 81.7 reduce-scatter.2
  358.8 82.2 reduce-scatter.4

commit v6 on v5

--- a/solution.py
+++ b/solution.py
@@ -304,10 +304,11 @@
 
 
 def start_kernel(
-    wide_ref, tall_ref, tokens_ref,
-    qkv_ref, out_ref, up_ref, down_ref, rows_ref,
+    wide_ref, tall_ref, tokens_ref, told_ref, ada_ref,
+    qkv_ref, out_ref, up_ref, down_ref, rows_ref, heard_ref, silu_ref, mod_ref,
+    partial, summed, banded, small_send, small_recv,
     held, turned, line_send, line_recv, row_send, row_recv, flat_send, flat_recv, local_sem,
-    *, bands, qkv_part, out_part,
+    *, imgs, bands, qkv_part, out_part,
 ):
     img, band = lax.axis_index("img"), lax.axis_index("band")
     depth, width = wide_ref.shape
@@ -319,13 +320,14 @@
     across = flip(beside_x, 4)
 
     barrier = pltpu.get_barrier_semaphore()
-    for other in (beside_x, beside_y, sibling):
+    for step in range(1, imgs):
+        other = lax.rem(img + step, imgs)
         pl.semaphore_signal(barrier, inc=1, device_id={"img": other}, device_id_type=MESH)
     for step in range(1, bands):
         pl.semaphore_signal(
             barrier, inc=1, device_id={"band": lax.rem(band + step, bands)}, device_id_type=MESH
         )
-    pl.semaphore_wait(barrier, 3 + bands - 1)
+    pl.semaphore_wait(barrier, imgs + bands - 2)
 
     def piece(part, owner):
         if part == 2:
@@ -434,9 +436,35 @@
         local_sem.at[0],
     )
     own_rows.start()
+
+    def small_copy(source, target, kind, step, axis, toward):
+        return pltpu.make_async_remote_copy(
+            src_ref=source, dst_ref=target,
+            send_sem=small_send.at[kind, step], recv_sem=small_recv.at[kind, step],
+            device_id={axis: toward}, device_id_type=MESH,
+        )
+
+    def told(step):
+        return small_copy(told_ref, heard_ref.at[img], 0, step, "img", lax.rem(img + step, imgs))
+
+    def partial_copy(step):
+        other = lax.rem(img + step, imgs)
+        return small_copy(partial.at[other], summed.at[img], 1, step, "img", other)
+
+    def banded_copy(step):
+        other = lax.rem(band + step, bands)
+        return small_copy(summed.at[:, other], banded.at[band], 2, step, "band", other)
+
+    def arrival(view, kind, step, axis):
+        me, count = (img, imgs) if axis == "img" else (band, bands)
+        small_copy(view, view, kind, step, axis, lax.rem(me + count - step, count)).wait_recv()
+
+    for step in range(1, imgs):
+        told(step).start()
     held[pl.ds(pl.multiple_of(band * depth, 16), depth), :] = wide_ref[...]
     down_ref[:, pl.ds(pl.multiple_of(band * tall_width, lanes), tall_width)] = tall_ref[...]
     line_sends(0, 0, start)
+    heard_ref[img] = told_ref[...]
     for step in range(bands - 1):
         line_arrivals(0, step)
         if step < bands - 2:
@@ -452,6 +480,24 @@
         flat_copy(at).start()
     keep_qkv.start()
     keep_out.start()
+    for step in range(1, imgs):
+        arrival(heard_ref.at[lax.rem(img + imgs - step, imgs)], 0, step, "img")
+    images = partial.shape[1]
+    for other in range(imgs):
+        for image in range(images):
+            silu_ref[pl.ds(other * images + image, 1), :] = heard_ref[
+                other, :, pl.ds(image * depth, depth)
+            ]
+    products = jnp.dot(
+        silu_ref[...].astype(jnp.bfloat16), ada_ref[...], preferred_element_type=jnp.float32
+    )
+    for other in range(imgs):
+        for image in range(images):
+            at = other * images + image
+            partial[other, image] = products[at : at + 1, :]
+    for step in range(1, imgs):
+        partial_copy(step).start()
+    summed[img] = partial[img]
     for step in range(bands - 2):
         for part in (1, 2):
             line_arrivals(part, step)
@@ -461,6 +507,11 @@
             flat_arrival(at)
         for at in sent:
             flat_copy(at).start()
+    for step in range(1, imgs):
+        arrival(summed.at[lax.rem(img + imgs - step, imgs)], 1, step, "img")
+    for step in range(1, bands):
+        banded_copy(step).start()
+    banded[band] = summed[:, band]
     for at in (6, 7, 8):
         flat_arrival(at)
         flat_copy(at + 7).start()
@@ -468,6 +519,12 @@
         line_arrivals(part, bands - 2)
     pl.loop(first // lanes, width // lanes)(turn)
     up_ref[...] = turned[pl.ds(qkv_part + out_part, width - qkv_part - out_part), :]
+    for step in range(1, bands):
+        arrival(banded.at[lax.rem(band + bands - step, bands)], 2, step, "band")
+    total = banded[0]
+    for at in range(1, bands):
+        total += banded[at]
+    mod_ref[...] = total
     for part in range(3):
         for step in range(bands - 1):
             line_sends(part, step, lambda copy: copy.wait_send())
@@ -478,29 +535,45 @@
     for step in range(1, bands):
         row_copy(step).wait_send()
         row_arrival(step).wait_recv()
+        banded_copy(step).wait_send()
+    for step in range(1, imgs):
+        told(step).wait_send()
+        partial_copy(step).wait_send()
     own_rows.wait()
     keep_qkv.wait()
     keep_out.wait()
 
 
-def start_exchange(wide, tall, tokens, bands, imgs, qkv_part, out_part):
+def start_exchange(wide, tall, tokens, told, ada, bands, imgs, qkv_part, out_part):
     depth, width = wide.shape
     up_part = width - qkv_part - out_part
     low = jnp.bfloat16
     anywhere, vmem = pl.BlockSpec(memory_space=pl.ANY), pl.BlockSpec(memory_space=pltpu.VMEM)
     features = depth * bands
+    images = tokens.shape[0]
+    ada_columns = ada.shape[1]
     return pl.pallas_call(
-        functools.partial(start_kernel, bands=bands, qkv_part=qkv_part, out_part=out_part),
+        functools.partial(
+            start_kernel, imgs=imgs, bands=bands, qkv_part=qkv_part, out_part=out_part
+        ),
         out_shape=(
             jax.ShapeDtypeStruct((qkv_part * imgs, features), low),
             jax.ShapeDtypeStruct((out_part * imgs, features), low),
             jax.ShapeDtypeStruct((up_part, features), low),
             jax.ShapeDtypeStruct((tall.shape[0], tall.shape[1] * bands), low),
             jax.ShapeDtypeStruct((tokens.shape[1] * bands, tokens.shape[2]), low),
+            jax.ShapeDtypeStruct((imgs,) + told.shape, jnp.float32),
+            jax.ShapeDtypeStruct((imgs * images, depth), jnp.float32),
+            jax.ShapeDtypeStruct((imgs, 1, ada_columns), jnp.float32),
         ),
-        in_specs=[vmem, vmem, anywhere],
-        out_specs=(anywhere, anywhere, vmem, vmem, anywhere),
+        in_specs=[vmem, vmem, anywhere, vmem, vmem],
+        out_specs=(anywhere, anywhere, vmem, vmem, anywhere, vmem, vmem, vmem),
         scratch_shapes=[
+            pltpu.VMEM((imgs, images, 1, ada_columns), jnp.float32),
+            pltpu.VMEM((imgs, images, 1, ada_columns), jnp.float32),
+            pltpu.VMEM((bands, imgs, 1, ada_columns), jnp.float32),
+            pltpu.SemaphoreType.DMA((3, imgs)),
+            pltpu.SemaphoreType.DMA((3, imgs)),
             pltpu.VMEM((features, width), low),
             pltpu.VMEM((width, features), low),
             pltpu.SemaphoreType.DMA((3, 2, bands - 1)),
@@ -513,9 +586,9 @@
         ],
         cost_estimate=expected(START_US),
         compiler_params=pltpu.CompilerParams(
-            collective_id=0, has_side_effects=True, vmem_limit_bytes=40 * 2**20
+            collective_id=0, has_side_effects=True, vmem_limit_bytes=48 * 2**20
         ),
-    )(wide, tall, tokens)
+    )(wide, tall, tokens, told, ada)
 
 
 def add_low(left, right):
@@ -704,11 +777,6 @@
     turned[pl.ds(both, width - both), :] = up_ref[...]
     pl.loop(first // lanes, width // lanes)(turn)
     line_ends(1)
-    keep_piece.wait()
-    for step in range(1, imgs):
-        arrival(pieces.at[band, lax.rem(img + imgs - step, imgs)], 0, step, "img")
-    for step in range(1, bands):
-        piece_line(step).start()
     for step in range(1, bands):
         row_copy(step).start()
     for at in order:
@@ -718,6 +786,11 @@
         own[at] = add_low(own[at], from_core[at])
         for ready in {3: (1, 3), 1: (0,), 2: (2,), 0: ()}[at]:
             flat_copy(ready).start()
+    keep_piece.wait()
+    for step in range(1, imgs):
+        arrival(pieces.at[band, lax.rem(img + imgs - step, imgs)], 0, step, "img")
+    for step in range(1, bands):
+        piece_line(step).start()
     flat_copy(1).wait_recv()
     own[2, upper] = add_low(own[2, upper], first_x[1])
     flat_copy(4).start()
@@ -741,6 +814,10 @@
     ).astype(jnp.bfloat16)
     pl.loop(0, first // lanes)(turn)
     line_ends(0)
+    for step in range(bands - 1):
+        line_round(0, step)
+        if step > 0:
+            line_round(1, step)
     for step in range(1, bands):
         arrival(pieces.at[lax.rem(band + bands - step, bands)], 1, step, "band")
     for image in range(imgs):
@@ -759,10 +836,6 @@
     squares = jnp.sum(ada * ada, axis=0, keepdims=True)
     squares = jnp.sum(squares, axis=1, keepdims=True)
     squares += jnp.sum(bias * bias, axis=1, keepdims=True) / bands
-    for step in range(bands - 1):
-        line_round(0, step)
-        if step > 0:
-            line_round(1, step)
     line_finish(1)
     line_finish(0)
     rows = jnp.sum(wide_ref[...] * wide_ref[...], axis=0, keepdims=True)
@@ -972,27 +1045,24 @@
     qkv_part, out_part = qkv_weight.shape[1], out_weight.shape[1]
 
     bias_rows, bias_columns = biases.shape
-    small = lax.all_gather(
-        jnp.concatenate([condition.reshape(1, -1), biases.astype(low_type).reshape(1, -1)], axis=1),
-        "img",
-        axis=0,
-        tiled=True,
-    )
-    condition_all = small[:, : images * features].reshape(img_count * images, features)
-    bias_vals = (
-        small[:, images * features :]
-        .astype(jnp.float32)
-        .reshape(img_count, bias_rows, bias_columns)
-        .transpose(1, 0, 2)
-        .reshape(bias_rows, features)
-    )
+    ada_rows, ada_columns = ada_weight.shape
+    silu_own = lax.reduce_precision(jax.nn.silu(condition.astype(jnp.float32)), 8, 7)
+    silu_own = lax.dynamic_slice_in_dim(silu_own, band_rank * ada_rows, ada_rows, axis=1)
+    told = jnp.concatenate(
+        [silu_own.reshape(1, -1), lax.reduce_precision(biases, 8, 7).reshape(1, -1)],
+        axis=1,
+    )
+    ada_low = ada_weight.astype(low_type)
     wide = jnp.concatenate([qkv_weight, out_weight, up_weight], axis=1).astype(low_type)
     tall = down_weight.T.astype(low_type)
     if img_count == 8 and own == 1 and split == 1:
-        qkv_full, out_full, up_rows, down_rows, tokens_low = start_exchange(
-            wide, tall, inputs, band_count, img_count, qkv_part, out_part
+        qkv_full, out_full, up_rows, down_rows, tokens_low, heard, silu_rows, mod_summed = (
+            start_exchange(
+                wide, tall, inputs, told, ada_low, band_count, img_count, qkv_part, out_part
+            )
         )
         tokens_low = tokens_low.reshape(own, image_rows, features)
+        mod_summed = mod_summed.reshape(own, img_count * ada_columns)
     else:
         turned = lax.all_gather(wide, "band", axis=0, tiled=True).T
         qkv_full = lax.all_gather(turned[:qkv_part], "img", axis=0, tiled=True)
@@ -1002,30 +1072,33 @@
         up_rows = turned[qkv_part + out_part :]
         down_rows = lax.all_gather(tall, "band", axis=1, tiled=True)
         tokens_low = to_images(inputs)
+        heard = lax.all_gather(told, "img", axis=0, tiled=True)
+        silu_rows = heard[:, : images * ada_rows].reshape(img_count * images, ada_rows)
+        mod_partial = jnp.dot(
+            silu_rows.astype(low_type), ada_low, preferred_element_type=jnp.float32
+        )
+        mod_sent = jnp.tile(
+            mod_partial.reshape(img_count, 1, images * ada_columns), (1, split, 1)
+        )
+        mod_pieces = lax.all_to_all(
+            mod_sent.reshape(img_count * band_count, own * ada_columns),
+            ("img", "band"),
+            split_axis=0,
+            concat_axis=0,
+            tiled=True,
+        ).reshape(img_count, band_count, own, ada_columns)
+        mod_summed = (
+            jnp.sum(mod_pieces, axis=1).transpose(1, 0, 2).reshape(own, img_count * ada_columns)
+        )
     up_full = lax.all_gather(up_rows, "img", axis=0, tiled=True)
     down_full = lax.all_gather(after(down_rows, up_rows), "img", axis=0, tiled=True)
-
-    silu_all = jax.nn.silu(condition_all.astype(jnp.float32)).astype(low_type)
-    ada_rows = ada_weight.shape[0]
-    silu_rows = lax.dynamic_slice_in_dim(silu_all, band_rank * ada_rows, ada_rows, axis=1)
-    mod_partial = jnp.dot(
-        silu_rows, ada_weight.astype(low_type), preferred_element_type=jnp.float32
-    )
-    ada_columns = mod_partial.shape[1]
-    mod_sent = jnp.tile(
-        mod_partial.reshape(img_count, 1, images * ada_columns), (1, split, 1)
-    )
-    mod_pieces = lax.all_to_all(
-        mod_sent.reshape(img_count * band_count, own * ada_columns),
-        ("img", "band"),
-        split_axis=0,
-        concat_axis=0,
-        tiled=True,
-    ).reshape(img_count, band_count, own, ada_columns)
-    modulation = (
-        jnp.sum(mod_pieces, axis=1).transpose(1, 0, 2).reshape(own, img_count * ada_columns)
-        + bias_vals[0:6].reshape(-1)
-    )
+    bias_vals = (
+        heard.reshape(img_count, -1)[:, images * ada_rows :]
+        .reshape(img_count, bias_rows, bias_columns)
+        .transpose(1, 0, 2)
+        .reshape(bias_rows, features)
+    )
+    modulation = mod_summed + bias_vals[0:6].reshape(-1)
     mod_parts = modulation.reshape(own, 6, 1, features)
     shift_one = mod_parts[:, 0]
     scale_one = mod_parts[:, 1]
@@ -1190,7 +1263,7 @@
         axis=1,
     )
     silu_terms = jnp.tile(
-        silu_rows.astype(jnp.float32).reshape(img_count, 1, images, ada_rows), (1, split, 1, 1)
+        silu_rows.reshape(img_count, 1, images, ada_rows), (1, split, 1, 1)
     ).reshape(img_count * band_count * own, ada_rows)
     if img_count == 8 and own == 1 and split == 1:
         wide_shard, input_grad_low, ada_shard, bias_total, squares_total = tail_exchange(

time: 676 us -> 664 us (0.982)
  waiting for transfers between devices: 4.37 us -> 20.7 us
  blocking collectives: 9.32 us -> 0 us
    reduce_scatter x1, waiting for transfers between devices: 0.02 us -> 15.5 us  [body(): lax.psum_scatter(down_grad, 'img', scatter_dimension=0, tiled=True)]
    all_gather x1 -> x0, blocking collectives: 9.32 us -> none  [body(): lax.all_gather(jnp.concatenate([condition.reshape(1, -1), biases.astype(l...]
    pallas_call x1, Pallas kernels: 123 us -> 115 us  [tail_exchange(): pl.pallas_call(functools.partial(tail_kernel, imgs=imgs, bands=bands), ou...]
    all_to_all x1 -> x0, starting transfers between devices: 7.41 us -> none  [body(): lax.all_to_all(mod_sent.reshape(img_count * band_count, own * ada_columns...]
    unnamed x122 -> x110, local copies, waits for them, and re-layouts: 32.2 us -> 26.8 us
  transfers between devices with their start and end apart: 7 -> 6, of which waited for: 1 -> 2; matrix products, arithmetic and copies ran while one was open for 35% -> 35% of each run, Pallas kernels for 15% -> 15%
where the time goes in v6:
time: 664 us; the launch traced here: 660 us
  Pallas kernels  344 us (52%)
  matrix products  199 us (30%)
  local copies, waits for them, and re-layouts  35.3 us (5%)
  other arithmetic  30.6 us (5%)
  waiting for transfers between devices  20.7 us (3%)
  between operations  16.9 us (3%)
  starting transfers between devices  13.4 us (2%)
    pallas_call x1, Pallas kernels, start_exchange(): pl.pallas_call(functools.partial(start_kernel, imgs=imgs, bands=bands, qk...  118 us
    pallas_call x1, Pallas kernels, tail_exchange(): pl.pallas_call(functools.partial(tail_kernel, imgs=imgs, bands=bands), ou...  115 us
    pallas_call x1, Pallas kernels, attention_backward(): pl.pallas_call(shared_kernel, out_shape=(jax.ShapeDtypeStruct((rows, 3 *...  60.9 us
    pallas_call x1, Pallas kernels, attention_forward(): pl.pallas_call(functools.partial(attention_forward_kernel, features=featu...  36.8 us
    dot_general x1, matrix products, body(): jnp.einsum('irf,df->ird', hidden_low, down_full, preferred_element_type=j...  27.8 us
    dot_general x1, matrix products, body(): jnp.einsum('ird,df->irf', after(branch_grad, down_grad), down_full, prefe...  27 us
    unnamed x110, local copies, waits for them, and re-layouts  26.8 us
    dot_general x1, matrix products, body(): jnp.einsum('irf,fd->ird', after(pre_grad, up_grad), up_full, preferred_el...  21.2 us
  transfers between devices with their start and end apart: 6, of which 2 were waited for; matrix products, arithmetic and copies ran while one was open for 35% of the time, Pallas kernels for 15%

profile of v6, /device:TPU:0, one launch (start us, length us, event | category | flops | bytes accessed | tf_op | source)
XLA Modules:
  0.0 659.7 jit_solution(9073333226569758443)
XLA Ops:
  15.3 118.4 %shard_map.381 = (bf16[3456,1152]{1,0:T(8,128)(2,1)}, bf16[1152,1152]{1,0:T(8,128)(2,1)}, bf16[576,1152]{1,0:T(8,128)(2,1)}, bf16[144,4608]{1,0:T(8,128)(2,1)}, ...) custom-call(bf16[288,1152]{1,0:T(8,128)(2,1)S(1)} %concatenate.29.wide, ...), custom_call_target="tpu_custom_call" | custom-call | bytes 368000000 | tf_op jit(solution)/shard_map/pallas_call | solution.py:555
  134.5 8.2 %all-to-all-start = ((bf16[4,256,1152]{2,1,0:T(8,128)(2,1)}), bf16[4,256,1152]{2,1,0:T(8,128)(2,1)}, u32[]{:S(2)}, u32[]{:S(2)}) async-start(bf16[4,256,1152]{2,1,0:T(8,128)(2,1)} %param.25), calls=%async_computation | async-start | bytes 4718592 | tf_op jit(solution)/shard_map/all_to_all | solution.py:1028
  147.4 15.5 %add_convert_fusion.query_ref.keyval_ref.both_ref = bf16[1024,3456]{1,0:T(8,128)(2,1)} fusion(bf16[3456,1152]{1,0:T(8,128)(2,1)} %get-tuple-element.67, f32[3456]{0:T(1024)S(1)} %pad_maximum_fusion.1, bf16[1024,1152]{1,0:T(8,128)(2,1)S(1)} %copy-done.10, f32[1152]{0:T(1024)S(1)} %get-tuple-element.210, f32[1152]{0:T(1024)S(1)} %get-tuple-element.211, ...), kind=kOutput, calls=%fused_computation.15 | convolution fusion | flops 8167882752 | bytes 17431040 | tf_op jit(solution)/shard_map/ird,ed->ire/dot_general | solution.py:1120
  162.9 36.8 %shard_map.382 = (bf16[1024,1152]{1,0:T(8,128)(2,1)}, f32[16,1024]{1,0:T(8,128)}) custom-call(bf16[1024,3456]{1,0:T(8,128)(2,1)} %add_convert_fusion.query_ref.keyval_ref.both_ref, bf16[1024,3456]{1,0:T(8,128)(2,1)} %add_convert_fusion.query_ref.keyval_ref.both_ref, f32[1024,1]{1,0:T(8,128)} %fusion.33.bias_ref), custom_call_target="tpu_custom_call" | custom-call | bytes 118400000 | tf_op jit(solution)/shard_map/pallas_call | solution.py:127
  200.4 7.5 %fusion.42 = (f32[1024]{0:T(1024)S(1)}, f32[1024,1152]{1,0:T(8,128)S(1)}, f32[1024,1152]{1,0:T(8,128)}) fusion(f32[1152]{0:T(1024)S(1)} %get-tuple-element.209, bf16[1024,1152]{1,0:T(8,128)(2,1)S(1)} %copy-done.10, f32[1152]{0:T(1024)S(1)} %add.180, bf16[1024,1152]{1,0:T(8,128)(2,1)} %get-tuple-element.68.mixed_ref, bf16[1152,1152]{1,0:T(8,128)(2,1)S(1)} %copy-done.34), kind=kOutput, calls=%fused_computation.110 | convolution fusion | flops 2723806208 | bytes 16823296 | tf_op jit(solution)/shard_map/ird,ed->ire/dot_general | solution.py:1142
  213.4 21.2 %fusion.40 = f32[1024,4608]{1,0:T(8,128)} fusion(bf16[4608,1152]{1,0:T(8,128)(2,1)} %all-gather.3.cloned.1.call-done, f32[1024,1152]{1,0:T(8,128)} %copy-done.14, f32[1152]{0:T(1024)S(1)} %get-tuple-element.207, f32[1152]{0:T(1024)S(1)} %get-tuple-element.208, f32[1024]{0:T(1024)S(1)} %add_rsqrt_fusion, f32[1024]{0:T(1024)S(1)} %broadcast_multiply_fusion.4), kind=kOutput, calls=%fused_computation.109 | convolution fusion | flops 10877534208 | bytes 34227200 | tf_op jit(solution)/shard_map/ird,fd->irf/dot_general | solution.py:1148
  234.6 19.2 %convolution_convert_fusion.1 = bf16[1152,4608]{1,0:T(8,128)(2,1)} fusion(bf16[1024,1152]{1,0:T(8,128)(2,1)S(1)} %multiply_convert_fusion.2, f32[1024,4608]{1,0:T(8,128)} %fusion.40, f32[4608]{0:T(1024)S(1)} %add.190), kind=kOutput, calls=%fused_computation.3 | convolution fusion | flops 10924130304 | bytes 31868928 | tf_op jit(solution)/shard_map/ird,irf->df/dot_general | solution.py:1160
  263.0 4.4 all-gather.5.cloned.1.call-done
  267.4 27.0 %convert_reduce_fusion = (f32[4608]{0:T(1024)S(1)}, bf16[1024,4608]{1,0:T(8,128)(2,1)S(1)}) fusion(f32[1024,4608]{1,0:T(8,128)} %fusion.40, f32[4608]{0:T(1024)S(1)} %add.190, bf16[1152,4608]{1,0:T(8,128)(2,1)} %all-gather.5.cloned.1.call-done, bf16[1,1024,1152]{2,1,0:T(8,128)(2,1)S(1)} %get-tuple-element.71), kind=kOutput, calls=%fused_computation.11 | convolution fusion | flops 10980159488 | bytes 41324544 | tf_op jit(solution)/shard_map/ird,df->irf/dot_general | solution.py:1164
  294.4 3.9 copy-done.37
  298.3 18.1 %convolution_convert_fusion = bf16[4608,1152]{1,0:T(8,128)(2,1)} fusion(bf16[1024,4608]{1,0:T(8,128)(2,1)S(1)} %get-tuple-element.232, f32[1024,1152]{1,0:T(8,128)} %copy-done.14, f32[1152]{0:T(1024)S(1)} %get-tuple-element.207, f32[1152]{0:T(1024)S(1)} %get-tuple-element.208, f32[1024]{0:T(1024)S(1)} %add_rsqrt_fusion, f32[1024]{0:T(1024)S(1)} %broadcast_multiply_fusion.4), kind=kOutput, calls=%fused_computation.2 | convolution fusion | flops 10882842624 | bytes 24790016 | tf_op jit(solution)/shard_map/irf,ird->fd/dot_general | solution.py:1171
  316.4 21.2 %multiply_reduce_fusion.1 = (f32[1152]{0:T(1024)S(1)}, f32[1024]{0:T(1024)S(1)}, f32[1024]{0:T(1024)S(1)}, f32[1152]{0:T(1024)S(1)}, f32[1024,1152]{1,0:T(8,128)}) fusion(f32[1024,1152]{1,0:T(8,128)} %copy-done.14, f32[1024]{0:T(1024)S(1)} %add_rsqrt_fusion, f32[1024]{0:T(1024)S(1)} %broadcast_multiply_fusion.4, f32[1152]{0:T(1024)S(1)} %get-tuple-element.208, ...), kind=kOutput, calls=%fused_computation.47 | convolution fusion | flops 10882248704 | bytes 29521408 | tf_op jit(solution)/shard_map/irf,fd->ird/dot_general | solution.py:1175
  337.6 15.5 %reduce-scatter.3.cloned.1.call-done = bf16[144,4608]{1,0:T(8,128)(2,1)} async-done(((bf16[1152,4608]{1,0:T(8,128)(2,1)}), bf16[144,4608]{1,0:T(8,128)(2,1)}) %reduce-scatter.3.cloned.1.call-update) | async-done | bytes 1327120 | tf_op jit(solution)/shard_map/reduce_scatter | solution.py:1163
  355.7 4.6 all-to-all-start.1
  360.3 27.8 %multiply_reduce_fusion = (f32[1152]{0:T(1024)S(1)}, bf16[1024,1152]{1,0:T(8,128)(2,1)}, f32[1152]{0:T(1024)S(1)}, bf16[1024,1152]{1,0:T(8,128)(2,1)}, f32[1024,1152]{1,0:T(8,128)}) fusion(bf16[4,256,1152]{2,1,0:T(8,128)(2,1)} %all-to-all-done, f32[1024]{0:T(1024)S(1)} %fusion.37, f32[1024,1152]{1,0:T(8,128)} %copy-done.14, ...), kind=kOutput, calls=%fused_computation.46 | convolution fusion | flops 10942412800 | bytes 50791424 | tf_op jit(solution)/shard_map/irf,df->ird/dot_general | solution.py:1154
  388.6 6.6 convolution_convert_fusion.3.out_ref
  395.1 4.7 convolution_convert_fusion.4.grad_ref
  403.5 60.9 %shard_map.383 = (bf16[1024,3456]{1,0:T(8,128)(2,1)}, bf16[4,256,1152]{2,1,0:T(8,128)(2,1)}, f32[8,128]{1,0:T(8,128)}) custom-call(bf16[1024,3456]{1,0:T(8,128)(2,1)} %add_convert_fusion.query_ref.keyval_ref.both_ref, f32[1024,1]{1,0:T(8,128)} %fusion.33.bias_ref, bf16[1024,1152]{1,0:T(8,128)(2,1)} %get-tuple-element.68.mixed_ref, ...), custom_call_target="tpu_custom_call" | custom-call | bytes 182400000 | tf_op jit(solution)/shard_map/pallas_call | solution.py:269
  464.5 16.2 %convolution_convert_fusion.2.qkv_ref = bf16[3456,1152]{1,0:T(8,128)(2,1)} fusion(bf16[1024,3456]{1,0:T(8,128)(2,1)} %get-tuple-element.78, bf16[1024,1152]{1,0:T(8,128)(2,1)S(1)} %copy-done.11, f32[1152]{0:T(1024)S(1)} %copy-done.31, f32[1152]{0:T(1024)S(1)} %copy-done.26, f32[1024]{0:T(1024)S(1)} %copy-done.29, f32[1024]{0:T(1024)S(1)} %copy-done.24), kind=kOutput, calls=%fused_computation.13 | convolution fusion | flops 8164786176 | bytes 17417216 | tf_op jit(solution)/shard_map/ire,ird->ed/dot_general | solution.py:1223
  480.8 13.5 %fusion.24 = (f32[1152]{0:T(1024)S(1)}, f32[1024]{0:T(1024)S(1)}, f32[1024]{0:T(1024)S(1)}, f32[1152]{0:T(1024)S(1)}, f32[1024,1152]{1,0:T(8,128)S(1)}) fusion(bf16[1024,1152]{1,0:T(8,128)(2,1)S(1)} %copy-done.11, f32[1024]{0:T(1024)S(1)} %copy-done.29, f32[1024]{0:T(1024)S(1)} %copy-done.24, f32[1152]{0:T(1024)S(1)} %copy-done.26, ...), kind=kOutput, calls=%fused_computation.38 | convolution fusion | flops 8165519360 | bytes 22148608 | tf_op jit(solution)/shard_map/ire,ed->ird/dot_general | solution.py:1226
  498.2 4.0 convert_reduce_fusion.1
  504.4 114.6 %shard_map.384 = (f32[288,1152]{1,0:T(8,128)S(1)}, bf16[4,256,1152]{2,1,0:T(8,128)(2,1)}, f32[288,864]{1,0:T(8,128)S(1)}, f32[14,144]{1,0:T(8,128)S(1)}, f32[8,128]{1,0:T(8,128)S(1)}) custom-call(bf16[3456,1152]{1,0:T(8,128)(2,1)} %convolution_convert_fusion.2.qkv_ref, bf16[1152,1152]{1,0:T(8,128)(2,1)} %convolution_convert_fusion.3.out_ref, ...), custom_call_target="tpu_custom_call" | custom-call | bytes 352000000 | tf_op jit(solution)/shard_map/pallas_call | solution.py:887
  622.3 4.2 convert_element_type.182
  626.5 13.5 %shard_map.385 = (f32[288,864]{1,0:T(8,128)}, f32[288,864]{1,0:T(8,128)}, f32[288,864]{1,0:T(8,128)}, f32[288,432]{1,0:T(8,128)}, f32[288,432]{1,0:T(8,128)}, /*...) custom-call(f32[8,128]{1,0:T(8,128)S(1)} %get-tuple-element.83.refs_, ...), custom_call_target="tpu_custom_call" | custom-call | tf_op jit(solution)/shard_map/pallas_call | solution.py:975
  (203 shorter events, 55.2 us)
Async XLA Ops:
  7.2 206.2 %all-gather.3.cloned.1.call-start = ((), (), s32[]{:S(2)}) async-start(), calls=%async_computation.4 | async-start | bytes 11943936 | tf_op jit(solution)/shard_map/all_gather | solution.py:1093
  133.7 133.6 %all-gather.5.cloned.1.call-start = ((), (), s32[]{:S(2)}) async-start(), calls=%async_computation.5 | async-start | bytes 11943936 | tf_op jit(solution)/shard_map/all_gather | solution.py:1094
  134.5 76.2 %all-to-all-start = ((bf16[4,256,1152]{2,1,0:T(8,128)(2,1)}), bf16[4,256,1152]{2,1,0:T(8,128)(2,1)}, u32[]{:S(2)}, u32[]{:S(2)}) async-start(bf16[4,256,1152]{2,1,0:T(8,128)(2,1)} %param.25), calls=%async_computation | async-start | bytes 4718592 | tf_op jit(solution)/shard_map/all_to_all | solution.py:1028
  142.7 210.5 %reduce-scatter.3.cloned.1.call-start = ((), (), s32[]{:S(2)}) async-start(), calls=%async_computation.6 | async-start | bytes 11943936 | tf_op jit(solution)/shard_map/reduce_scatter | solution.py:1163
  144.6 18.2 %copy-start.25 = (f32[1152]{0:T(1024)}, f32[1152]{0:T(1024)S(1)}, u32[]{:S(2)}) copy-start(f32[1152]{0:T(1024)S(1)} %get-tuple-element.211) | copy-start | bytes 13828
  144.7 18.2 %copy-start.30 = (f32[1152]{0:T(1024)}, f32[1152]{0:T(1024)S(1)}, u32[]{:S(2)}) copy-start(f32[1152]{0:T(1024)S(1)} %get-tuple-element.210) | copy-start | bytes 13828
  144.7 55.7 %copy-start.32 = (f32[1152]{0:T(1024)}, f32[1152]{0:T(1024)S(1)}, u32[]{:S(2)}) copy-start(f32[1152]{0:T(1024)S(1)} %get-tuple-element.209) | copy-start | bytes 13828
  146.6 16.3 %copy-start.23 = (f32[1024]{0:T(1024)}, f32[1024]{0:T(1024)S(1)}, u32[]{:S(2)}) copy-start(f32[1024]{0:T(1024)S(1)} %broadcast_multiply_fusion.5) | copy-start | bytes 12292
  147.4 15.5 %copy-start.28 = (f32[1024]{0:T(1024)}, f32[1024]{0:T(1024)S(1)}, u32[]{:S(2)}) copy-start(f32[1024]{0:T(1024)S(1)} %add_rsqrt_fusion.1) | copy-start | bytes 12292
  162.9 37.5 %copy-start.34 = (bf16[1152,1152]{1,0:T(8,128)(2,1)S(1)}, bf16[1152,1152]{1,0:T(8,128)(2,1)}, u32[]{:S(2)}) copy-start(bf16[1152,1152]{1,0:T(8,128)(2,1)} %get-tuple-element.69) | copy-start | bytes 7962628
  253.9 249.2 %reduce-scatter.5.cloned.1.call-start = ((), (), s32[]{:S(2)}) async-start(), calls=%async_computation.7 | async-start | bytes 11943936 | tf_op jit(solution)/shard_map/reduce_scatter | solution.py:1174
  337.6 22.7 %copy-start.33 = (f32[1152]{0:T(1024)S(1)}, f32[1152]{0:T(1024)}, u32[]{:S(2)}) copy-start(f32[1152]{0:T(1024)} %copy-done.32) | copy-start | bytes 13828
  355.7 44.2 %all-to-all-start.1 = ((bf16[4,144,1152]{2,1,0:T(8,128)(2,1)}), bf16[4,144,1152]{2,1,0:T(8,128)(2,1)}, u32[]{:S(2)}, u32[]{:S(2)}) async-start(bf16[4,144,1152]{2,1,0:T(8,128)(2,1)} %bitcast.69), calls=%async_computation.2 | async-start | bytes 2654208 | tf_op jit(solution)/shard_map/all_to_all | solution.py:1191
  360.3 28.2 %copy-start.16 = (bf16[1024,1152]{1,0:T(8,128)(2,1)S(1)}, bf16[1024,1152]{1,0:T(8,128)(2,1)}, u32[]{:S(2)}) copy-start(bf16[1024,1152]{1,0:T(8,128)(2,1)} %get-tuple-element.68.mixed_ref) | copy-start | bytes 7077892
  401.4 63.0 %copy-start.13 = (f32[144,1152]{1,0:T(8,128)}, f32[144,1152]{1,0:T(8,128)S(1)}, u32[]{:S(2)}) copy-start(f32[144,1152]{1,0:T(8,128)S(1)} %convert_reduce_fusion.5.refs_2_) | copy-start | bytes 1990660
  403.5 61.0 %copy-start.11 = (bf16[1024,1152]{1,0:T(8,128)(2,1)S(1)}, bf16[1024,1152]{1,0:T(8,128)(2,1)}, u32[]{:S(2)}) copy-start(bf16[1024,1152]{1,0:T(8,128)(2,1)} %get-tuple-element.64) | copy-start | bytes 7077892
  403.5 61.0 %copy-start.24 = (f32[1024]{0:T(1024)S(1)}, f32[1024]{0:T(1024)}, u32[]{:S(2)}) copy-start(f32[1024]{0:T(1024)} %copy-done.23) | copy-start | bytes 12292
  403.5 61.0 %copy-start.26 = (f32[1152]{0:T(1024)S(1)}, f32[1152]{0:T(1024)}, u32[]{:S(2)}) copy-start(f32[1152]{0:T(1024)} %copy-done.25) | copy-start | bytes 13828
  403.5 61.0 %copy-start.29 = (f32[1024]{0:T(1024)S(1)}, f32[1024]{0:T(1024)}, u32[]{:S(2)}) copy-start(f32[1024]{0:T(1024)} %copy-done.28) | copy-start | bytes 12292
  403.5 61.0 %copy-start.31 = (f32[1152]{0:T(1024)S(1)}, f32[1152]{0:T(1024)}, u32[]{:S(2)}) copy-start(f32[1152]{0:T(1024)} %copy-done.30) | copy-start | bytes 13828
  464.5 16.3 %copy-start.12 = (bf16[1024,3456]{1,0:T(8,128)(2,1)S(1)}, bf16[1024,3456]{1,0:T(8,128)(2,1)}, u32[]{:S(2)}) copy-start(bf16[1024,3456]{1,0:T(8,128)(2,1)} %get-tuple-element.78) | copy-start | bytes 21233668
  464.5 29.8 %slice-start = ((s8[4718592]{0:T(1024)(128)(4,1)}), s8[4194304]{0:T(1024)(128)(4,1)S(1)}, s32[]{:S(2)}) async-start(s8[4718592]{0:T(1024)(128)(4,1)} %bitcast.74), calls=%async_computation.8 | async-start | bytes 8388608
  464.5 29.8 %slice-start.2 = ((s8[4718592]{0:T(1024)(128)(4,1)}), s8[4194304]{0:T(1024)(128)(4,1)S(1)}, s32[]{:S(2)}) async-start(s8[4718592]{0:T(1024)(128)(4,1)} %bitcast.76), calls=%async_computation.10 | async-start | bytes 8388608
  480.8 13.6 %slice-start.3 = ((s8[4718592]{0:T(1024)(128)(4,1)}), s8[524288]{0:T(1024)(128)(4,1)S(1)}, s32[]{:S(2)}) async-start(s8[4718592]{0:T(1024)(128)(4,1)} %bitcast.76), calls=%async_computation.11 | async-start | bytes 1048576
  (25 other events, 123.5 us)
Sparse Core Ops, SparseCore 0:
  133.9 67.7 all-gather.2
  203.5 63.8 all-gather.4
  270.9 82.2 reduce-scatter.2
  356.5 82.1 reduce-scatter.4

commit v7 on v6

--- a/solution.py
+++ b/solution.py
@@ -956,16 +956,12 @@
         update(2, rows, wide_ref[rows, qkv_part:both])
         update(3, rows, wide_ref[rows, both:])
 
-    tall_width = sources[12].shape[0]
-    whole = tall_width // 128 * 128
-
-    @pl.loop(0, tall_width // 128)
-    def _(step):
-        rows = pl.ds(pl.multiple_of(step * 128, 128), 128)
-        update(4, rows, tall_ref[:, rows].T)
-
-    if whole < tall_width:
-        update(4, pl.ds(whole, tall_width - whole), tall_ref[:, whole:].T)
+    tall_rows = tall_ref.shape[0]
+    tall_block = 16 if tall_rows % 16 == 0 else tall_rows
+    for start in range(0, tall_rows, tall_block):
+        rows = pl.ds(start, tall_block)
+        update(4, rows, tall_ref[rows, :])
+
     update(5, slice(None), bias_ref[...])
     results[18][...] = bias_ref[pl.ds(13, 1), :] * factor
 
@@ -1310,7 +1306,7 @@
         (qkv_weight, qkv_first, qkv_second),
         (out_weight, out_first, out_second),
         (up_weight, up_first, up_second),
-        (down_weight, down_first, down_second),
+        (down_weight.T, down_first.T, down_second.T),
         (biases, bias_first, bias_second),
     )
     updated = adam_all(squares_total, wide_shard, tall_shard, ada_shard, bias_total, groups)
@@ -1318,7 +1314,7 @@
     qkv_new, qkv_first_new, qkv_second_new = updated[3:6]
     out_new, out_first_new, out_second_new = updated[6:9]
     up_new, up_first_new, up_second_new = updated[9:12]
-    down_new, down_first_new, down_second_new = updated[12:15]
+    down_new, down_first_new, down_second_new = (array.T for array in updated[12:15])
     bias_new, bias_first_new, bias_second_new = updated[15:18]
     branch_bias_grad = updated[18][0]
     return (

time: 664 us -> 657 us (0.989)
  local copies, waits for them, and re-layouts: 35.3 us -> 25 us
    unnamed x110 -> x96, local copies, waits for them, and re-layouts: 26.8 us -> 16.5 us
where the time goes in v7:
time: 657 us; the launch traced here: 654 us
  Pallas kernels  343 us (52%)
  matrix products  199 us (30%)
  other arithmetic  30.8 us (5%)
  waiting for transfers between devices  25.6 us (4%)
  local copies, waits for them, and re-layouts  25 us (4%)
  between operations  16.9 us (3%)
  starting transfers between devices  13.7 us (2%)
    pallas_call x1, Pallas kernels, start_exchange(): pl.pallas_call(functools.partial(start_kernel, imgs=imgs, bands=bands, qk...  118 us
    pallas_call x1, Pallas kernels, tail_exchange(): pl.pallas_call(functools.partial(tail_kernel, imgs=imgs, bands=bands), ou...  117 us
    pallas_call x1, Pallas kernels, attention_backward(): pl.pallas_call(shared_kernel, out_shape=(jax.ShapeDtypeStruct((rows, 3 *...  60.6 us
    pallas_call x1, Pallas kernels, attention_forward(): pl.pallas_call(functools.partial(attention_forward_kernel, features=featu...  36.9 us
    dot_general x1, matrix products, body(): jnp.einsum('irf,df->ird', hidden_low, down_full, preferred_element_type=j...  28.1 us
    dot_general x1, matrix products, body(): jnp.einsum('ird,df->irf', after(branch_grad, down_grad), down_full, prefe...  27 us
    dot_general x1, matrix products, body(): jnp.einsum('ird,fd->irf', second_in, up_full, preferred_element_type=jnp....  21.1 us
    dot_general x1, matrix products, body(): jnp.einsum('irf,fd->ird', after(pre_grad, up_grad), up_full, preferred_el...  20.8 us
  transfers between devices with their start and end apart: 6, of which 2 were waited for; matrix products, arithmetic and copies ran while one was open for 35% of the time, Pallas kernels for 15%

profile of v7, /device:TPU:0, one launch (start us, length us, event | category | flops | bytes accessed | tf_op | source)
XLA Modules:
  0.0 653.9 jit_solution(5198368426564427890)
XLA Ops:
  15.3 118.4 %shard_map.381 = (bf16[3456,1152]{1,0:T(8,128)(2,1)}, bf16[1152,1152]{1,0:T(8,128)(2,1)}, bf16[576,1152]{1,0:T(8,128)(2,1)}, bf16[144,4608]{1,0:T(8,128)(2,1)}, ...) custom-call(bf16[288,1152]{1,0:T(8,128)(2,1)S(1)} %concatenate.29.wide, ...), custom_call_target="tpu_custom_call" | custom-call | bytes 368000000 | tf_op jit(solution)/shard_map/pallas_call | solution.py:555
  134.5 8.2 %all-to-all-start = ((bf16[4,256,1152]{2,1,0:T(8,128)(2,1)}), bf16[4,256,1152]{2,1,0:T(8,128)(2,1)}, u32[]{:S(2)}, u32[]{:S(2)}) async-start(bf16[4,256,1152]{2,1,0:T(8,128)(2,1)} %param.25), calls=%async_computation | async-start | bytes 4718592 | tf_op jit(solution)/shard_map/all_to_all | solution.py:1024
  147.3 15.5 %add_convert_fusion.query_ref.keyval_ref.both_ref = bf16[1024,3456]{1,0:T(8,128)(2,1)} fusion(bf16[3456,1152]{1,0:T(8,128)(2,1)} %get-tuple-element.67, f32[3456]{0:T(1024)S(1)} %pad_maximum_fusion.1, bf16[1024,1152]{1,0:T(8,128)(2,1)S(1)} %copy-done.10, f32[1152]{0:T(1024)S(1)} %get-tuple-element.210, f32[1152]{0:T(1024)S(1)} %get-tuple-element.211, ...), kind=kOutput, calls=%fused_computation.15 | convolution fusion | flops 8167882752 | bytes 17431040 | tf_op jit(solution)/shard_map/ird,ed->ire/dot_general | solution.py:1116
  162.8 36.9 %shard_map.382 = (bf16[1024,1152]{1,0:T(8,128)(2,1)}, f32[16,1024]{1,0:T(8,128)}) custom-call(bf16[1024,3456]{1,0:T(8,128)(2,1)} %add_convert_fusion.query_ref.keyval_ref.both_ref, bf16[1024,3456]{1,0:T(8,128)(2,1)} %add_convert_fusion.query_ref.keyval_ref.both_ref, f32[1024,1]{1,0:T(8,128)} %fusion.33.bias_ref), custom_call_target="tpu_custom_call" | custom-call | bytes 118400000 | tf_op jit(solution)/shard_map/pallas_call | solution.py:127
  200.3 7.5 %fusion.42 = (f32[1024]{0:T(1024)S(1)}, f32[1024,1152]{1,0:T(8,128)S(1)}, f32[1024,1152]{1,0:T(8,128)}) fusion(f32[1152]{0:T(1024)S(1)} %get-tuple-element.209, bf16[1024,1152]{1,0:T(8,128)(2,1)S(1)} %copy-done.10, f32[1152]{0:T(1024)S(1)} %add.180, bf16[1024,1152]{1,0:T(8,128)(2,1)} %get-tuple-element.68.mixed_ref, bf16[1152,1152]{1,0:T(8,128)(2,1)S(1)} %copy-done.30), kind=kOutput, calls=%fused_computation.110 | convolution fusion | flops 2723806208 | bytes 16823296 | tf_op jit(solution)/shard_map/ird,ed->ire/dot_general | solution.py:1138
  213.3 21.1 %fusion.40 = f32[1024,4608]{1,0:T(8,128)} fusion(bf16[4608,1152]{1,0:T(8,128)(2,1)} %all-gather.3.cloned.1.call-done, f32[1024,1152]{1,0:T(8,128)} %copy-done.14, f32[1152]{0:T(1024)S(1)} %get-tuple-element.207, f32[1152]{0:T(1024)S(1)} %get-tuple-element.208, f32[1024]{0:T(1024)S(1)} %add_rsqrt_fusion, f32[1024]{0:T(1024)S(1)} %broadcast_multiply_fusion.4), kind=kOutput, calls=%fused_computation.109 | convolution fusion | flops 10877534208 | bytes 34227200 | tf_op jit(solution)/shard_map/ird,fd->irf/dot_general | solution.py:1144
  234.4 19.3 %convolution_convert_fusion.1 = bf16[1152,4608]{1,0:T(8,128)(2,1)} fusion(bf16[1024,1152]{1,0:T(8,128)(2,1)S(1)} %multiply_convert_fusion.2, f32[1024,4608]{1,0:T(8,128)} %fusion.40, f32[4608]{0:T(1024)S(1)} %add.190), kind=kOutput, calls=%fused_computation.3 | convolution fusion | flops 10924130304 | bytes 31868928 | tf_op jit(solution)/shard_map/ird,irf->df/dot_general | solution.py:1156
  258.6 8.8 %all-gather.5.cloned.1.call-done = bf16[1152,4608]{1,0:T(8,128)(2,1)} async-done(((bf16[144,4608]{1,0:T(8,128)(2,1)}), bf16[1152,4608]{1,0:T(8,128)(2,1)}) %all-gather.5.cloned.1.call-update) | async-done | bytes 10616848 | tf_op jit(solution)/shard_map/all_gather | solution.py:1090
  267.4 27.0 %convert_reduce_fusion = (f32[4608]{0:T(1024)S(1)}, bf16[1024,4608]{1,0:T(8,128)(2,1)S(1)}) fusion(f32[1024,4608]{1,0:T(8,128)} %fusion.40, f32[4608]{0:T(1024)S(1)} %add.190, bf16[1152,4608]{1,0:T(8,128)(2,1)} %all-gather.5.cloned.1.call-done, bf16[1,1024,1152]{2,1,0:T(8,128)(2,1)S(1)} %get-tuple-element.71), kind=kOutput, calls=%fused_computation.11 | convolution fusion | flops 10980159488 | bytes 41324544 | tf_op jit(solution)/shard_map/ird,df->irf/dot_general | solution.py:1160
  294.4 3.9 copy-done.33
  298.3 18.1 %convolution_convert_fusion = bf16[4608,1152]{1,0:T(8,128)(2,1)} fusion(bf16[1024,4608]{1,0:T(8,128)(2,1)S(1)} %get-tuple-element.232, f32[1024,1152]{1,0:T(8,128)} %copy-done.14, f32[1152]{0:T(1024)S(1)} %get-tuple-element.207, f32[1152]{0:T(1024)S(1)} %get-tuple-element.208, f32[1024]{0:T(1024)S(1)} %add_rsqrt_fusion, f32[1024]{0:T(1024)S(1)} %broadcast_multiply_fusion.4), kind=kOutput, calls=%fused_computation.2 | convolution fusion | flops 10882842624 | bytes 24790016 | tf_op jit(solution)/shard_map/irf,ird->fd/dot_general | solution.py:1167
  316.4 20.8 %multiply_reduce_fusion.1 = (f32[1152]{0:T(1024)S(1)}, f32[1024]{0:T(1024)S(1)}, f32[1024]{0:T(1024)S(1)}, f32[1152]{0:T(1024)S(1)}, f32[1024,1152]{1,0:T(8,128)}) fusion(f32[1024,1152]{1,0:T(8,128)} %copy-done.14, f32[1024]{0:T(1024)S(1)} %add_rsqrt_fusion, f32[1024]{0:T(1024)S(1)} %broadcast_multiply_fusion.4, f32[1152]{0:T(1024)S(1)} %get-tuple-element.208, ...), kind=kOutput, calls=%fused_computation.47 | convolution fusion | flops 10882248704 | bytes 29521408 | tf_op jit(solution)/shard_map/irf,fd->ird/dot_general | solution.py:1171
  337.2 16.0 %reduce-scatter.3.cloned.1.call-done = bf16[144,4608]{1,0:T(8,128)(2,1)} async-done(((bf16[1152,4608]{1,0:T(8,128)(2,1)}), bf16[144,4608]{1,0:T(8,128)(2,1)}) %reduce-scatter.3.cloned.1.call-update) | async-done | bytes 1327120 | tf_op jit(solution)/shard_map/reduce_scatter | solution.py:1159
  355.7 5.0 all-to-all-start.1
  360.7 28.1 %multiply_reduce_fusion = (f32[1152]{0:T(1024)S(1)}, bf16[1024,1152]{1,0:T(8,128)(2,1)}, f32[1152]{0:T(1024)S(1)}, bf16[1024,1152]{1,0:T(8,128)(2,1)}, f32[1024,1152]{1,0:T(8,128)}) fusion(bf16[4,256,1152]{2,1,0:T(8,128)(2,1)} %all-to-all-done, f32[1024]{0:T(1024)S(1)} %fusion.37, f32[1024,1152]{1,0:T(8,128)} %copy-done.14, ...), kind=kOutput, calls=%fused_computation.46 | convolution fusion | flops 10942412800 | bytes 50791424 | tf_op jit(solution)/shard_map/irf,df->ird/dot_general | solution.py:1150
  389.3 6.8 %convolution_convert_fusion.3.out_ref = bf16[1152,1152]{1,0:T(8,128)(2,1)} fusion(bf16[1024,1152]{1,0:T(8,128)(2,1)} %get-tuple-element.222, bf16[1024,1152]{1,0:T(8,128)(2,1)S(1)} %copy-done.15), kind=kOutput, calls=%fused_computation.18 | convolution fusion | flops 2719236096 | bytes 7372800 | tf_op jit(solution)/shard_map/ire,ird->ed/dot_general | solution.py:1179
  396.1 4.7 convolution_convert_fusion.4.grad_ref
  404.6 60.6 %shard_map.383 = (bf16[1024,3456]{1,0:T(8,128)(2,1)}, bf16[4,256,1152]{2,1,0:T(8,128)(2,1)}, f32[8,128]{1,0:T(8,128)}) custom-call(bf16[1024,3456]{1,0:T(8,128)(2,1)} %add_convert_fusion.query_ref.keyval_ref.both_ref, f32[1024,1]{1,0:T(8,128)} %fusion.33.bias_ref, bf16[1024,1152]{1,0:T(8,128)(2,1)} %get-tuple-element.68.mixed_ref, ...), custom_call_target="tpu_custom_call" | custom-call | bytes 182400000 | tf_op jit(solution)/shard_map/pallas_call | solution.py:269
  465.3 16.2 %convolution_convert_fusion.2.qkv_ref = bf16[3456,1152]{1,0:T(8,128)(2,1)} fusion(bf16[1024,3456]{1,0:T(8,128)(2,1)} %get-tuple-element.78, bf16[1024,1152]{1,0:T(8,128)(2,1)S(1)} %copy-done.11, f32[1152]{0:T(1024)S(1)} %copy-done.27, f32[1152]{0:T(1024)S(1)} %copy-done.22, f32[1024]{0:T(1024)S(1)} %copy-done.25, f32[1024]{0:T(1024)S(1)} %copy-done.20), kind=kOutput, calls=%fused_computation.13 | convolution fusion | flops 8164786176 | bytes 17417216 | tf_op jit(solution)/shard_map/ire,ird->ed/dot_general | solution.py:1219
  481.6 13.5 %fusion.24 = (f32[1152]{0:T(1024)S(1)}, f32[1024]{0:T(1024)S(1)}, f32[1024]{0:T(1024)S(1)}, f32[1152]{0:T(1024)S(1)}, f32[1024,1152]{1,0:T(8,128)S(1)}) fusion(bf16[1024,1152]{1,0:T(8,128)(2,1)S(1)} %copy-done.11, f32[1024]{0:T(1024)S(1)} %copy-done.25, f32[1024]{0:T(1024)S(1)} %copy-done.20, f32[1152]{0:T(1024)S(1)} %copy-done.22, ...), kind=kOutput, calls=%fused_computation.38 | convolution fusion | flops 8165519360 | bytes 22148608 | tf_op jit(solution)/shard_map/ire,ed->ird/dot_general | solution.py:1222
  499.0 4.0 convert_reduce_fusion.1
  505.2 116.6 %shard_map.384 = (f32[288,1152]{1,0:T(8,128)S(1)}, bf16[4,256,1152]{2,1,0:T(8,128)(2,1)}, f32[288,864]{1,0:T(8,128)S(1)}, f32[14,144]{1,0:T(8,128)S(1)}, f32[8,128]{1,0:T(8,128)S(1)}) custom-call(bf16[3456,1152]{1,0:T(8,128)(2,1)} %convolution_convert_fusion.2.qkv_ref, bf16[1152,1152]{1,0:T(8,128)(2,1)} %convolution_convert_fusion.3.out_ref, ...), custom_call_target="tpu_custom_call" | custom-call | bytes 352000000 | tf_op jit(solution)/shard_map/pallas_call | solution.py:887
  625.1 4.2 convert_element_type.179
  629.3 11.0 %shard_map.385 = (f32[288,864]{1,0:T(8,128)}, f32[288,864]{1,0:T(8,128)}, f32[288,864]{1,0:T(8,128)}, f32[288,432]{1,0:T(8,128)}, f32[288,432]{1,0:T(8,128)}, /*...) custom-call(f32[8,128]{1,0:T(8,128)S(1)} %get-tuple-element.83.refs_, ...), custom_call_target="tpu_custom_call" | custom-call | tf_op jit(solution)/shard_map/pallas_call | solution.py:971
  (189 shorter events, 45.0 us)
Async XLA Ops:
  7.2 206.1 %all-gather.3.cloned.1.call-start = ((), (), s32[]{:S(2)}) async-start(), calls=%async_computation.4 | async-start | bytes 11943936 | tf_op jit(solution)/shard_map/all_gather | solution.py:1089
  133.7 133.6 %all-gather.5.cloned.1.call-start = ((), (), s32[]{:S(2)}) async-start(), calls=%async_computation.5 | async-start | bytes 11943936 | tf_op jit(solution)/shard_map/all_gather | solution.py:1090
  134.5 76.2 %all-to-all-start = ((bf16[4,256,1152]{2,1,0:T(8,128)(2,1)}), bf16[4,256,1152]{2,1,0:T(8,128)(2,1)}, u32[]{:S(2)}, u32[]{:S(2)}) async-start(bf16[4,256,1152]{2,1,0:T(8,128)(2,1)} %param.25), calls=%async_computation | async-start | bytes 4718592 | tf_op jit(solution)/shard_map/all_to_all | solution.py:1024
  142.7 210.5 %reduce-scatter.3.cloned.1.call-start = ((), (), s32[]{:S(2)}) async-start(), calls=%async_computation.6 | async-start | bytes 11943936 | tf_op jit(solution)/shard_map/reduce_scatter | solution.py:1159
  144.5 18.3 %copy-start.21 = (f32[1152]{0:T(1024)}, f32[1152]{0:T(1024)S(1)}, u32[]{:S(2)}) copy-start(f32[1152]{0:T(1024)S(1)} %get-tuple-element.211) | copy-start | bytes 13828
  144.5 18.3 %copy-start.26 = (f32[1152]{0:T(1024)}, f32[1152]{0:T(1024)S(1)}, u32[]{:S(2)}) copy-start(f32[1152]{0:T(1024)S(1)} %get-tuple-element.210) | copy-start | bytes 13828
  144.6 55.8 %copy-start.28 = (f32[1152]{0:T(1024)}, f32[1152]{0:T(1024)S(1)}, u32[]{:S(2)}) copy-start(f32[1152]{0:T(1024)S(1)} %get-tuple-element.209) | copy-start | bytes 13828
  146.5 16.3 %copy-start.19 = (f32[1024]{0:T(1024)}, f32[1024]{0:T(1024)S(1)}, u32[]{:S(2)}) copy-start(f32[1024]{0:T(1024)S(1)} %broadcast_multiply_fusion.5) | copy-start | bytes 12292
  147.2 15.6 %copy-start.24 = (f32[1024]{0:T(1024)}, f32[1024]{0:T(1024)S(1)}, u32[]{:S(2)}) copy-start(f32[1024]{0:T(1024)S(1)} %add_rsqrt_fusion.1) | copy-start | bytes 12292
  162.8 37.5 %copy-start.30 = (bf16[1152,1152]{1,0:T(8,128)(2,1)S(1)}, bf16[1152,1152]{1,0:T(8,128)(2,1)}, u32[]{:S(2)}) copy-start(bf16[1152,1152]{1,0:T(8,128)(2,1)} %get-tuple-element.69) | copy-start | bytes 7962628
  253.7 250.2 %reduce-scatter.5.cloned.1.call-start = ((), (), s32[]{:S(2)}) async-start(), calls=%async_computation.7 | async-start | bytes 11943936 | tf_op jit(solution)/shard_map/reduce_scatter | solution.py:1170
  337.2 23.5 %copy-start.29 = (f32[1152]{0:T(1024)S(1)}, f32[1152]{0:T(1024)}, u32[]{:S(2)}) copy-start(f32[1152]{0:T(1024)} %copy-done.28) | copy-start | bytes 13828
  355.7 45.1 %all-to-all-start.1 = ((bf16[4,144,1152]{2,1,0:T(8,128)(2,1)}), bf16[4,144,1152]{2,1,0:T(8,128)(2,1)}, u32[]{:S(2)}, u32[]{:S(2)}) async-start(bf16[4,144,1152]{2,1,0:T(8,128)(2,1)} %bitcast.74), calls=%async_computation.2 | async-start | bytes 2654208 | tf_op jit(solution)/shard_map/all_to_all | solution.py:1187
  360.7 28.6 %copy-start.15 = (bf16[1024,1152]{1,0:T(8,128)(2,1)S(1)}, bf16[1024,1152]{1,0:T(8,128)(2,1)}, u32[]{:S(2)}) copy-start(bf16[1024,1152]{1,0:T(8,128)(2,1)} %get-tuple-element.68.mixed_ref) | copy-start | bytes 7077892
  402.6 62.6 %copy-start.13 = (f32[144,1152]{1,0:T(8,128)}, f32[144,1152]{1,0:T(8,128)S(1)}, u32[]{:S(2)}) copy-start(f32[144,1152]{1,0:T(8,128)S(1)} %convert_reduce_fusion.5.refs_2_) | copy-start | bytes 1990660
  404.6 60.6 %copy-start.11 = (bf16[1024,1152]{1,0:T(8,128)(2,1)S(1)}, bf16[1024,1152]{1,0:T(8,128)(2,1)}, u32[]{:S(2)}) copy-start(bf16[1024,1152]{1,0:T(8,128)(2,1)} %get-tuple-element.64) | copy-start | bytes 7077892
  404.6 60.6 %copy-start.20 = (f32[1024]{0:T(1024)S(1)}, f32[1024]{0:T(1024)}, u32[]{:S(2)}) copy-start(f32[1024]{0:T(1024)} %copy-done.19) | copy-start | bytes 12292
  404.6 60.6 %copy-start.22 = (f32[1152]{0:T(1024)S(1)}, f32[1152]{0:T(1024)}, u32[]{:S(2)}) copy-start(f32[1152]{0:T(1024)} %copy-done.21) | copy-start | bytes 13828
  404.6 60.7 %copy-start.25 = (f32[1024]{0:T(1024)S(1)}, f32[1024]{0:T(1024)}, u32[]{:S(2)}) copy-start(f32[1024]{0:T(1024)} %copy-done.24) | copy-start | bytes 12292
  404.6 60.7 %copy-start.27 = (f32[1152]{0:T(1024)S(1)}, f32[1152]{0:T(1024)}, u32[]{:S(2)}) copy-start(f32[1152]{0:T(1024)} %copy-done.26) | copy-start | bytes 13828
  465.3 16.3 %copy-start.12 = (bf16[1024,3456]{1,0:T(8,128)(2,1)S(1)}, bf16[1024,3456]{1,0:T(8,128)(2,1)}, u32[]{:S(2)}) copy-start(bf16[1024,3456]{1,0:T(8,128)(2,1)} %get-tuple-element.78) | copy-start | bytes 21233668
  465.3 29.8 %slice-start = ((s8[4718592]{0:T(1024)(128)(4,1)}), s8[4194304]{0:T(1024)(128)(4,1)S(1)}, s32[]{:S(2)}) async-start(s8[4718592]{0:T(1024)(128)(4,1)} %bitcast.79), calls=%async_computation.8 | async-start | bytes 8388608
  465.3 29.8 %slice-start.2 = ((s8[4718592]{0:T(1024)(128)(4,1)}), s8[4194304]{0:T(1024)(128)(4,1)S(1)}, s32[]{:S(2)}) async-start(s8[4718592]{0:T(1024)(128)(4,1)} %bitcast.81), calls=%async_computation.10 | async-start | bytes 8388608
  481.6 13.6 %slice-start.3 = ((s8[4718592]{0:T(1024)(128)(4,1)}), s8[524288]{0:T(1024)(128)(4,1)S(1)}, s32[]{:S(2)}) async-start(s8[4718592]{0:T(1024)(128)(4,1)} %bitcast.81), calls=%async_computation.11 | async-start | bytes 1048576
  (21 other events, 104.9 us)
Sparse Core Ops, SparseCore 0:
  133.9 67.7 all-gather.2
  203.5 63.8 all-gather.4
  270.9 82.2 reduce-scatter.2
  356.5 82.2 reduce-scatter.4

commit v8 on v7

--- a/solution.py
+++ b/solution.py
@@ -244,7 +244,7 @@
 
 
 def attention_backward(
-    query, keyval, key_bias, mixed, grad, log_total, features, block, exchanged, known, bands
+    query, keyval, key_bias, mixed, grad, log_total, features, block, exchanged, bands
 ):
     rows, length = query.shape[0], keyval.shape[0]
     shared = exchanged is not None
@@ -256,8 +256,7 @@
     params = pltpu.CompilerParams(vmem_limit_bytes=56 * 2**20)
     if shared:
 
-        def shared_kernel(both_ref, bias_ref, mixed_ref, grad_ref, log_ref, rows_ref, known_ref, out_ref, back_ref, kept_ref, *held):
-            kept_ref[...] = known_ref[...]
+        def shared_kernel(both_ref, bias_ref, mixed_ref, grad_ref, log_ref, rows_ref, out_ref, back_ref, *held):
             finish = exchange_rows(rows_ref, back_ref, *held[3:], bands=bands)
             attention_backward_kernel(
                 both_ref, both_ref, bias_ref, mixed_ref, grad_ref, log_ref, out_ref, out_ref, *held[:3],
@@ -271,10 +270,9 @@
             out_shape=(
                 jax.ShapeDtypeStruct((rows, 3 * features), jnp.bfloat16),
                 jax.ShapeDtypeStruct((bands, rows // bands, features), jnp.bfloat16),
-                jax.ShapeDtypeStruct(known.shape, jnp.float32),
             ),
-            in_specs=[vmem] * 5 + [anywhere, vmem],
-            out_specs=(vmem, anywhere, vmem),
+            in_specs=[vmem] * 5 + [anywhere],
+            out_specs=(vmem, anywhere),
             scratch_shapes=scratch
             + [
                 pltpu.SemaphoreType.DMA((bands,)),
@@ -285,7 +283,7 @@
             compiler_params=pltpu.CompilerParams(
                 collective_id=2, has_side_effects=True, vmem_limit_bytes=56 * 2**20
             ),
-        )(query, key_bias, mixed, grad, log_total, exchanged, known)
+        )(query, key_bias, mixed, grad, log_total, exchanged)
     return pl.pallas_call(
         functools.partial(
             attention_backward_kernel, features=features, shift=0, out_shift=0, block=block
@@ -1192,12 +1190,12 @@
     attention_grads = [
         attention_backward(
             queries[i], keys_values[i], key_bias[i], mixed_parts[i], mixed_grad[i], log_total[i],
-            features, 512, output_low[i] if hosted else None, tall_squares, band_count,
+            features, 512, output_low[i] if hosted else None, band_count,
         )
         for i in range(own)
     ]
     if hosted:
-        output, tall_squares = attention_grads[0][1:]
+        output = attention_grads[0][1]
     else:
         output = to_bands(output_low)
     if split > 1:
@@ -1217,7 +1215,7 @@
         qkv_grad = jnp.stack([jnp.concatenate(pair, axis=-1) for pair in attention_grads])
     qkv_sums = jnp.sum(qkv_grad.astype(jnp.float32), axis=(0, 1))
     qkv_weight_grad = jnp.einsum(
-        "ire,ird->ed", qkv_grad, first_in, preferred_element_type=jnp.float32
+        "ire,ird->ed", after(qkv_grad, tall_shard), first_in, preferred_element_type=jnp.float32
     ).astype(low_type)
     first_grad = jnp.einsum("ire,ed->ird", after(qkv_grad, qkv_weight_grad), qkv_full, preferred_element_type=jnp.float32)
     shift_one_grad = jnp.sum(first_grad, axis=1)

time: 657 us -> 655 us (level)
  waiting for transfers between devices: 25.6 us -> 9.68 us
  Pallas kernels: 343 us -> 358 us
    reduce_scatter x1, waiting for transfers between devices: 16 us -> 0.02 us  [body(): lax.psum_scatter(down_grad, 'img', scatter_dimension=0, tiled=True)]
    pallas_call x1, Pallas kernels: 117 us -> 130 us  [tail_exchange(): pl.pallas_call(functools.partial(tail_kernel, imgs=imgs, bands=bands), ou...]
    unnamed x96 -> x94, local copies, waits for them, and re-layouts: 16.5 us -> 16.5 us
  transfers between devices with their start and end apart: 6 -> 6, of which waited for: 2 -> 1; matrix products, arithmetic and copies ran while one was open for 35% -> 34% of each run, Pallas kernels for 15% -> 15%
where the time goes in v8:
time: 655 us; the launch traced here: 652 us
  Pallas kernels  358 us (55%)
  matrix products  195 us (30%)
  other arithmetic  32.6 us (5%)
  local copies, waits for them, and re-layouts  24.8 us (4%)
  between operations  16.9 us (3%)
  starting transfers between devices  13.9 us (2%)
  waiting for transfers between devices  9.68 us (1%)
    pallas_call x1, Pallas kernels, tail_exchange(): pl.pallas_call(functools.partial(tail_kernel, imgs=imgs, bands=bands), ou...  130 us
    pallas_call x1, Pallas kernels, start_exchange(): pl.pallas_call(functools.partial(start_kernel, imgs=imgs, bands=bands, qk...  118 us
    pallas_call x1, Pallas kernels, attention_backward(): pl.pallas_call(shared_kernel, out_shape=(jax.ShapeDtypeStruct((rows, 3 *...  62.3 us
    pallas_call x1, Pallas kernels, attention_forward(): pl.pallas_call(functools.partial(attention_forward_kernel, features=featu...  36.9 us
    dot_general x1, matrix products, body(): jnp.einsum('ird,df->irf', after(branch_grad, down_grad), down_full, prefe...  26.9 us
    dot_general x1, matrix products, body(): jnp.einsum('irf,df->ird', hidden_low, down_full, preferred_element_type=j...  24.2 us
    dot_general x1, matrix products, body(): jnp.einsum('irf,fd->ird', after(pre_grad, up_grad), up_full, preferred_el...  21.2 us
    dot_general x1, matrix products, body(): jnp.einsum('ird,fd->irf', second_in, up_full, preferred_element_type=jnp....  20.8 us
  transfers between devices with their start and end apart: 6, of which 1 were waited for; matrix products, arithmetic and copies ran while one was open for 34% of the time, Pallas kernels for 15%

profile of v8, /device:TPU:0, one launch (start us, length us, event | category | flops | bytes accessed | tf_op | source)
XLA Modules:
  0.0 651.6 jit_solution(1103683715286675717)
XLA Ops:
  15.3 118.5 %shard_map.381 = (bf16[3456,1152]{1,0:T(8,128)(2,1)}, bf16[1152,1152]{1,0:T(8,128)(2,1)}, bf16[576,1152]{1,0:T(8,128)(2,1)}, bf16[144,4608]{1,0:T(8,128)(2,1)}, ...) custom-call(bf16[288,1152]{1,0:T(8,128)(2,1)S(1)} %concatenate.29.wide, ...), custom_call_target="tpu_custom_call" | custom-call | bytes 368000000 | tf_op jit(solution)/shard_map/pallas_call | solution.py:553
  134.6 8.2 %all-to-all-start = ((bf16[4,256,1152]{2,1,0:T(8,128)(2,1)}), bf16[4,256,1152]{2,1,0:T(8,128)(2,1)}, u32[]{:S(2)}, u32[]{:S(2)}) async-start(bf16[4,256,1152]{2,1,0:T(8,128)(2,1)} %param.25), calls=%async_computation | async-start | bytes 4718592 | tf_op jit(solution)/shard_map/all_to_all | solution.py:1022
  147.7 15.4 %add_convert_fusion.query_ref.keyval_ref.both_ref = bf16[1024,3456]{1,0:T(8,128)(2,1)} fusion(bf16[3456,1152]{1,0:T(8,128)(2,1)} %get-tuple-element.67, f32[3456]{0:T(1024)S(1)} %pad_maximum_fusion.1, bf16[1024,1152]{1,0:T(8,128)(2,1)S(1)} %copy-done.9, f32[1152]{0:T(1024)S(1)} %get-tuple-element.210, f32[1152]{0:T(1024)S(1)} %get-tuple-element.211, ...), kind=kOutput, calls=%fused_computation.15 | convolution fusion | flops 8167882752 | bytes 17431040 | tf_op jit(solution)/shard_map/ird,ed->ire/dot_general | solution.py:1114
  163.1 36.9 %shard_map.382 = (bf16[1024,1152]{1,0:T(8,128)(2,1)}, f32[16,1024]{1,0:T(8,128)}) custom-call(bf16[1024,3456]{1,0:T(8,128)(2,1)} %add_convert_fusion.query_ref.keyval_ref.both_ref, bf16[1024,3456]{1,0:T(8,128)(2,1)} %add_convert_fusion.query_ref.keyval_ref.both_ref, f32[1024,1]{1,0:T(8,128)} %fusion.34.bias_ref), custom_call_target="tpu_custom_call" | custom-call | bytes 118400000 | tf_op jit(solution)/shard_map/pallas_call | solution.py:127
  200.6 7.5 %fusion.43 = (f32[1024]{0:T(1024)S(1)}, f32[1024,1152]{1,0:T(8,128)S(1)}, f32[1024,1152]{1,0:T(8,128)}) fusion(f32[1152]{0:T(1024)S(1)} %get-tuple-element.209, bf16[1024,1152]{1,0:T(8,128)(2,1)S(1)} %copy-done.9, f32[1152]{0:T(1024)S(1)} %add.180, bf16[1024,1152]{1,0:T(8,128)(2,1)} %get-tuple-element.68.mixed_ref, bf16[1152,1152]{1,0:T(8,128)(2,1)S(1)} %copy-done.27), kind=kOutput, calls=%fused_computation.111 | convolution fusion | flops 2723806208 | bytes 16823296 | tf_op jit(solution)/shard_map/ird,ed->ire/dot_general | solution.py:1136
  213.5 20.8 %fusion.41 = f32[1024,4608]{1,0:T(8,128)} fusion(bf16[4608,1152]{1,0:T(8,128)(2,1)} %all-gather.3.cloned.1.call-done, f32[1024,1152]{1,0:T(8,128)} %copy-done.11, f32[1152]{0:T(1024)S(1)} %get-tuple-element.207, f32[1152]{0:T(1024)S(1)} %get-tuple-element.208, f32[1024]{0:T(1024)S(1)} %add_rsqrt_fusion, f32[1024]{0:T(1024)S(1)} %broadcast_multiply_fusion.4), kind=kOutput, calls=%fused_computation.110 | convolution fusion | flops 10877534208 | bytes 34227200 | tf_op jit(solution)/shard_map/ird,fd->irf/dot_general | solution.py:1142
  234.4 19.2 %convolution_convert_fusion.1 = bf16[1152,4608]{1,0:T(8,128)(2,1)} fusion(bf16[1024,1152]{1,0:T(8,128)(2,1)S(1)} %multiply_convert_fusion.2, f32[1024,4608]{1,0:T(8,128)} %fusion.41, f32[4608]{0:T(1024)S(1)} %add.190), kind=kOutput, calls=%fused_computation.3 | convolution fusion | flops 10924130304 | bytes 31868928 | tf_op jit(solution)/shard_map/ird,irf->df/dot_general | solution.py:1154
  258.5 8.9 %all-gather.5.cloned.1.call-done = bf16[1152,4608]{1,0:T(8,128)(2,1)} async-done(((bf16[144,4608]{1,0:T(8,128)(2,1)}), bf16[1152,4608]{1,0:T(8,128)(2,1)}) %all-gather.5.cloned.1.call-update) | async-done | bytes 10616848 | tf_op jit(solution)/shard_map/all_gather | solution.py:1088
  267.4 26.9 %convert_reduce_fusion = (f32[4608]{0:T(1024)S(1)}, bf16[1024,4608]{1,0:T(8,128)(2,1)S(1)}) fusion(f32[1024,4608]{1,0:T(8,128)} %fusion.41, f32[4608]{0:T(1024)S(1)} %add.190, bf16[1152,4608]{1,0:T(8,128)(2,1)} %all-gather.5.cloned.1.call-done, bf16[1,1024,1152]{2,1,0:T(8,128)(2,1)S(1)} %get-tuple-element.71), kind=kOutput, calls=%fused_computation.11 | convolution fusion | flops 10980159488 | bytes 41324544 | tf_op jit(solution)/shard_map/ird,df->irf/dot_general | solution.py:1158
  294.4 3.9 copy-done.30
  298.3 18.1 %convolution_convert_fusion = bf16[4608,1152]{1,0:T(8,128)(2,1)} fusion(bf16[1024,4608]{1,0:T(8,128)(2,1)S(1)} %get-tuple-element.232, f32[1024,1152]{1,0:T(8,128)} %copy-done.11, f32[1152]{0:T(1024)S(1)} %get-tuple-element.207, f32[1152]{0:T(1024)S(1)} %get-tuple-element.208, f32[1024]{0:T(1024)S(1)} %add_rsqrt_fusion, f32[1024]{0:T(1024)S(1)} %broadcast_multiply_fusion.4), kind=kOutput, calls=%fused_computation.2 | convolution fusion | flops 10882842624 | bytes 24790016 | tf_op jit(solution)/shard_map/irf,ird->fd/dot_general | solution.py:1165
  316.5 21.2 %multiply_reduce_fusion.1 = (f32[1152]{0:T(1024)S(1)}, f32[1024]{0:T(1024)S(1)}, f32[1024]{0:T(1024)S(1)}, f32[1152]{0:T(1024)S(1)}, f32[1024,1152]{1,0:T(8,128)}) fusion(f32[1024,1152]{1,0:T(8,128)} %copy-done.11, f32[1024]{0:T(1024)S(1)} %add_rsqrt_fusion, f32[1024]{0:T(1024)S(1)} %broadcast_multiply_fusion.4, f32[1152]{0:T(1024)S(1)} %get-tuple-element.208, ...), kind=kOutput, calls=%fused_computation.48 | convolution fusion | flops 10882248704 | bytes 29521408 | tf_op jit(solution)/shard_map/irf,fd->ird/dot_general | solution.py:1169
  337.7 24.2 %multiply_reduce_fusion = (f32[1152]{0:T(1024)S(1)}, bf16[1024,1152]{1,0:T(8,128)(2,1)}, f32[1152]{0:T(1024)S(1)}, bf16[1024,1152]{1,0:T(8,128)(2,1)}, f32[1024,1152]{1,0:T(8,128)}) fusion(bf16[4,256,1152]{2,1,0:T(8,128)(2,1)} %all-to-all-done, f32[1024]{0:T(1024)S(1)} %fusion.38, f32[1024,1152]{1,0:T(8,128)} %copy-done.11, ...), kind=kOutput, calls=%fused_computation.47 | convolution fusion | flops 10942412800 | bytes 50791424 | tf_op jit(solution)/shard_map/irf,df->ird/dot_general | solution.py:1148
  365.4 4.9 all-to-all-start.1
  370.3 7.1 %convolution_convert_fusion.3.out_ref = bf16[1152,1152]{1,0:T(8,128)(2,1)} fusion(bf16[1024,1152]{1,0:T(8,128)(2,1)} %get-tuple-element.222, bf16[1024,1152]{1,0:T(8,128)(2,1)S(1)} %copy-done.12), kind=kOutput, calls=%fused_computation.18 | convolution fusion | flops 2719236096 | bytes 7372800 | tf_op jit(solution)/shard_map/ire,ird->ed/dot_general | solution.py:1177
  377.4 4.7 convolution_convert_fusion.4.grad_ref
  382.1 62.3 %shard_map.383 = (bf16[1024,3456]{1,0:T(8,128)(2,1)}, bf16[4,256,1152]{2,1,0:T(8,128)(2,1)}) custom-call(bf16[1024,3456]{1,0:T(8,128)(2,1)} %add_convert_fusion.query_ref.keyval_ref.both_ref, f32[1024,1]{1,0:T(8,128)} %fusion.34.bias_ref, bf16[1024,1152]{1,0:T(8,128)(2,1)} %get-tuple-element.68.mixed_ref, ...), custom_call_target="tpu_custom_call" | custom-call | bytes 182400000 | tf_op jit(solution)/shard_map/pallas_call | solution.py:268
  444.5 4.2 convert_reduce_fusion.1
  451.5 16.4 %convolution_convert_fusion.2.qkv_ref = bf16[3456,1152]{1,0:T(8,128)(2,1)} fusion(bf16[1,1024,3456]{2,1,0:T(8,128)(2,1)} %bitcast.80, bf16[1024,1152]{1,0:T(8,128)(2,1)S(1)} %copy-done.10, f32[1152]{0:T(1024)S(1)} %copy-done.24, f32[1152]{0:T(1024)S(1)} %copy-done.19, f32[1024]{0:T(1024)S(1)} %copy-done.22, f32[1024]{0:T(1024)S(1)} %copy-done.17), kind=kOutput, calls=%fused_computation.13 | convolution fusion | flops 8164786176 | bytes 17417216 | tf_op jit(solution)/shard_map/ire,ird->ed/dot_general | solution.py:1217
  468.0 13.5 %fusion.25 = (f32[1152]{0:T(1024)S(1)}, f32[1024]{0:T(1024)S(1)}, f32[1024]{0:T(1024)S(1)}, f32[1152]{0:T(1024)S(1)}, f32[1024,1152]{1,0:T(8,128)S(1)}) fusion(bf16[1024,1152]{1,0:T(8,128)(2,1)S(1)} %copy-done.10, f32[1024]{0:T(1024)S(1)} %copy-done.22, f32[1024]{0:T(1024)S(1)} %copy-done.17, f32[1152]{0:T(1024)S(1)} %copy-done.19, ...), kind=kOutput, calls=%fused_computation.39 | convolution fusion | flops 8165519360 | bytes 22148608 | tf_op jit(solution)/shard_map/ire,ed->ird/dot_general | solution.py:1220
  481.6 3.3 multiply_reduce_fusion.2
  489.7 129.7 %shard_map.384 = (f32[288,1152]{1,0:T(8,128)S(1)}, bf16[4,256,1152]{2,1,0:T(8,128)(2,1)}, f32[288,864]{1,0:T(8,128)S(1)}, f32[14,144]{1,0:T(8,128)S(1)}, f32[8,128]{1,0:T(8,128)S(1)}) custom-call(bf16[3456,1152]{1,0:T(8,128)(2,1)} %convolution_convert_fusion.2.qkv_ref, bf16[1152,1152]{1,0:T(8,128)(2,1)} %convolution_convert_fusion.3.out_ref, ...), custom_call_target="tpu_custom_call" | custom-call | bytes 352000000 | tf_op jit(solution)/shard_map/pallas_call | solution.py:885
  622.7 4.2 convert_element_type.179
  626.9 11.0 %shard_map.385 = (f32[288,864]{1,0:T(8,128)}, f32[288,864]{1,0:T(8,128)}, f32[288,864]{1,0:T(8,128)}, f32[288,432]{1,0:T(8,128)}, f32[288,432]{1,0:T(8,128)}, /*...) custom-call(f32[8,128]{1,0:T(8,128)S(1)} %get-tuple-element.83.refs_, ...), custom_call_target="tpu_custom_call" | custom-call | tf_op jit(solution)/shard_map/pallas_call | solution.py:969
  (188 shorter events, 43.5 us)
Async XLA Ops:
  7.2 206.3 %all-gather.3.cloned.1.call-start = ((), (), s32[]{:S(2)}) async-start(), calls=%async_computation.4 | async-start | bytes 11943936 | tf_op jit(solution)/shard_map/all_gather | solution.py:1087
  133.8 10.5 %copy-start.29 = (s32[4]{0:T(128)S(1)}, s32[4]{0:T(128)}, u32[]{:S(2)}) copy-start(s32[4]{0:T(128)} %param.24) | copy-start | bytes 52
  133.8 12.7 %copy-start.9 = (bf16[1024,1152]{1,0:T(8,128)(2,1)S(1)}, bf16[1024,1152]{1,0:T(8,128)(2,1)}, u32[]{:S(2)}) copy-start(bf16[1024,1152]{1,0:T(8,128)(2,1)} %get-tuple-element.64) | copy-start | bytes 7077892
  133.8 133.6 %all-gather.5.cloned.1.call-start = ((), (), s32[]{:S(2)}) async-start(), calls=%async_computation.5 | async-start | bytes 11943936 | tf_op jit(solution)/shard_map/all_gather | solution.py:1088
  134.6 76.4 %all-to-all-start = ((bf16[4,256,1152]{2,1,0:T(8,128)(2,1)}), bf16[4,256,1152]{2,1,0:T(8,128)(2,1)}, u32[]{:S(2)}, u32[]{:S(2)}) async-start(bf16[4,256,1152]{2,1,0:T(8,128)(2,1)} %param.25), calls=%async_computation | async-start | bytes 4718592 | tf_op jit(solution)/shard_map/all_to_all | solution.py:1022
  142.8 219.7 %reduce-scatter.3.cloned.1.call-start = ((), (), s32[]{:S(2)}) async-start(), calls=%async_computation.6 | async-start | bytes 11943936 | tf_op jit(solution)/shard_map/reduce_scatter | solution.py:1157
  144.9 18.1 %copy-start.18 = (f32[1152]{0:T(1024)}, f32[1152]{0:T(1024)S(1)}, u32[]{:S(2)}) copy-start(f32[1152]{0:T(1024)S(1)} %get-tuple-element.211) | copy-start | bytes 13828
  145.0 18.1 %copy-start.23 = (f32[1152]{0:T(1024)}, f32[1152]{0:T(1024)S(1)}, u32[]{:S(2)}) copy-start(f32[1152]{0:T(1024)S(1)} %get-tuple-element.210) | copy-start | bytes 13828
  145.0 55.7 %copy-start.25 = (f32[1152]{0:T(1024)}, f32[1152]{0:T(1024)S(1)}, u32[]{:S(2)}) copy-start(f32[1152]{0:T(1024)S(1)} %get-tuple-element.209) | copy-start | bytes 13828
  146.9 16.2 %copy-start.16 = (f32[1024]{0:T(1024)}, f32[1024]{0:T(1024)S(1)}, u32[]{:S(2)}) copy-start(f32[1024]{0:T(1024)S(1)} %broadcast_multiply_fusion.5) | copy-start | bytes 12292
  147.7 15.4 %copy-start.21 = (f32[1024]{0:T(1024)}, f32[1024]{0:T(1024)S(1)}, u32[]{:S(2)}) copy-start(f32[1024]{0:T(1024)S(1)} %add_rsqrt_fusion.1) | copy-start | bytes 12292
  163.1 37.5 %copy-start.27 = (bf16[1152,1152]{1,0:T(8,128)(2,1)S(1)}, bf16[1152,1152]{1,0:T(8,128)(2,1)}, u32[]{:S(2)}) copy-start(bf16[1152,1152]{1,0:T(8,128)(2,1)} %get-tuple-element.69) | copy-start | bytes 7962628
  253.6 234.1 %reduce-scatter.5.cloned.1.call-start = ((), (), s32[]{:S(2)}) async-start(), calls=%async_computation.7 | async-start | bytes 11943936 | tf_op jit(solution)/shard_map/reduce_scatter | solution.py:1168
  316.4 21.2 %copy-start.26 = (f32[1152]{0:T(1024)S(1)}, f32[1152]{0:T(1024)}, u32[]{:S(2)}) copy-start(f32[1152]{0:T(1024)} %copy-done.25) | copy-start | bytes 13828
  361.9 8.4 %copy-start.12 = (bf16[1024,1152]{1,0:T(8,128)(2,1)S(1)}, bf16[1024,1152]{1,0:T(8,128)(2,1)}, u32[]{:S(2)}) copy-start(bf16[1024,1152]{1,0:T(8,128)(2,1)} %get-tuple-element.68.mixed_ref) | copy-start | bytes 7077892
  365.4 83.5 %all-to-all-start.1 = ((bf16[4,144,1152]{2,1,0:T(8,128)(2,1)}), bf16[4,144,1152]{2,1,0:T(8,128)(2,1)}, u32[]{:S(2)}, u32[]{:S(2)}) async-start(bf16[4,144,1152]{2,1,0:T(8,128)(2,1)} %bitcast.76), calls=%async_computation.2 | async-start | bytes 2654208 | tf_op jit(solution)/shard_map/all_to_all | solution.py:1185
  370.3 7.1 %copy-start.28 = (bf16[1152,1152]{1,0:T(8,128)(2,1)S(1)}, bf16[1152,1152]{1,0:T(8,128)(2,1)}, u32[]{:S(2)}) copy-start(bf16[1152,1152]{1,0:T(8,128)(2,1)} %get-tuple-element.69) | copy-start | bytes 7962628
  370.3 7.1 %copy-start.31 = (bf16[1024,1152]{1,0:T(8,128)(2,1)S(1)}, bf16[1024,1152]{1,0:T(8,128)(2,1)}, u32[]{:S(2)}) copy-start(bf16[1024,1152]{1,0:T(8,128)(2,1)} %get-tuple-element.222) | copy-start | bytes 7077892
  448.9 19.1 %slice-start = ((s8[7077888]{0:T(1024)(128)(4,1)}), s8[4194304]{0:T(1024)(128)(4,1)S(1)}, s32[]{:S(2)}) async-start(s8[7077888]{0:T(1024)(128)(4,1)} %bitcast.81), calls=%async_computation.8 | async-start | bytes 8388608
  451.5 16.5 %slice-start.1 = ((s8[7077888]{0:T(1024)(128)(4,1)}), s8[2883584]{0:T(1024)(128)(4,1)S(1)}, s32[]{:S(2)}) async-start(s8[7077888]{0:T(1024)(128)(4,1)} %bitcast.81), calls=%async_computation.9 | async-start | bytes 5767168
  451.5 30.1 %slice-start.2 = ((s8[4718592]{0:T(1024)(128)(4,1)}), s8[4194304]{0:T(1024)(128)(4,1)S(1)}, s32[]{:S(2)}) async-start(s8[4718592]{0:T(1024)(128)(4,1)} %bitcast.84), calls=%async_computation.10 | async-start | bytes 8388608
  451.5 30.1 %slice-start.4 = ((s8[4718592]{0:T(1024)(128)(4,1)}), s8[4194304]{0:T(1024)(128)(4,1)S(1)}, s32[]{:S(2)}) async-start(s8[4718592]{0:T(1024)(128)(4,1)} %bitcast.86), calls=%async_computation.12 | async-start | bytes 8388608
  468.0 13.6 %slice-start.3 = ((s8[4718592]{0:T(1024)(128)(4,1)}), s8[524288]{0:T(1024)(128)(4,1)S(1)}, s32[]{:S(2)}) async-start(s8[4718592]{0:T(1024)(128)(4,1)} %bitcast.84), calls=%async_computation.11 | async-start | bytes 1048576
  468.0 13.6 %slice-start.5 = ((s8[4718592]{0:T(1024)(128)(4,1)}), s8[524288]{0:T(1024)(128)(4,1)S(1)}, s32[]{:S(2)}) async-start(s8[4718592]{0:T(1024)(128)(4,1)} %bitcast.86), calls=%async_computation.13 | async-start | bytes 1048576
  (20 other events, 84.2 us)
Sparse Core Ops, SparseCore 0:
  133.9 67.7 all-gather.2
  203.6 63.8 all-gather.4
  270.9 82.2 reduce-scatter.2
  356.5 82.2 reduce-scatter.4

commit v9 on v7

--- a/solution.py
+++ b/solution.py
@@ -762,6 +762,8 @@
         small_copy(view, view, kind, step, axis, lax.rem(me + count - step, count)).wait_recv()
 
     order = (3, 1, 2, 0)
+    for step in range(1, bands):
+        row_copy(step).start()
     for step in range(1, imgs):
         piece_flat(step).start()
     keep_piece = pltpu.make_async_copy(pieces_ref.at[img], pieces.at[band, img], local_sem.at[9])
@@ -777,8 +779,6 @@
     turned[pl.ds(both, width - both), :] = up_ref[...]
     pl.loop(first // lanes, width // lanes)(turn)
     line_ends(1)
-    for step in range(1, bands):
-        row_copy(step).start()
     for at in order:
         for kind in range(2):
             own_copy(kind, at).wait()

time: 657 us -> 655 us (level)
  no operation moved by 1% of the time
where the time goes in v9:
time: 655 us; the launch traced here: 652 us
  Pallas kernels  342 us (52%)
  matrix products  199 us (30%)
  other arithmetic  30.8 us (5%)
  waiting for transfers between devices  25.6 us (4%)
  local copies, waits for them, and re-layouts  25 us (4%)
  between operations  16.9 us (3%)
  starting transfers between devices  13.7 us (2%)
    pallas_call x1, Pallas kernels, start_exchange(): pl.pallas_call(functools.partial(start_kernel, imgs=imgs, bands=bands, qk...  118 us
    pallas_call x1, Pallas kernels, tail_exchange(): pl.pallas_call(functools.partial(tail_kernel, imgs=imgs, bands=bands), ou...  115 us
    pallas_call x1, Pallas kernels, attention_backward(): pl.pallas_call(shared_kernel, out_shape=(jax.ShapeDtypeStruct((rows, 3 *...  60.6 us
    pallas_call x1, Pallas kernels, attention_forward(): pl.pallas_call(functools.partial(attention_forward_kernel, features=featu...  36.9 us
    dot_general x1, matrix products, body(): jnp.einsum('irf,df->ird', hidden_low, down_full, preferred_element_type=j...  28.1 us
    dot_general x1, matrix products, body(): jnp.einsum('ird,df->irf', after(branch_grad, down_grad), down_full, prefe...  27 us
    dot_general x1, matrix products, body(): jnp.einsum('ird,fd->irf', second_in, up_full, preferred_element_type=jnp....  21.1 us
    dot_general x1, matrix products, body(): jnp.einsum('irf,fd->ird', after(pre_grad, up_grad), up_full, preferred_el...  20.8 us
  transfers between devices with their start and end apart: 6, of which 2 were waited for; matrix products, arithmetic and copies ran while one was open for 35% of the time, Pallas kernels for 15%

profile of v9, /device:TPU:0, one launch (start us, length us, event | category | flops | bytes accessed | tf_op | source)
XLA Modules:
  0.0 652.1 jit_solution(533367004879588176)
XLA Ops:
  15.3 118.4 %shard_map.381 = (bf16[3456,1152]{1,0:T(8,128)(2,1)}, bf16[1152,1152]{1,0:T(8,128)(2,1)}, bf16[576,1152]{1,0:T(8,128)(2,1)}, bf16[144,4608]{1,0:T(8,128)(2,1)}, ...) custom-call(bf16[288,1152]{1,0:T(8,128)(2,1)S(1)} %concatenate.29.wide, ...), custom_call_target="tpu_custom_call" | custom-call | bytes 368000000 | tf_op jit(solution)/shard_map/pallas_call | solution.py:555
  134.5 8.2 %all-to-all-start = ((bf16[4,256,1152]{2,1,0:T(8,128)(2,1)}), bf16[4,256,1152]{2,1,0:T(8,128)(2,1)}, u32[]{:S(2)}, u32[]{:S(2)}) async-start(bf16[4,256,1152]{2,1,0:T(8,128)(2,1)} %param.25), calls=%async_computation | async-start | bytes 4718592 | tf_op jit(solution)/shard_map/all_to_all | solution.py:1024
  147.3 15.5 %add_convert_fusion.query_ref.keyval_ref.both_ref = bf16[1024,3456]{1,0:T(8,128)(2,1)} fusion(bf16[3456,1152]{1,0:T(8,128)(2,1)} %get-tuple-element.67, f32[3456]{0:T(1024)S(1)} %pad_maximum_fusion.1, bf16[1024,1152]{1,0:T(8,128)(2,1)S(1)} %copy-done.10, f32[1152]{0:T(1024)S(1)} %get-tuple-element.210, f32[1152]{0:T(1024)S(1)} %get-tuple-element.211, ...), kind=kOutput, calls=%fused_computation.15 | convolution fusion | flops 8167882752 | bytes 17431040 | tf_op jit(solution)/shard_map/ird,ed->ire/dot_general | solution.py:1116
  162.8 36.9 %shard_map.382 = (bf16[1024,1152]{1,0:T(8,128)(2,1)}, f32[16,1024]{1,0:T(8,128)}) custom-call(bf16[1024,3456]{1,0:T(8,128)(2,1)} %add_convert_fusion.query_ref.keyval_ref.both_ref, bf16[1024,3456]{1,0:T(8,128)(2,1)} %add_convert_fusion.query_ref.keyval_ref.both_ref, f32[1024,1]{1,0:T(8,128)} %fusion.33.bias_ref), custom_call_target="tpu_custom_call" | custom-call | bytes 118400000 | tf_op jit(solution)/shard_map/pallas_call | solution.py:127
  200.3 7.5 %fusion.42 = (f32[1024]{0:T(1024)S(1)}, f32[1024,1152]{1,0:T(8,128)S(1)}, f32[1024,1152]{1,0:T(8,128)}) fusion(f32[1152]{0:T(1024)S(1)} %get-tuple-element.209, bf16[1024,1152]{1,0:T(8,128)(2,1)S(1)} %copy-done.10, f32[1152]{0:T(1024)S(1)} %add.180, bf16[1024,1152]{1,0:T(8,128)(2,1)} %get-tuple-element.68.mixed_ref, bf16[1152,1152]{1,0:T(8,128)(2,1)S(1)} %copy-done.30), kind=kOutput, calls=%fused_computation.110 | convolution fusion | flops 2723806208 | bytes 16823296 | tf_op jit(solution)/shard_map/ird,ed->ire/dot_general | solution.py:1138
  213.3 21.1 %fusion.40 = f32[1024,4608]{1,0:T(8,128)} fusion(bf16[4608,1152]{1,0:T(8,128)(2,1)} %all-gather.3.cloned.1.call-done, f32[1024,1152]{1,0:T(8,128)} %copy-done.14, f32[1152]{0:T(1024)S(1)} %get-tuple-element.207, f32[1152]{0:T(1024)S(1)} %get-tuple-element.208, f32[1024]{0:T(1024)S(1)} %add_rsqrt_fusion, f32[1024]{0:T(1024)S(1)} %broadcast_multiply_fusion.4), kind=kOutput, calls=%fused_computation.109 | convolution fusion | flops 10877534208 | bytes 34227200 | tf_op jit(solution)/shard_map/ird,fd->irf/dot_general | solution.py:1144
  234.4 19.3 %convolution_convert_fusion.1 = bf16[1152,4608]{1,0:T(8,128)(2,1)} fusion(bf16[1024,1152]{1,0:T(8,128)(2,1)S(1)} %multiply_convert_fusion.2, f32[1024,4608]{1,0:T(8,128)} %fusion.40, f32[4608]{0:T(1024)S(1)} %add.190), kind=kOutput, calls=%fused_computation.3 | convolution fusion | flops 10924130304 | bytes 31868928 | tf_op jit(solution)/shard_map/ird,irf->df/dot_general | solution.py:1156
  258.6 8.8 %all-gather.5.cloned.1.call-done = bf16[1152,4608]{1,0:T(8,128)(2,1)} async-done(((bf16[144,4608]{1,0:T(8,128)(2,1)}), bf16[1152,4608]{1,0:T(8,128)(2,1)}) %all-gather.5.cloned.1.call-update) | async-done | bytes 10616848 | tf_op jit(solution)/shard_map/all_gather | solution.py:1090
  267.4 27.0 %convert_reduce_fusion = (f32[4608]{0:T(1024)S(1)}, bf16[1024,4608]{1,0:T(8,128)(2,1)S(1)}) fusion(f32[1024,4608]{1,0:T(8,128)} %fusion.40, f32[4608]{0:T(1024)S(1)} %add.190, bf16[1152,4608]{1,0:T(8,128)(2,1)} %all-gather.5.cloned.1.call-done, bf16[1,1024,1152]{2,1,0:T(8,128)(2,1)S(1)} %get-tuple-element.71), kind=kOutput, calls=%fused_computation.11 | convolution fusion | flops 10980159488 | bytes 41324544 | tf_op jit(solution)/shard_map/ird,df->irf/dot_general | solution.py:1160
  294.4 3.9 copy-done.33
  298.3 18.1 %convolution_convert_fusion = bf16[4608,1152]{1,0:T(8,128)(2,1)} fusion(bf16[1024,4608]{1,0:T(8,128)(2,1)S(1)} %get-tuple-element.232, f32[1024,1152]{1,0:T(8,128)} %copy-done.14, f32[1152]{0:T(1024)S(1)} %get-tuple-element.207, f32[1152]{0:T(1024)S(1)} %get-tuple-element.208, f32[1024]{0:T(1024)S(1)} %add_rsqrt_fusion, f32[1024]{0:T(1024)S(1)} %broadcast_multiply_fusion.4), kind=kOutput, calls=%fused_computation.2 | convolution fusion | flops 10882842624 | bytes 24790016 | tf_op jit(solution)/shard_map/irf,ird->fd/dot_general | solution.py:1167
  316.4 20.8 %multiply_reduce_fusion.1 = (f32[1152]{0:T(1024)S(1)}, f32[1024]{0:T(1024)S(1)}, f32[1024]{0:T(1024)S(1)}, f32[1152]{0:T(1024)S(1)}, f32[1024,1152]{1,0:T(8,128)}) fusion(f32[1024,1152]{1,0:T(8,128)} %copy-done.14, f32[1024]{0:T(1024)S(1)} %add_rsqrt_fusion, f32[1024]{0:T(1024)S(1)} %broadcast_multiply_fusion.4, f32[1152]{0:T(1024)S(1)} %get-tuple-element.208, ...), kind=kOutput, calls=%fused_computation.47 | convolution fusion | flops 10882248704 | bytes 29521408 | tf_op jit(solution)/shard_map/irf,fd->ird/dot_general | solution.py:1171
  337.2 16.0 %reduce-scatter.3.cloned.1.call-done = bf16[144,4608]{1,0:T(8,128)(2,1)} async-done(((bf16[1152,4608]{1,0:T(8,128)(2,1)}), bf16[144,4608]{1,0:T(8,128)(2,1)}) %reduce-scatter.3.cloned.1.call-update) | async-done | bytes 1327120 | tf_op jit(solution)/shard_map/reduce_scatter | solution.py:1159
  355.7 5.0 all-to-all-start.1
  360.7 28.1 %multiply_reduce_fusion = (f32[1152]{0:T(1024)S(1)}, bf16[1024,1152]{1,0:T(8,128)(2,1)}, f32[1152]{0:T(1024)S(1)}, bf16[1024,1152]{1,0:T(8,128)(2,1)}, f32[1024,1152]{1,0:T(8,128)}) fusion(bf16[4,256,1152]{2,1,0:T(8,128)(2,1)} %all-to-all-done, f32[1024]{0:T(1024)S(1)} %fusion.37, f32[1024,1152]{1,0:T(8,128)} %copy-done.14, ...), kind=kOutput, calls=%fused_computation.46 | convolution fusion | flops 10942412800 | bytes 50791424 | tf_op jit(solution)/shard_map/irf,df->ird/dot_general | solution.py:1150
  389.3 6.8 %convolution_convert_fusion.3.out_ref = bf16[1152,1152]{1,0:T(8,128)(2,1)} fusion(bf16[1024,1152]{1,0:T(8,128)(2,1)} %get-tuple-element.222, bf16[1024,1152]{1,0:T(8,128)(2,1)S(1)} %copy-done.15), kind=kOutput, calls=%fused_computation.18 | convolution fusion | flops 2719236096 | bytes 7372800 | tf_op jit(solution)/shard_map/ire,ird->ed/dot_general | solution.py:1179
  396.1 4.7 convolution_convert_fusion.4.grad_ref
  404.6 60.6 %shard_map.383 = (bf16[1024,3456]{1,0:T(8,128)(2,1)}, bf16[4,256,1152]{2,1,0:T(8,128)(2,1)}, f32[8,128]{1,0:T(8,128)}) custom-call(bf16[1024,3456]{1,0:T(8,128)(2,1)} %add_convert_fusion.query_ref.keyval_ref.both_ref, f32[1024,1]{1,0:T(8,128)} %fusion.33.bias_ref, bf16[1024,1152]{1,0:T(8,128)(2,1)} %get-tuple-element.68.mixed_ref, ...), custom_call_target="tpu_custom_call" | custom-call | bytes 182400000 | tf_op jit(solution)/shard_map/pallas_call | solution.py:269
  465.3 16.2 %convolution_convert_fusion.2.qkv_ref = bf16[3456,1152]{1,0:T(8,128)(2,1)} fusion(bf16[1024,3456]{1,0:T(8,128)(2,1)} %get-tuple-element.78, bf16[1024,1152]{1,0:T(8,128)(2,1)S(1)} %copy-done.11, f32[1152]{0:T(1024)S(1)} %copy-done.27, f32[1152]{0:T(1024)S(1)} %copy-done.22, f32[1024]{0:T(1024)S(1)} %copy-done.25, f32[1024]{0:T(1024)S(1)} %copy-done.20), kind=kOutput, calls=%fused_computation.13 | convolution fusion | flops 8164786176 | bytes 17417216 | tf_op jit(solution)/shard_map/ire,ird->ed/dot_general | solution.py:1219
  481.6 13.5 %fusion.24 = (f32[1152]{0:T(1024)S(1)}, f32[1024]{0:T(1024)S(1)}, f32[1024]{0:T(1024)S(1)}, f32[1152]{0:T(1024)S(1)}, f32[1024,1152]{1,0:T(8,128)S(1)}) fusion(bf16[1024,1152]{1,0:T(8,128)(2,1)S(1)} %copy-done.11, f32[1024]{0:T(1024)S(1)} %copy-done.25, f32[1024]{0:T(1024)S(1)} %copy-done.20, f32[1152]{0:T(1024)S(1)} %copy-done.22, ...), kind=kOutput, calls=%fused_computation.38 | convolution fusion | flops 8165519360 | bytes 22148608 | tf_op jit(solution)/shard_map/ire,ed->ird/dot_general | solution.py:1222
  499.0 4.0 convert_reduce_fusion.1
  505.2 114.8 %shard_map.384 = (f32[288,1152]{1,0:T(8,128)S(1)}, bf16[4,256,1152]{2,1,0:T(8,128)(2,1)}, f32[288,864]{1,0:T(8,128)S(1)}, f32[14,144]{1,0:T(8,128)S(1)}, f32[8,128]{1,0:T(8,128)S(1)}) custom-call(bf16[3456,1152]{1,0:T(8,128)(2,1)} %convolution_convert_fusion.2.qkv_ref, bf16[1152,1152]{1,0:T(8,128)(2,1)} %convolution_convert_fusion.3.out_ref, ...), custom_call_target="tpu_custom_call" | custom-call | bytes 352000000 | tf_op jit(solution)/shard_map/pallas_call | solution.py:887
  623.3 4.2 convert_element_type.179
  627.5 11.0 %shard_map.385 = (f32[288,864]{1,0:T(8,128)}, f32[288,864]{1,0:T(8,128)}, f32[288,864]{1,0:T(8,128)}, f32[288,432]{1,0:T(8,128)}, f32[288,432]{1,0:T(8,128)}, /*...) custom-call(f32[8,128]{1,0:T(8,128)S(1)} %get-tuple-element.83.refs_, ...), custom_call_target="tpu_custom_call" | custom-call | tf_op jit(solution)/shard_map/pallas_call | solution.py:971
  (189 shorter events, 45.0 us)
Async XLA Ops:
  7.2 206.1 %all-gather.3.cloned.1.call-start = ((), (), s32[]{:S(2)}) async-start(), calls=%async_computation.4 | async-start | bytes 11943936 | tf_op jit(solution)/shard_map/all_gather | solution.py:1089
  133.7 133.6 %all-gather.5.cloned.1.call-start = ((), (), s32[]{:S(2)}) async-start(), calls=%async_computation.5 | async-start | bytes 11943936 | tf_op jit(solution)/shard_map/all_gather | solution.py:1090
  134.5 76.2 %all-to-all-start = ((bf16[4,256,1152]{2,1,0:T(8,128)(2,1)}), bf16[4,256,1152]{2,1,0:T(8,128)(2,1)}, u32[]{:S(2)}, u32[]{:S(2)}) async-start(bf16[4,256,1152]{2,1,0:T(8,128)(2,1)} %param.25), calls=%async_computation | async-start | bytes 4718592 | tf_op jit(solution)/shard_map/all_to_all | solution.py:1024
  142.7 210.5 %reduce-scatter.3.cloned.1.call-start = ((), (), s32[]{:S(2)}) async-start(), calls=%async_computation.6 | async-start | bytes 11943936 | tf_op jit(solution)/shard_map/reduce_scatter | solution.py:1159
  144.5 18.3 %copy-start.21 = (f32[1152]{0:T(1024)}, f32[1152]{0:T(1024)S(1)}, u32[]{:S(2)}) copy-start(f32[1152]{0:T(1024)S(1)} %get-tuple-element.211) | copy-start | bytes 13828
  144.5 18.3 %copy-start.26 = (f32[1152]{0:T(1024)}, f32[1152]{0:T(1024)S(1)}, u32[]{:S(2)}) copy-start(f32[1152]{0:T(1024)S(1)} %get-tuple-element.210) | copy-start | bytes 13828
  144.6 55.8 %copy-start.28 = (f32[1152]{0:T(1024)}, f32[1152]{0:T(1024)S(1)}, u32[]{:S(2)}) copy-start(f32[1152]{0:T(1024)S(1)} %get-tuple-element.209) | copy-start | bytes 13828
  146.5 16.3 %copy-start.19 = (f32[1024]{0:T(1024)}, f32[1024]{0:T(1024)S(1)}, u32[]{:S(2)}) copy-start(f32[1024]{0:T(1024)S(1)} %broadcast_multiply_fusion.5) | copy-start | bytes 12292
  147.2 15.6 %copy-start.24 = (f32[1024]{0:T(1024)}, f32[1024]{0:T(1024)S(1)}, u32[]{:S(2)}) copy-start(f32[1024]{0:T(1024)S(1)} %add_rsqrt_fusion.1) | copy-start | bytes 12292
  162.8 37.5 %copy-start.30 = (bf16[1152,1152]{1,0:T(8,128)(2,1)S(1)}, bf16[1152,1152]{1,0:T(8,128)(2,1)}, u32[]{:S(2)}) copy-start(bf16[1152,1152]{1,0:T(8,128)(2,1)} %get-tuple-element.69) | copy-start | bytes 7962628
  253.7 250.2 %reduce-scatter.5.cloned.1.call-start = ((), (), s32[]{:S(2)}) async-start(), calls=%async_computation.7 | async-start | bytes 11943936 | tf_op jit(solution)/shard_map/reduce_scatter | solution.py:1170
  337.2 23.5 %copy-start.29 = (f32[1152]{0:T(1024)S(1)}, f32[1152]{0:T(1024)}, u32[]{:S(2)}) copy-start(f32[1152]{0:T(1024)} %copy-done.28) | copy-start | bytes 13828
  355.7 45.1 %all-to-all-start.1 = ((bf16[4,144,1152]{2,1,0:T(8,128)(2,1)}), bf16[4,144,1152]{2,1,0:T(8,128)(2,1)}, u32[]{:S(2)}, u32[]{:S(2)}) async-start(bf16[4,144,1152]{2,1,0:T(8,128)(2,1)} %bitcast.74), calls=%async_computation.2 | async-start | bytes 2654208 | tf_op jit(solution)/shard_map/all_to_all | solution.py:1187
  360.7 28.6 %copy-start.15 = (bf16[1024,1152]{1,0:T(8,128)(2,1)S(1)}, bf16[1024,1152]{1,0:T(8,128)(2,1)}, u32[]{:S(2)}) copy-start(bf16[1024,1152]{1,0:T(8,128)(2,1)} %get-tuple-element.68.mixed_ref) | copy-start | bytes 7077892
  402.6 62.6 %copy-start.13 = (f32[144,1152]{1,0:T(8,128)}, f32[144,1152]{1,0:T(8,128)S(1)}, u32[]{:S(2)}) copy-start(f32[144,1152]{1,0:T(8,128)S(1)} %convert_reduce_fusion.5.refs_2_) | copy-start | bytes 1990660
  404.6 60.6 %copy-start.11 = (bf16[1024,1152]{1,0:T(8,128)(2,1)S(1)}, bf16[1024,1152]{1,0:T(8,128)(2,1)}, u32[]{:S(2)}) copy-start(bf16[1024,1152]{1,0:T(8,128)(2,1)} %get-tuple-element.64) | copy-start | bytes 7077892
  404.6 60.6 %copy-start.20 = (f32[1024]{0:T(1024)S(1)}, f32[1024]{0:T(1024)}, u32[]{:S(2)}) copy-start(f32[1024]{0:T(1024)} %copy-done.19) | copy-start | bytes 12292
  404.6 60.6 %copy-start.22 = (f32[1152]{0:T(1024)S(1)}, f32[1152]{0:T(1024)}, u32[]{:S(2)}) copy-start(f32[1152]{0:T(1024)} %copy-done.21) | copy-start | bytes 13828
  404.6 60.7 %copy-start.25 = (f32[1024]{0:T(1024)S(1)}, f32[1024]{0:T(1024)}, u32[]{:S(2)}) copy-start(f32[1024]{0:T(1024)} %copy-done.24) | copy-start | bytes 12292
  404.6 60.7 %copy-start.27 = (f32[1152]{0:T(1024)S(1)}, f32[1152]{0:T(1024)}, u32[]{:S(2)}) copy-start(f32[1152]{0:T(1024)} %copy-done.26) | copy-start | bytes 13828
  465.3 16.3 %copy-start.12 = (bf16[1024,3456]{1,0:T(8,128)(2,1)S(1)}, bf16[1024,3456]{1,0:T(8,128)(2,1)}, u32[]{:S(2)}) copy-start(bf16[1024,3456]{1,0:T(8,128)(2,1)} %get-tuple-element.78) | copy-start | bytes 21233668
  465.3 29.8 %slice-start = ((s8[4718592]{0:T(1024)(128)(4,1)}), s8[4194304]{0:T(1024)(128)(4,1)S(1)}, s32[]{:S(2)}) async-start(s8[4718592]{0:T(1024)(128)(4,1)} %bitcast.79), calls=%async_computation.8 | async-start | bytes 8388608
  465.3 29.8 %slice-start.2 = ((s8[4718592]{0:T(1024)(128)(4,1)}), s8[4194304]{0:T(1024)(128)(4,1)S(1)}, s32[]{:S(2)}) async-start(s8[4718592]{0:T(1024)(128)(4,1)} %bitcast.81), calls=%async_computation.10 | async-start | bytes 8388608
  481.6 13.6 %slice-start.3 = ((s8[4718592]{0:T(1024)(128)(4,1)}), s8[524288]{0:T(1024)(128)(4,1)S(1)}, s32[]{:S(2)}) async-start(s8[4718592]{0:T(1024)(128)(4,1)} %bitcast.81), calls=%async_computation.11 | async-start | bytes 1048576
  (21 other events, 104.9 us)
Sparse Core Ops, SparseCore 0:
  133.9 67.7 all-gather.2
  203.5 63.8 all-gather.4
  270.9 82.2 reduce-scatter.2
  356.5 82.2 reduce-scatter.4
